TPU v7x, 256 devices: a whole 4x4x8 slice. The times are simulated.
256 devices in a mesh: wl: 8 (over y, z_lo), gz: 32 (over z_hi, x, core).
Axes of the slice: x: 4, y: 4, z: 8 (z_hi: 4, z_lo: 2; z = z_hi * 2 + z_lo), core: 2. Of those that a mesh axis runs over, the one named last changes fastest.
Arguments:
- labels: int32 [256, 128, 128], P('gz'), may hold values from 0 to 7
- label_table: float32 [8, 5], replicated, may hold values from 0.1 to 1.5
- spectra: float32 [32, 6], P('wl'), may hold values from 0.2 to 2
- illumination: int32 [128, 128], replicated, may hold values 0 or 1
- fluence_start: float32 [32, 256, 128, 128], P('wl', 'gz'), as said below
- measured: float32 [32, 256, 128, 128], P('wl', 'gz'), may hold values from 0 to 2
Outputs:
- fluence: float32 [32, 256, 128, 128], P('wl', 'gz')
- concentrations: float32 [4, 256, 128, 128], P(None, 'gz')
- scattering: float32 [256, 128, 128], P('gz')
Inputs may be any that keep to these rules, and one draw needn't show every extreme that they name: `fluence_start`: positive, of order one.
All inputs are finite; a program needn't handle non-finite values.
Results may differ from a plain program's by a relative error of at most 0.0003.
Values sent between devices are 32-bit elements; how exact they have to be, the bound alone decides.
No kernel may reach another device: no remote copies, remote signals or barrier semaphores. Data moves between devices by JAX's collectives and lax.ppermute only.
A program may use at most 128 MiB of HBM per device.

v0:
```python
import jax
import jax.numpy as jnp
from jax import lax
from jax.sharding import PartitionSpec as P

ITERS = 2


eta_step = 0.3


def extended(block, sides, width):
    for axis, dim in sides:
        count = lax.axis_size(axis)
        forward = [(i, i + 1) for i in range(count - 1)]
        backward = [(target, source) for source, target in forward]
        low = lax.ppermute(
            lax.slice_in_dim(block, block.shape[dim] - width, None, axis=dim), axis, forward
        )
        high = lax.ppermute(lax.slice_in_dim(block, 0, width, axis=dim), axis, backward)
        block = jnp.concatenate([low, block, high], axis=dim)
    return block


def neighbours(padded):
    center = padded[:, 1:-1]
    ypadded = jnp.pad(center, ((0, 0), (0, 0), (1, 1), (0, 0)))
    xpadded = jnp.pad(center, ((0, 0), (0, 0), (0, 0), (1, 1)))
    return [
        padded[:, 2:],
        padded[:, :-2],
        ypadded[:, :, 2:],
        ypadded[:, :, :-2],
        xpadded[:, :, :, 2:],
        xpadded[:, :, :, :-2],
    ]


def lookup(classes, label_table):
    count = label_table.shape[0]
    onehot = (classes[None] == jnp.arange(count, dtype=jnp.int32)[:, None, None, None]).astype(
        jnp.float32
    )
    return jnp.tensordot(label_table.T, onehot, axes=1, precision=lax.Precision.HIGHEST)


def optics(spectra, coeffs):
    absorb = spectra[:, 0, None, None, None] * coeffs[0][None]
    for chrom in range(1, 4):
        absorb = absorb + spectra[:, chrom, None, None, None] * coeffs[chrom][None]
    diffuse = 1.0 / (3.0 * (absorb + spectra[:, 4, None, None, None] * coeffs[4][None]))
    return (absorb, diffuse)


def sweep(padded, weights, total, rhs):
    accum = rhs
    for weight, other in zip(weights, neighbours(padded)):
        accum = accum + weight * other
    return accum / total


def relax(field, weights, total, rhs):
    padded = extended(field, (("gz", 1),), 1)
    return sweep(padded, weights, total, rhs)


def shards(labels, label_table, spectra, illumination, fluence_start, measured):
    coeffs = lookup(labels, label_table)
    absorb, diffuse = optics(spectra, coeffs)
    diffuse_pad = extended(diffuse, (("gz", 1),), 1)
    weights = [0.5 * (diffuse + other) for other in neighbours(diffuse_pad)]
    total = absorb
    for weight in weights:
        total = total + weight
    source = spectra[:, 5, None, None, None] * illumination.astype(jnp.float32)[None, None]
    fluence = fluence_start
    for step in range(ITERS):
        fluence = relax(fluence, weights, total, source)
    misfit = absorb * fluence - measured
    adjoint = jnp.zeros_like(fluence)
    for step in range(ITERS):
        adjoint = relax(adjoint, weights, total, absorb * misfit)
    common = fluence * (misfit - adjoint)
    grads = [jnp.sum(spectra[:, chrom, None, None, None] * common, axis=0) for chrom in range(4)]
    paired = extended(jnp.stack([fluence, adjoint]), (("gz", 2),), 1)
    flu_nb = neighbours(paired[0])
    adj_nb = neighbours(paired[1])
    coupling = jnp.zeros_like(fluence)
    for weight, fother, aother in zip(weights, flu_nb, adj_nb):
        coupling = coupling + weight * (fother - fluence) * (aother - adjoint)
    grads.append(
        jnp.sum(spectra[:, 4, None, None, None] * 3.0 * diffuse * diffuse * coupling, axis=0)
    )
    partial_grad = jnp.stack(grads)
    cell_count = labels.shape[0] * lax.axis_size("gz") * labels.shape[1] * labels.shape[2]
    grad = lax.psum(partial_grad, "wl")
    squares = lax.psum(jnp.sum(grad * grad, axis=(1, 2, 3)), "gz")
    rms = jnp.sqrt(squares / cell_count + 1e-06)
    updated = coeffs * jnp.exp(-eta_step * grad / rms[:, None, None, None])
    return (fluence, updated[:4], updated[4])


def solution(mesh):
    in_specs = (
        P("gz", None, None),
        P(),
        P("wl", None),
        P(),
        P("wl", "gz", None, None),
        P("wl", "gz", None, None),
    )
    out_specs = (P("wl", "gz", None, None), P(None, "gz", None, None), P("gz", None, None))
    return jax.shard_map(shards, mesh=mesh, in_specs=in_specs, out_specs=out_specs, check_vma=False)
```

profile of v0, /device:TPU:8, one launch (start us, length us, event | category | flops | bytes accessed | tf_op | source)
XLA Modules:
  0.0 426.5 jit_solution(9827986577986211246)
XLA Ops:
  9.6 3.0 collective-permute-start.3
  13.8 3.1 fusion.1
  17.0 2.3 fusion.98
  20.2 3.0 collective-permute-start.2
  24.5 3.0 collective-permute-start.7
  29.1 4.8 %fusion.11 = f32[4,8,128,128]{3,2,1,0:T(8,128)S(1)} fusion(f32[4,8,128,128]{3,2,1,0:T(8,128)S(1)} %copy-done.7, f32[4,1,128,128]{3,2,1,0:T(8,128)S(1)} %collective-permute-done.3, f32[4,1,128,128]{3,2,1,0:T(8,128)S(1)} %collective-permute-done.1, f32[8,128,128]{2,1,0:T(8,128)S(1)} %bitcast.27, f32[4]{0:T(128)S(1)} %get-tuple-element.15, ...), kind=kLoop, calls=%fused_computation.48 | loop fusion | flops 22020096 | bytes 9699392 | tf_op jit(solution)/shard_map/div | solution.py:59
  33.9 1.4 collective-permute-start.4
  35.4 4.9 %collective-permute-start.5 = (f32[4,1,128,128]{3,2,1,0:T(8,128)S(1)}, f32[4,1,128,128]{3,2,1,0:T(8,128)S(1)}, u32[]{:S(2)}, u32[]{:S(2)}) collective-permute-start(f32[4,1,128,128]{3,2,1,0:T(8,128)S(1)} %get-tuple-element.32), channel_id=1, source_target_pairs={{0,1},{1,2},{2,3},{3,4},{4,5},{5,6},{6,7},{7,8},{8,9},{9,10},{10,1... | collective-permute-start | bytes 786440 | tf_op jit(solution)/shard_map/ppermute | solution.py:17
  41.6 8.5 %fusion.48 = (f32[4,8,128,128]{3,2,1,0:T(8,128)S(1)}, f32[4,8,128,128]{3,2,1,0:T(8,128)S(1)}) fusion(f32[4,1,128,128]{3,2,1,0:T(8,128)S(1)} %collective-permute-done.6, f32[4,1,128,128]{3,2,1,0:T(8,128)S(1)} %collective-permute-done.7, f32[4,8,128,128]{3,2,1,0:T(8,128)S(1)} %broadcast_in_dim.2, f32[8,128,128]{2,1,0:T(8,128)S(1)} %bitcast.28, ...), kind=kLoop, calls=%fused_computation.85 | loop fusion | flops 36700160 | bytes 16515136 | tf_op jit(solution)/shard_map/div | solution.py:59
  51.5 6.4 %collective-permute-start.9 = (f32[4,1,128,128]{3,2,1,0:T(8,128)S(1)}, f32[4,1,128,128]{3,2,1,0:T(8,128)S(1)}, u32[]{:S(2)}, u32[]{:S(2)}) collective-permute-start(f32[4,1,128,128]{3,2,1,0:T(8,128)S(1)} %get-tuple-element.30), channel_id=1, source_target_pairs={{0,1},{1,2},{2,3},{3,4},{4,5},{5,6},{6,7},{7,8},{8,9},{9,10},{10,1... | collective-permute-start | bytes 786440 | tf_op jit(solution)/shard_map/ppermute | solution.py:17
  59.1 7.8 %subtract_multiply_fusion = (f32[4,8,128,128]{3,2,1,0:T(8,128)}, f32[4,8,128,128]{3,2,1,0:T(8,128)S(1)}) fusion(f32[4,8,128,128]{3,2,1,0:T(8,128)S(1)} %get-tuple-element.19, f32[4,8,128,128]{3,2,1,0:T(8,128)} %param.11, f32[8,128,128]{2,1,0:T(8,128)S(1)} %bitcast.29, f32[4]{0:T(128)S(1)} %get-tuple-element.15, f32[8,128,128]{2,1,0:T(8,128)S(1)} %bitcast.33, ...), kind=kLoop, calls=%fused_computation.146 | loop fusion | flops 24641536 | bytes 15728704 | tf_op jit(solution)/shard_map/mul | solution.py:83
  67.0 6.7 %collective-permute-start.10 = (f32[2,4,1,128,128]{4,3,2,1,0:T(8,128)S(1)}, f32[2,4,1,128,128]{4,3,2,1,0:T(8,128)S(1)}, u32[]{:S(2)}, u32[]{:S(2)}) collective-permute-start(f32[2,4,1,128,128]{4,3,2,1,0:T(8,128)S(1)} %get-tuple-element.22), channel_id=1, source_target_pairs={{0,1},{1,2},{2,3},{3,4},{4,5},{5,6},{6,7},{7,8},{8,9},{9,10},{10,1... | collective-permute-start | bytes 1572872 | tf_op jit(solution)/shard_map/ppermute | solution.py:17
  73.7 1.5 collective-permute-start.11
  75.2 2.0 multiply_reduce_fusion.1
  77.2 2.3 collective-permute-done.11
  80.7 1.8 slice.309
  83.0 1.6 slice.308
  84.5 12.9 %fusion.35 = f32[8,128,128]{2,1,0:T(8,128)} fusion(f32[4,8,128,128]{3,2,1,0:T(8,128)S(1)} %get-tuple-element.19, f32[4,8,128,128]{3,2,1,0:T(8,128)} %slice.308, f32[4,8,128,128]{3,2,1,0:T(8,128)S(1)} %get-tuple-element.17, f32[4,8,128,128]{3,2,1,0:T(8,128)} %slice.309, f32[4,8,128,128]{3,2,1,0:T(8,128)S(1)} %multiply_divide_fusion, ...), kind=kLoop, calls=%fused_computation.72 | loop fusion | flops 24510464 | bytes 19922960 | tf_op jit(solution)/shard_map/reduce_sum | solution.py:92
  97.4 10.5 %stack.35 = f32[5,8,128,128]{3,0,2,1:T(8,128)} concatenate(f32[1,8,128,128]{3,0,2,1:T(1,128)} %bitcast.47, f32[1,8,128,128]{3,0,2,1:T(1,128)} %bitcast.46, f32[1,8,128,128]{3,0,2,1:T(1,128)} %bitcast.45, f32[1,8,128,128]{3,0,2,1:T(1,128)} %bitcast.44, f32[1,8,128,128]{3,0,2,1:T(1,128)} %bitcast.43), dimensions={0} | concatenate | bytes 5242880 | tf_op jit(solution)/shard_map/stack | solution.py:94
  107.9 226.1 %all-reduce.18.cloned.1.call-done = f32[5,8,128,128]{3,0,2,1:T(8,128)} async-done(((f32[5,8,128,128]{3,0,2,1:T(8,128)}), f32[5,8,128,128]{3,0,2,1:T(8,128)}) %all-reduce.18.cloned.1.call-update) | async-done | bytes 2621456 | tf_op jit(solution)/shard_map/psum | solution.py:96
  334.0 3.4 multiply_reduce_fusion
  337.4 74.6 %psum.15 = f32[5]{0:T(128)S(1)} all-reduce(f32[5]{0:T(128)S(1)} %multiply_reduce_fusion), channel_id=1, replica_groups=mesh['wl'=8,'gz'=32] {'gz'}, use_global_device_ids=true, to_apply=%region_7.8 | all-reduce | flops 5 | bytes 40 | tf_op jit(solution)/shard_map/psum | solution.py:97
  412.1 4.3 %exponential_multiply_fusion = f32[5,8,128,128]{3,0,2,1:T(8,128)S(1)} fusion(f32[5,8,128,128]{3,0,2,1:T(8,128)} %copy-done.4, f32[5,8,128,128]{3,0,2,1:T(8,128)} %all-reduce.18.cloned.1.call-done, f32[5]{0:T(128)S(1)} %add_sqrt_fusion), kind=kLoop, calls=%fused_computation.15 | loop fusion | flops 1966080 | bytes 7864340 | tf_op jit(solution)/shard_map/mul | solution.py:99
  418.1 1.6 copy.10
  (52 shorter events, 14.5 us)
Async XLA Ops:
  7.2 6.7 %copy-start = (f32[8,5]{1,0:T(8,128)S(1)}, f32[8,5]{1,0:T(8,128)}, u32[]{:S(2)}) copy-start(f32[8,5]{1,0:T(8,128)} %param.7) | copy-start | bytes 484
  7.2 326.8 %all-reduce.18.cloned.1.call-start = ((), (), s32[]{:S(2)}) async-start(), calls=%async_computation | async-start | bytes 8388608 | tf_op jit(solution)/shard_map/psum | solution.py:96
  8.3 19.4 %collective-permute-start.1 = (f32[4,1,128,128]{3,2,1,0:T(8,128)S(1)}, f32[4,1,128,128]{3,2,1,0:T(8,128)S(1)}, u32[]{:S(2)}, u32[]{:S(2)}) collective-permute-start(f32[4,1,128,128]{3,2,1,0:T(8,128)S(1)} %get-tuple-element.33), channel_id=1, source_target_pairs={{1,0},{2,1},{3,2},{4,3},{5,4},{6,5},{7,6},{8,7},{9,8},{10,9},{11,1... | collective-permute-start | bytes 786440 | tf_op jit(solution)/shard_map/ppermute | solution.py:20
  9.6 19.4 %collective-permute-start.3 = (f32[4,1,128,128]{3,2,1,0:T(8,128)S(1)}, f32[4,1,128,128]{3,2,1,0:T(8,128)S(1)}, u32[]{:S(2)}, u32[]{:S(2)}) collective-permute-start(f32[4,1,128,128]{3,2,1,0:T(8,128)S(1)} %get-tuple-element.34), channel_id=1, source_target_pairs={{0,1},{1,2},{2,3},{3,4},{4,5},{5,6},{6,7},{7,8},{8,9},{9,10},{10,1... | collective-permute-start | bytes 786440 | tf_op jit(solution)/shard_map/ppermute | solution.py:17
  17.0 2.3 copy-start.4
  19.3 8.3 %copy-start.8 = (s32[128,128]{1,0:T(8,128)S(1)}, s32[128,128]{1,0:T(8,128)}, u32[]{:S(2)}) copy-start(s32[128,128]{1,0:T(8,128)} %param.9) | copy-start | bytes 196612
  19.3 9.7 %copy-start.7 = (f32[4,8,128,128]{3,2,1,0:T(8,128)S(1)}, f32[4,8,128,128]{3,2,1,0:T(8,128)}, u32[]{:S(2)}) copy-start(f32[4,8,128,128]{3,2,1,0:T(8,128)} %param.10) | copy-start | bytes 6291460
  20.2 8.8 %collective-permute-start.2 = (f32[4,1,128,128]{3,2,1,0:T(8,128)S(1)}, f32[4,1,128,128]{3,2,1,0:T(8,128)S(1)}, u32[]{:S(2)}, u32[]{:S(2)}) collective-permute-start(f32[4,1,128,128]{3,2,1,0:T(8,128)S(1)} %get-tuple-element.35), channel_id=1, source_target_pairs={{0,1},{1,2},{2,3},{3,4},{4,5},{5,6},{6,7},{7,8},{8,9},{9,10},{10,1... | collective-permute-start | bytes 786440 | tf_op jit(solution)/shard_map/ppermute | solution.py:17
  23.2 5.8 %collective-permute-start = (f32[4,1,128,128]{3,2,1,0:T(8,128)S(1)}, f32[4,1,128,128]{3,2,1,0:T(8,128)S(1)}, u32[]{:S(2)}, u32[]{:S(2)}) collective-permute-start(f32[4,1,128,128]{3,2,1,0:T(8,128)S(1)} %get-tuple-element.36), channel_id=1, source_target_pairs={{1,0},{2,1},{3,2},{4,3},{5,4},{6,5},{7,6},{8,7},{9,8},{10,9},{11,1... | collective-permute-start | bytes 786440 | tf_op jit(solution)/shard_map/ppermute | solution.py:20
  24.5 15.7 %collective-permute-start.7 = (f32[4,1,128,128]{3,2,1,0:T(8,128)S(1)}, f32[4,1,128,128]{3,2,1,0:T(8,128)S(1)}, u32[]{:S(2)}, u32[]{:S(2)}) collective-permute-start(f32[4,1,128,128]{3,2,1,0:T(8,128)S(1)} %broadcast.69), channel_id=1, source_target_pairs={{0,1},{1,2},{2,3},{3,4},{4,5},{5,6},{6,7},{7,8},{8,9},{9,10},{10,1... | collective-permute-start | bytes 786440 | tf_op jit(solution)/shard_map/ppermute | solution.py:17
  27.7 12.5 %collective-permute-start.6 = (f32[4,1,128,128]{3,2,1,0:T(8,128)S(1)}, f32[4,1,128,128]{3,2,1,0:T(8,128)S(1)}, u32[]{:S(2)}, u32[]{:S(2)}) collective-permute-start(f32[4,1,128,128]{3,2,1,0:T(8,128)S(1)} %broadcast.69), channel_id=1, source_target_pairs={{1,0},{2,1},{3,2},{4,3},{5,4},{6,5},{7,6},{8,7},{9,8},{10,9},{11,1... | collective-permute-start | bytes 786440 | tf_op jit(solution)/shard_map/ppermute | solution.py:20
  33.9 7.8 %copy-start.5 = (f32[4,8,128,128]{3,2,1,0:T(8,128)S(1)}, f32[4,8,128,128]{3,2,1,0:T(8,128)}, u32[]{:S(2)}) copy-start(f32[4,8,128,128]{3,2,1,0:T(8,128)} %param.11) | copy-start | bytes 6291460
  33.9 6.4 %collective-permute-start.4 = (f32[4,1,128,128]{3,2,1,0:T(8,128)S(1)}, f32[4,1,128,128]{3,2,1,0:T(8,128)S(1)}, u32[]{:S(2)}, u32[]{:S(2)}) collective-permute-start(f32[4,1,128,128]{3,2,1,0:T(8,128)S(1)} %get-tuple-element.31), channel_id=1, source_target_pairs={{1,0},{2,1},{3,2},{4,3},{5,4},{6,5},{7,6},{8,7},{9,8},{10,9},{11,1... | collective-permute-start | bytes 786440 | tf_op jit(solution)/shard_map/ppermute | solution.py:20
  35.4 6.0 %collective-permute-start.5 = (f32[4,1,128,128]{3,2,1,0:T(8,128)S(1)}, f32[4,1,128,128]{3,2,1,0:T(8,128)S(1)}, u32[]{:S(2)}, u32[]{:S(2)}) collective-permute-start(f32[4,1,128,128]{3,2,1,0:T(8,128)S(1)} %get-tuple-element.32), channel_id=1, source_target_pairs={{0,1},{1,2},{2,3},{3,4},{4,5},{5,6},{6,7},{7,8},{8,9},{9,10},{10,1... | collective-permute-start | bytes 786440 | tf_op jit(solution)/shard_map/ppermute | solution.py:17
  50.1 34.4 %copy-start.2 = (f32[4,8,128,128]{3,2,1,0:T(8,128)}, f32[4,8,128,128]{3,2,1,0:T(8,128)S(1)}, u32[]{:S(2)}) copy-start(f32[4,8,128,128]{3,2,1,0:T(8,128)S(1)} %get-tuple-element.19) | copy-start | bytes 6291460
  50.2 7.7 %collective-permute-start.8 = (f32[4,1,128,128]{3,2,1,0:T(8,128)S(1)}, f32[4,1,128,128]{3,2,1,0:T(8,128)S(1)}, u32[]{:S(2)}, u32[]{:S(2)}) collective-permute-start(f32[4,1,128,128]{3,2,1,0:T(8,128)S(1)} %get-tuple-element.29), channel_id=1, source_target_pairs={{1,0},{2,1},{3,2},{4,3},{5,4},{6,5},{7,6},{8,7},{9,8},{10,9},{11,1... | collective-permute-start | bytes 786440 | tf_op jit(solution)/shard_map/ppermute | solution.py:20
  51.5 7.6 %collective-permute-start.9 = (f32[4,1,128,128]{3,2,1,0:T(8,128)S(1)}, f32[4,1,128,128]{3,2,1,0:T(8,128)S(1)}, u32[]{:S(2)}, u32[]{:S(2)}) collective-permute-start(f32[4,1,128,128]{3,2,1,0:T(8,128)S(1)} %get-tuple-element.30), channel_id=1, source_target_pairs={{0,1},{1,2},{2,3},{3,4},{4,5},{5,6},{6,7},{7,8},{8,9},{9,10},{10,1... | collective-permute-start | bytes 786440 | tf_op jit(solution)/shard_map/ppermute | solution.py:17
  66.9 8.3 %copy-start.6 = (f32[4,8,128,128]{3,2,1,0:T(8,128)S(1)}, f32[4,8,128,128]{3,2,1,0:T(8,128)}, u32[]{:S(2)}) copy-start(f32[4,8,128,128]{3,2,1,0:T(8,128)} %get-tuple-element.16) | copy-start | bytes 6291460
  67.0 10.2 %collective-permute-start.10 = (f32[2,4,1,128,128]{4,3,2,1,0:T(8,128)S(1)}, f32[2,4,1,128,128]{4,3,2,1,0:T(8,128)S(1)}, u32[]{:S(2)}, u32[]{:S(2)}) collective-permute-start(f32[2,4,1,128,128]{4,3,2,1,0:T(8,128)S(1)} %get-tuple-element.22), channel_id=1, source_target_pairs={{0,1},{1,2},{2,3},{3,4},{4,5},{5,6},{6,7},{7,8},{8,9},{9,10},{10,1... | collective-permute-start | bytes 1572872 | tf_op jit(solution)/shard_map/ppermute | solution.py:17
  73.7 5.8 %collective-permute-start.11 = (f32[2,4,1,128,128]{4,3,2,1,0:T(8,128)S(1)}, f32[2,4,1,128,128]{4,3,2,1,0:T(8,128)S(1)}, u32[]{:S(2)}, u32[]{:S(2)}) collective-permute-start(f32[2,4,1,128,128]{4,3,2,1,0:T(8,128)S(1)} %get-tuple-element.23), channel_id=1, source_target_pairs={{1,0},{2,1},{3,2},{4,3},{5,4},{6,5},{7,6},{8,7},{9,8},{10,9},{11,1... | collective-permute-start | bytes 1572872 | tf_op jit(solution)/shard_map/ppermute | solution.py:20
  80.7 2.2 copy-start.3
  417.7 1.9 copy-start.1
Sparse Core Ops, SparseCore 0:
  108.1 225.9 all-reduce.17
where the time goes:
time: 429 us; the launch traced here: 427 us
  waiting for transfers between devices  231 us (54%)
  blocking collectives  74.6 us (17%)
  other arithmetic  45.3 us (11%)
  starting transfers between devices  35.2 us (8%)
  local copies, waits for them, and re-layouts  23.2 us (5%)
  between operations  14.4 us (3%)
    psum x1, waiting for transfers between devices, shards(): grad = lax.psum(partial_grad, 'wl')  226 us
    psum x1, blocking collectives, shards(): squares = lax.psum(jnp.sum(grad * grad, axis=(1, 2, 3)), 'gz')  74.6 us
    ppermute x6, starting transfers between devices, extended(): lax.ppermute(lax.slice_in_dim(block, block.shape[dim] - width, None, axis...  27.1 us
    div x2, other arithmetic, sweep(): return accum / total  13.3 us
    reduce_sum x1, other arithmetic, shards(): jnp.sum(spectra[:, 4, None, None, None] * 3.0 * diffuse * diffuse * coupl...  12.9 us
    another operation x1, local copies, waits for them, and re-layouts, shards(): partial_grad = jnp.stack(grads)  10.5 us
  transfers between devices with their start and end apart: 13, of which 4 were waited for; matrix products, arithmetic and copies ran while one was open for 3% of the time, Pallas kernels for 0%

commit v1 on v0

v1 whole, which is shorter than its diff:
```python
import functools

import jax
import jax.numpy as jnp
from jax import lax
from jax.experimental import pallas as pl
from jax.experimental.pallas import tpu as pltpu
from jax.sharding import PartitionSpec as P

STEP = 0.3
HF = 4
HM = 2
NP = 8
EXT = NP + 2 * HF
N = 128
F32 = jnp.float32

GENS = (2, 6, 1)
ORDERS = ((0, 1, 2), (1, 2, 0), (2, 0, 1))
PARTS = ((0, 14), (14, 27), (27, 40))
ROWS = 16


def code_of(part, slot):
    order = ORDERS[part]
    bits = (slot >> 2 & 1, slot >> 1 & 1, slot & 1)
    code = 0
    for dim, bit in zip(order, bits):
        code ^= GENS[dim] * bit
    return code


def slot_of(part, code):
    return [code_of(part, slot) for slot in range(8)].index(code)


def part_of(plane, field):
    at = plane * 5 + field
    for part, (first, last) in enumerate(PARTS):
        if at < last:
            return part, at - first


def ahead(x, axis):
    return pltpu.roll(x, N - 1, axis)


def behind(x, axis):
    return pltpu.roll(x, 1, axis)


def pick(classes, entries):
    bit0 = (classes & 1) != 0
    bit1 = (classes & 2) != 0
    bit2 = (classes & 4) != 0
    low = [jnp.where(bit0, entries[2 * i + 1], entries[2 * i]) for i in range(4)]
    mid = [jnp.where(bit1, low[2 * i + 1], low[2 * i]) for i in range(2)]
    return jnp.where(bit2, mid[1], mid[0])


def gather_faces(v, above, below, wx, wy, wabove, wbelow):
    return (
        wabove * above
        + wbelow * below
        + wy * ahead(v, 0)
        + behind(wy * v, 0)
        + wx * ahead(v, 1)
        + behind(wx * v, 1)
    )


def solve_kernel(
    where, spectra, absorb_t, half_t,
    labels, labels_a, labels_b, illum, start, start_a, start_b, meas, meas_a, meas_b,
    fluence, *rest,
):
    outs = rest[:6]
    cls, fl, hd, ab, wxs, wys, inv, tmp, mis, adj, ms, sem = rest[6:]
    sends, keeps = outs[0::2], outs[1::2]
    gz = where[0]
    me = where[1]
    odd = lax.rem(gz, 2)
    at_a = (1 - odd) * (HF + NP)
    at_b = odd * (HF + NP)
    mat_a = (1 - odd) * (HM + NP)
    mat_b = odd * (HM + NP)
    copies = [
        pltpu.make_async_copy(labels, cls.at[pl.ds(HF, NP)], sem.at[0]),
        pltpu.make_async_copy(labels_a, cls.at[pl.ds(at_a, HF)], sem.at[1]),
        pltpu.make_async_copy(labels_b, cls.at[pl.ds(at_b, HF)], sem.at[2]),
        pltpu.make_async_copy(start, fl.at[:, pl.ds(HF, NP)], sem.at[3]),
        pltpu.make_async_copy(start_a, fl.at[:, pl.ds(at_a, HF)], sem.at[4]),
        pltpu.make_async_copy(start_b, fl.at[:, pl.ds(at_b, HF)], sem.at[5]),
        pltpu.make_async_copy(meas, ms.at[:, pl.ds(HM, NP)], sem.at[6]),
        pltpu.make_async_copy(meas_a, ms.at[:, pl.ds(mat_a, HM)], sem.at[7]),
        pltpu.make_async_copy(meas_b, ms.at[:, pl.ds(mat_b, HM)], sem.at[8]),
    ]
    for copy in copies:
        copy.start()
    row = lax.broadcasted_iota(jnp.int32, (N, N), 0)
    col = lax.broadcasted_iota(jnp.int32, (N, N), 1)
    notlast_x = (col < N - 1).astype(F32)
    notlast_y = (row < N - 1).astype(F32)
    outer = (
        (col == 0).astype(F32) + (col == N - 1).astype(F32)
        + (row == 0).astype(F32) + (row == N - 1).astype(F32)
    )
    for copy in copies[:3]:
        copy.wait()

    def inside(e):
        z = gz * NP + e - HF
        return jnp.where((z >= 0) & (z < 32 * NP), 1.0, 0.0).astype(F32)

    def optics(e, _):
        classes = cls[e]
        there = inside(e)
        for l in range(4):
            ab[l, e] = pick(classes, [absorb_t[l, i] for i in range(8)])
            hd[l, e] = pick(classes, [half_t[l, i] * there for i in range(8)])
        return 0

    lax.fori_loop(0, EXT, optics, 0)
    for copy in copies[3:6]:
        copy.wait()

    def per_plane(first, last, body):
        def outerloop(l, _):
            def innerloop(e, _):
                body(l, e)
                return 0

            lax.fori_loop(first, last, innerloop, 0)
            return 0

        lax.fori_loop(0, 4, outerloop, 0)

    def first(l, e):
        h = hd[l, e]
        wx = (h + ahead(h, 1)) * notlast_x
        wy = (h + ahead(h, 0)) * notlast_y
        above = h + hd[l, e + 1]
        below = h + hd[l, e - 1]
        total = ab[l, e] + above + below + wx + behind(wx, 1) + wy + behind(wy, 0) + h * outer
        r = inside(e) / total
        wxs[l, e] = wx
        wys[l, e] = wy
        inv[l, e] = r
        source = spectra[l, 5] * illum[...].astype(F32)
        moved = gather_faces(fl[l, e], fl[l, e + 1], fl[l, e - 1], wx, wy, above, below)
        tmp[l, e] = (source + moved) * r

    per_plane(1, EXT - 1, first)
    for copy in copies[6:]:
        copy.wait()

    def second(l, e):
        h = hd[l, e]
        above = h + hd[l, e + 1]
        below = h + hd[l, e - 1]
        source = spectra[l, 5] * illum[...].astype(F32)
        moved = gather_faces(tmp[l, e], tmp[l, e + 1], tmp[l, e - 1], wxs[l, e], wys[l, e], above, below)
        r = inv[l, e]
        f = (source + moved) * r
        fl[l, e] = f
        absorb = ab[l, e]
        misfit = absorb * f - ms[l, e - (HF - HM)]
        mis[l, e] = misfit
        adj[l, e] = absorb * misfit * r

    per_plane(2, EXT - 2, second)
    write = pltpu.make_async_copy(fl.at[:, pl.ds(HF, NP)], fluence, sem.at[0])
    write.start()

    def third(l, e):
        h = hd[l, e]
        above = h + hd[l, e + 1]
        below = h + hd[l, e - 1]
        moved = gather_faces(adj[l, e], adj[l, e + 1], adj[l, e - 1], wxs[l, e], wys[l, e], above, below)
        tmp[l, e] = (ab[l, e] * mis[l, e] + moved) * inv[l, e]

    per_plane(3, EXT - 3, third)

    def couple(l, e):
        h = hd[l, e]
        f = fl[l, e]
        a = tmp[l, e]
        qx = wxs[l, e] * (ahead(f, 1) - f) * (ahead(a, 1) - a)
        qy = wys[l, e] * (ahead(f, 0) - f) * (ahead(a, 0) - a)
        total = (
            qx + behind(qx, 1) + qy + behind(qy, 0) + h * outer * f * a
            + (h + hd[l, e + 1]) * (fl[l, e + 1] - f) * (tmp[l, e + 1] - a)
            + (h + hd[l, e - 1]) * (fl[l, e - 1] - f) * (tmp[l, e - 1] - a)
        )
        ab[l, e] = 12.0 * h * h * total

    per_plane(HF, HF + NP, couple)

    for code in range(8):
        at = pl.multiple_of((me ^ code) * ROWS, ROWS)
        rows = pl.ds(at, ROWS)
        for plane in range(NP):
            e = plane + HF
            common = [fl[l, e, rows] * (mis[l, e, rows] - tmp[l, e, rows]) for l in range(4)]
            paired = [ab[l, e, rows] for l in range(4)]
            for field in range(5):
                terms = common if field < 4 else paired
                value = spectra[0, field] * terms[0]
                for l in range(1, 4):
                    value = value + spectra[l, field] * terms[l]
                part, index = part_of(plane, field)
                slot = slot_of(part, code)
                if slot >= 4:
                    sends[part][slot - 4, index] = value
                else:
                    keeps[part][slot, index] = value
    write.wait()


def squares_kernel(*refs):
    keeps, recvs, owns, sums = refs[:3], refs[3:6], refs[6:9], refs[9]
    total = [jnp.zeros((8, N), F32) for _ in range(5)]
    for plane in range(NP):
        for field in range(5):
            part, index = part_of(plane, field)
            value = keeps[part][0, index] + recvs[part][0, index]
            owns[part][0, index] = value
            squared = value * value
            total[field] = total[field] + squared[:8] + squared[8:]
    rows = [jnp.sum(t, axis=0, keepdims=True) for t in total]
    sums[...] = jnp.concatenate(rows + [jnp.zeros((3, N), F32)], axis=0)


def final_kernel(where, table, sums, labels, *refs):
    pieces, conc, scat = refs[:12], refs[12], refs[13]
    me = where[1]
    cells = 32 * NP * N * N
    total = jnp.sum(sums[...], axis=1, keepdims=True)
    factor = jnp.broadcast_to(-STEP / jnp.sqrt(total / cells + 1e-06), (8, N))
    factors = [jnp.broadcast_to(factor[c : c + 1], (ROWS, N)) for c in range(5)]
    for code in range(8):
        at = pl.multiple_of((me ^ code) * ROWS, ROWS)
        rows = pl.ds(at, ROWS)
        for plane in range(NP):
            classes = labels[plane, rows]
            for field in range(5):
                part, index = part_of(plane, field)
                slot = slot_of(part, code)
                own, one, two, four = pieces[4 * part : 4 * part + 4]
                if slot == 0:
                    grad = own[0, index]
                elif slot == 1:
                    grad = one[0, index]
                elif slot < 4:
                    grad = two[slot - 2, index]
                else:
                    grad = four[slot - 4, index]
                coeff = pick(classes, [table[i, field] for i in range(8)])
                value = coeff * jnp.exp(grad * factors[field])
                if field < 4:
                    conc[field, plane, rows] = value
                else:
                    scat[plane, rows] = value


VMEM = pl.BlockSpec(memory_space=pltpu.VMEM)
SMEM = pl.BlockSpec(memory_space=pltpu.SMEM)
ANY = pl.BlockSpec(memory_space=pl.ANY)


def swap(x, code):
    return lax.ppermute(x, "wl", [(i, i ^ code) for i in range(8)])


ON_CHIP = [(i, i ^ 1) for i in range(32)]
OFF_CHIP = [(i, i + 1) for i in range(1, 31, 2)] + [(i + 1, i) for i in range(1, 31, 2)]


def halo(x, axis, width, odd):
    extent = x.shape[axis]
    high = extent - width
    a = lax.dynamic_slice_in_dim(x, jnp.where(odd == 0, high, 0), width, axis)
    b = lax.dynamic_slice_in_dim(x, jnp.where(odd == 0, 0, high), width, axis)
    return lax.ppermute(a, "gz", ON_CHIP), lax.ppermute(b, "gz", OFF_CHIP)


def shards(labels, label_table, spectra, illumination, fluence_start, measured):
    gz = lax.axis_index("gz")
    me = lax.axis_index("wl")
    odd = lax.rem(gz, 2)
    where = jnp.stack([gz, me]).astype(jnp.int32)
    labels_a, labels_b = halo(labels, 0, HF, odd)
    start_a, start_b = halo(fluence_start, 1, HF, odd)
    meas_a, meas_b = halo(measured, 1, HM, odd)

    absorb_t = spectra[:, 0, None] * label_table[None, :, 0]
    for c in range(1, 4):
        absorb_t = absorb_t + spectra[:, c, None] * label_table[None, :, c]
    half_t = 0.5 / (3.0 * (absorb_t + spectra[:, 4, None] * label_table[None, :, 4]))

    sizes = [last - first for first, last in PARTS]
    field = pltpu.VMEM((4, EXT, N, N), F32)
    out = pl.pallas_call(
        solve_kernel,
        out_shape=[jax.ShapeDtypeStruct((4, NP, N, N), F32)]
        + [jax.ShapeDtypeStruct((4, size, ROWS, N), F32) for size in sizes for _ in range(2)],
        in_specs=[SMEM] * 4 + [ANY] * 3 + [VMEM] + [ANY] * 6,
        out_specs=[ANY] + [VMEM] * 6,
        scratch_shapes=[pltpu.VMEM((EXT, N, N), jnp.int32)]
        + [field] * 9
        + [pltpu.VMEM((4, NP + 2 * HM, N, N), F32), pltpu.SemaphoreType.DMA((9,))],
        compiler_params=pltpu.CompilerParams(vmem_limit_bytes=56 * 2**20),
        name="solve",
    )(where, spectra, absorb_t, half_t, labels, labels_a, labels_b, illumination,
      fluence_start, start_a, start_b, measured, meas_a, meas_b)
    fluence = out[0]
    sends = list(out[1::2])
    keeps = list(out[2::2])
    for phase in range(2):
        recvs = [swap(sends[q], GENS[ORDERS[q][phase]]) for q in range(3)]
        half = keeps[0].shape[0] // 2
        sends = [keeps[q][half:] + recvs[q][half:] for q in range(3)]
        keeps = [keeps[q][:half] + recvs[q][:half] for q in range(3)]
    recvs = [swap(sends[q], GENS[ORDERS[q][2]]) for q in range(3)]
    *owns, sums = pl.pallas_call(
        squares_kernel,
        out_shape=[jax.ShapeDtypeStruct((1, size, ROWS, N), F32) for size in sizes]
        + [jax.ShapeDtypeStruct((8, N), F32)],
        in_specs=[VMEM] * 6,
        out_specs=[VMEM] * 4,
        name="squares",
    )(*keeps, *recvs)

    ones = [swap(owns[q], GENS[ORDERS[q][2]]) for q in range(3)]
    for code in (1, 2, 4, 8, 16):
        sums = sums + lax.ppermute(sums, "gz", [(i, i ^ code) for i in range(32)])
    pairs = [jnp.concatenate([owns[q], ones[q]]) for q in range(3)]
    twos = [swap(pairs[q], GENS[ORDERS[q][1]]) for q in range(3)]
    quads = [jnp.concatenate([pairs[q], twos[q]]) for q in range(3)]
    fours = [swap(quads[q], GENS[ORDERS[q][0]]) for q in range(3)]
    for code in GENS:
        sums = sums + swap(sums, code)
    pieces = []
    for q in range(3):
        pieces += [owns[q], ones[q], twos[q], fours[q]]
    conc, scat = pl.pallas_call(
        final_kernel,
        out_shape=[jax.ShapeDtypeStruct((4, NP, N, N), F32), jax.ShapeDtypeStruct((NP, N, N), F32)],
        in_specs=[SMEM] * 2 + [VMEM] * 14,
        out_specs=[VMEM] * 2,
        compiler_params=pltpu.CompilerParams(vmem_limit_bytes=32 * 2**20),
        name="final",
    )(where, label_table, sums, labels, *pieces)
    return fluence, conc, scat


def solution(mesh):
    in_specs = (
        P("gz", None, None),
        P(),
        P("wl", None),
        P(),
        P("wl", "gz", None, None),
        P("wl", "gz", None, None),
    )
    out_specs = (P("wl", "gz", None, None), P(None, "gz", None, None), P("gz", None, None))
    return jax.shard_map(shards, mesh=mesh, in_specs=in_specs, out_specs=out_specs, check_vma=False)
```

time: 429 us -> 178 us (0.41)
  waiting for transfers between devices: 231 us -> 29.3 us
  blocking collectives: 74.6 us -> 0 us
  starting transfers between devices: 35.2 us -> 92.6 us
  Pallas kernels: 0 us -> 37.9 us
  other arithmetic: 45.3 us -> 9.29 us
  local copies, waits for them, and re-layouts: 23.2 us -> 7.19 us
  between operations: 14.4 us -> 0.91 us
    psum x1 -> x0, waiting for transfers between devices: 226 us -> none  [shards(): grad = lax.psum(partial_grad, 'wl')]
    psum x1 -> x0, blocking collectives: 74.6 us -> none  [shards(): squares = lax.psum(jnp.sum(grad * grad, axis=(1, 2, 3)), 'gz')]
    ppermute x12 -> x32, starting transfers between devices: 35.2 us -> 92.6 us  [the longest x5 42.8 us: shards(): sums = sums + lax.ppermute(sums, 'gz', [(i, i ^ code) for i in range(32)])]
    pallas_call x0 -> x3, Pallas kernels: none -> 37.9 us  [the longest x1 32.7 us: shards(): pl.pallas_call(solve_kernel, out_shape=[jax.ShapeDtypeStruct((4, NP, N, N...]
    ppermute x12 -> x32, waiting for transfers between devices: 4.51 us -> 29.3 us  [the longest x21 21.6 us: swap(): return lax.ppermute(x, 'wl', [(i, i ^ code) for i in range(8)])]
    reduce_sum x3 -> x0, other arithmetic: 18.2 us -> none  [the longest x1 12.9 us: shards(): jnp.sum(spectra[:, 4, None, None, None] * 3.0 * diffuse * diffuse * coupl...]
    div x3 -> x1, other arithmetic: 14.1 us -> 0.67 us  [shards(): 0.5 / (3.0 * (absorb_t + spectra[:, 4, None] * label_table[None, :, 4]))]
    mul x4 -> x0, other arithmetic: 12.2 us -> none  [the longest x1 7.82 us: shards(): common = fluence * (misfit - adjoint)]
  transfers between devices with their start and end apart: 13 -> 32, of which waited for: 4 -> 14; matrix products, arithmetic and copies ran while one was open for 3% -> 6% of each run, Pallas kernels for 0% -> 0%
where the time goes in v1:
time: 178 us; the launch traced here: 177 us
  starting transfers between devices  92.6 us (52%)
  Pallas kernels  37.9 us (21%)
  waiting for transfers between devices  29.3 us (16%)
  other arithmetic  9.29 us (5%)
  local copies, waits for them, and re-layouts  7.19 us (4%)
    ppermute x5, starting transfers between devices, shards(): sums = sums + lax.ppermute(sums, 'gz', [(i, i ^ code) for i in range(32)])  42.8 us
    ppermute x21, starting transfers between devices, swap(): return lax.ppermute(x, 'wl', [(i, i ^ code) for i in range(8)])  33 us
    pallas_call x1, Pallas kernels, shards(): pl.pallas_call(solve_kernel, out_shape=[jax.ShapeDtypeStruct((4, NP, N, N...  32.7 us
    ppermute x21, waiting for transfers between devices, swap(): return lax.ppermute(x, 'wl', [(i, i ^ code) for i in range(8)])  21.6 us
    ppermute x6, starting transfers between devices, halo(): return (lax.ppermute(a, 'gz', ON_CHIP), lax.ppermute(b, 'gz', OFF_CHIP))  16.8 us
    ppermute x5, waiting for transfers between devices, shards(): sums = sums + lax.ppermute(sums, 'gz', [(i, i ^ code) for i in range(32)])  7.5 us
    dynamic_slice x3, local copies, waits for them, and re-layouts, halo(): b = lax.dynamic_slice_in_dim(x, jnp.where(odd == 0, 0, high), width, axis)  4.96 us
  transfers between devices with their start and end apart: 32, of which 14 were waited for; matrix products, arithmetic and copies ran while one was open for 6% of the time, Pallas kernels for 0%

profile of v1, /device:TPU:8, one launch (start us, length us, event | category | flops | bytes accessed | tf_op | source)
XLA Modules:
  0.0 177.2 jit_solution(14747586415880027967)
XLA Ops:
  0.7 3.2 %constant_dynamic-slice_fusion.2 = (f32[4,4,128,128]{3,2,1,0:T(8,128)}, f32[4,4,128,128]{3,2,1,0:T(8,128)}) fusion(f32[4,8,128,128]{3,2,1,0:T(8,128)} %start.1, s32[]{:T(128)S(6)} %select_n.22, s32[]{:T(128)S(6)} %select_n.21), kind=kLoop, calls=%fused_computation.32 | loop fusion | bytes 4194312 | tf_op jit(solution)/shard_map/dynamic_slice | solution.py:283
  5.7 2.0 %collective-permute-start.2 = (f32[4,4,128,128]{3,2,1,0:T(8,128)}, f32[4,4,128,128]{3,2,1,0:T(8,128)}, u32[]{:S(2)}, u32[]{:S(2)}) collective-permute-start(f32[4,4,128,128]{3,2,1,0:T(8,128)} %get-tuple-element.44), channel_id=1, source_target_pairs={{0,1},{1,0},{2,3},{3,2},{4,5},{5,4},{6,7},{7,6},{8,9},{9,8},{10,11... | collective-permute-start | bytes 3145736 | tf_op jit(solution)/shard_map/ppermute | solution.py:284
  10.8 4.3 %collective-permute-start.4 = (f32[4,2,128,128]{3,2,1,0:T(8,128)S(1)}, f32[4,2,128,128]{3,2,1,0:T(8,128)S(1)}, u32[]{:S(2)}, u32[]{:S(2)}) collective-permute-start(f32[4,2,128,128]{3,2,1,0:T(8,128)S(1)} %get-tuple-element.42), channel_id=1, source_target_pairs={{0,1},{1,0},{2,3},{3,2},{4,5},{5,4},{6,7},{7,6},{8,9},{9,8},{10,11... | collective-permute-start | bytes 1572872 | tf_op jit(solution)/shard_map/ppermute | solution.py:284
  15.6 7.5 %collective-permute-start = (s32[4,128,128]{2,1,0:T(8,128)}, s32[4,128,128]{2,1,0:T(8,128)S(1)}, u32[]{:S(2)}, u32[]{:S(2)}) collective-permute-start(s32[4,128,128]{2,1,0:T(8,128)} %get-tuple-element.52), channel_id=1, source_target_pairs={{0,1},{1,0},{2,3},{3,2},{4,5},{5,4},{6,7},{7,6},{8,9},{9,8},{10,11... | collective-permute-start | bytes 786440 | tf_op jit(solution)/shard_map/ppermute | solution.py:284
  25.5 32.7 %solve.1 = (f32[4,8,128,128]{3,2,1,0:T(8,128)}, f32[4,14,16,128]{3,2,1,0:T(8,128)}, f32[4,14,16,128]{3,2,1,0:T(8,128)}, f32[4,13,16,128]{3,2,1,0:T(8,128)}, f32[...) custom-call(s32[2]{0:T(128)} %pad_add_fusion.where, f32[4,6]{1,0:T(4,128)} %spectra.1, ...), custom_call_target="tpu_custom_call" | custom-call | tf_op jit(solution)/shard_map/solve/pallas_call | solution.py:303
  63.6 4.3 %collective-permute-done.8 = f32[4,13,16,128]{3,2,1,0:T(8,128)S(1)} collective-permute-done((f32[4,13,16,128]{3,2,1,0:T(8,128)}, f32[4,13,16,128]{3,2,1,0:T(8,128)S(1)}, u32[]{:S(2)}, u32[]{:S(2)}) %collective-permute-start.8) | collective-permute-done | bytes 426016 | tf_op jit(solution)/shard_map/ppermute | solution.py:272
  69.0 2.0 %collective-permute-start.9 = (f32[2,13,16,128]{3,2,1,0:T(8,128)S(1)}, f32[2,13,16,128]{3,2,1,0:T(8,128)S(1)}, u32[]{:S(2)}, u32[]{:S(2)}) collective-permute-start(f32[2,13,16,128]{3,2,1,0:T(8,128)S(1)} %get-tuple-element.50), channel_id=1, source_target_pairs={{0,32},{32,0},{64,96},{96,64},{128,160},{160,128},{192,224},{224,1... | collective-permute-start | bytes 638984 | tf_op jit(solution)/shard_map/ppermute | solution.py:272
  73.8 2.6 %collective-permute-start.7 = (f32[2,14,16,128]{3,2,1,0:T(8,128)S(1)}, f32[2,14,16,128]{3,2,1,0:T(8,128)S(1)}, u32[]{:S(2)}, u32[]{:S(2)}) collective-permute-start(f32[2,14,16,128]{3,2,1,0:T(8,128)S(1)} %get-tuple-element.46), channel_id=1, source_target_pairs={{0,192},{32,224},{64,128},{96,160},{128,64},{160,96},{192,0},{224,... | collective-permute-start | bytes 688136 | tf_op jit(solution)/shard_map/ppermute | solution.py:272
  77.8 3.2 %collective-permute-done.7 = f32[2,14,16,128]{3,2,1,0:T(8,128)S(1)} collective-permute-done((f32[2,14,16,128]{3,2,1,0:T(8,128)S(1)}, f32[2,14,16,128]{3,2,1,0:T(8,128)S(1)}, u32[]{:S(2)}, u32[]{:S(2)}) %collective-permute-start.7) | collective-permute-done | bytes 229408 | tf_op jit(solution)/shard_map/ppermute | solution.py:272
  82.5 2.1 %collective-permute-start.14 = (f32[1,13,16,128]{3,2,1,0:T(8,128)S(1)}, f32[1,13,16,128]{3,2,1,0:T(8,128)S(1)}, u32[]{:S(2)}, u32[]{:S(2)}) collective-permute-start(f32[1,13,16,128]{3,2,1,0:T(8,128)S(1)} %get-tuple-element.55), channel_id=1, source_target_pairs={{0,192},{32,224},{64,128},{96,160},{128,64},{160,96},{192,0},{224,... | collective-permute-start | bytes 319496 | tf_op jit(solution)/shard_map/ppermute | solution.py:272
  84.6 3.1 %collective-permute-done.14.refs_5_ = f32[1,13,16,128]{3,2,1,0:T(8,128)S(1)} collective-permute-done((f32[1,13,16,128]{3,2,1,0:T(8,128)S(1)}, f32[1,13,16,128]{3,2,1,0:T(8,128)S(1)}, u32[]{:S(2)}, u32[]{:S(2)}) %collective-permute-start.14) | collective-permute-done | bytes 106528 | tf_op jit(solution)/shard_map/ppermute | solution.py:272
  90.4 2.6 %collective-permute-start.26 = (f32[1,13,16,128]{3,2,1,0:T(8,128)}, f32[1,13,16,128]{3,2,1,0:T(8,128)S(1)}, u32[]{:S(2)}, u32[]{:S(2)}) collective-permute-start(f32[1,13,16,128]{3,2,1,0:T(8,128)} %get-tuple-element.25.refs_4_), channel_id=1, source_target_pairs={{0,64},{32,96},{64,0},{96,32},{128,192},{160,224},{192,128},{224,1... | collective-permute-start | bytes 319496 | tf_op jit(solution)/shard_map/ppermute | solution.py:272
  94.7 2.3 %collective-permute-start.23 = (f32[1,14,16,128]{3,2,1,0:T(8,128)}, f32[1,14,16,128]{3,2,1,0:T(8,128)S(1)}, u32[]{:S(2)}, u32[]{:S(2)}) collective-permute-start(f32[1,14,16,128]{3,2,1,0:T(8,128)} %get-tuple-element.24.refs_0_), channel_id=1, source_target_pairs={{0,32},{32,0},{64,96},{96,64},{128,160},{160,128},{192,224},{224,1... | collective-permute-start | bytes 344072 | tf_op jit(solution)/shard_map/ppermute | solution.py:272
  97.9 2.0 %collective-permute-start.27 = (f32[2,13,16,128]{3,2,1,0:T(8,128)S(1)}, f32[2,13,16,128]{3,2,1,0:T(8,128)S(1)}, u32[]{:S(2)}, u32[]{:S(2)}) collective-permute-start(f32[2,13,16,128]{3,2,1,0:T(8,128)S(1)} %pad_maximum_fusion.4), channel_id=1, source_target_pairs={{0,32},{32,0},{64,96},{96,64},{128,160},{160,128},{192,224},{224,1... | collective-permute-start | bytes 638984 | tf_op jit(solution)/shard_map/ppermute | solution.py:272
  103.7 2.4 %collective-permute-start.30 = (f32[2,13,16,128]{3,2,1,0:T(8,128)S(1)}, f32[2,13,16,128]{3,2,1,0:T(8,128)S(1)}, u32[]{:S(2)}, u32[]{:S(2)}) collective-permute-start(f32[2,13,16,128]{3,2,1,0:T(8,128)S(1)} %pad_maximum_fusion.5), channel_id=1, source_target_pairs={{0,64},{32,96},{64,0},{96,32},{128,192},{160,224},{192,128},{224,1... | collective-permute-start | bytes 638984 | tf_op jit(solution)/shard_map/ppermute | solution.py:272
  108.0 3.0 %collective-permute-start.25 = (f32[4,14,16,128]{3,2,1,0:T(8,128)S(1)}, f32[4,14,16,128]{3,2,1,0:T(8,128)S(1)}, u32[]{:S(2)}, u32[]{:S(2)}) collective-permute-start(f32[4,14,16,128]{3,2,1,0:T(8,128)S(1)} %pad_maximum_fusion), channel_id=1, source_target_pairs={{0,64},{32,96},{64,0},{96,32},{128,192},{160,224},{192,128},{224,1... | collective-permute-start | bytes 1376264 | tf_op jit(solution)/shard_map/ppermute | solution.py:272
  113.8 8.6 %collective-permute-start.16 = (f32[8,128]{1,0:T(8,128)S(1)}, f32[8,128]{1,0:T(8,128)S(1)}, u32[]{:S(2)}, u32[]{:S(2)}) collective-permute-start(f32[8,128]{1,0:T(8,128)S(1)} %add.94), channel_id=1, source_target_pairs={{0,2},{1,3},{2,0},{3,1},{4,6},{5,7},{6,4},{7,5},{8,10},{9,11},{10,... | collective-permute-start | bytes 12296 | tf_op jit(solution)/shard_map/ppermute | solution.py:336
  124.0 17.5 %collective-permute-start.17 = (f32[8,128]{1,0:T(8,128)S(1)}, f32[8,128]{1,0:T(8,128)S(1)}, u32[]{:S(2)}, u32[]{:S(2)}) collective-permute-start(f32[8,128]{1,0:T(8,128)S(1)} %add.95), channel_id=1, source_target_pairs={{0,4},{1,5},{2,6},{3,7},{4,0},{5,1},{6,2},{7,3},{8,12},{9,13},{10,... | collective-permute-start | bytes 12296 | tf_op jit(solution)/shard_map/ppermute | solution.py:336
  143.1 10.1 %collective-permute-start.18 = (f32[8,128]{1,0:T(8,128)S(1)}, f32[8,128]{1,0:T(8,128)S(1)}, u32[]{:S(2)}, u32[]{:S(2)}) collective-permute-start(f32[8,128]{1,0:T(8,128)S(1)} %add.96), channel_id=1, source_target_pairs={{0,8},{1,9},{2,10},{3,11},{4,12},{5,13},{6,14},{7,15},{8,0},{9,1},... | collective-permute-start | bytes 12296 | tf_op jit(solution)/shard_map/ppermute | solution.py:336
  154.8 6.6 %collective-permute-start.19 = (f32[8,128]{1,0:T(8,128)S(1)}, f32[8,128]{1,0:T(8,128)S(1)}, u32[]{:S(2)}, u32[]{:S(2)}) collective-permute-start(f32[8,128]{1,0:T(8,128)S(1)} %add.97), channel_id=1, source_target_pairs={{0,16},{1,17},{2,18},{3,19},{4,20},{5,21},{6,22},{7,23},{8,24},{9,... | collective-permute-start | bytes 12296 | tf_op jit(solution)/shard_map/ppermute | solution.py:336
  163.0 3.6 %collective-permute-done.20 = f32[8,128]{1,0:T(8,128)S(1)} collective-permute-done((f32[8,128]{1,0:T(8,128)S(1)}, f32[8,128]{1,0:T(8,128)S(1)}, u32[]{:S(2)}, u32[]{:S(2)}) %collective-permute-start.20) | collective-permute-done | bytes 4128 | tf_op jit(solution)/shard_map/ppermute | solution.py:272
  166.8 3.4 %collective-permute-done.21 = f32[8,128]{1,0:T(8,128)S(1)} collective-permute-done((f32[8,128]{1,0:T(8,128)S(1)}, f32[8,128]{1,0:T(8,128)S(1)}, u32[]{:S(2)}, u32[]{:S(2)}) %collective-permute-start.21) | collective-permute-done | bytes 4128 | tf_op jit(solution)/shard_map/ppermute | solution.py:272
  170.3 3.5 %collective-permute-done.22 = f32[8,128]{1,0:T(8,128)S(1)} collective-permute-done((f32[8,128]{1,0:T(8,128)S(1)}, f32[8,128]{1,0:T(8,128)S(1)}, u32[]{:S(2)}, u32[]{:S(2)}) %collective-permute-start.22) | collective-permute-done | bytes 4128 | tf_op jit(solution)/shard_map/ppermute | solution.py:272
  173.8 3.3 %final.1 = (f32[4,8,128,128]{3,2,1,0:T(8,128)}, f32[8,128,128]{2,1,0:T(8,128)}) custom-call(s32[2]{0:T(128)S(1)} %copy-done.6, f32[8,5]{1,0:T(8,128)S(1)} %copy-done.5, f32[8,128]{1,0:T(8,128)S(1)} %add.101.sums, s32[8,128,128]{2,1,0:T(8,128)S(1)} %copy-done.1, f32[1,14,16,128]{3,2,1,0:T(8,128)S(1)} %copy-done.2, ...), custom_call_target="tpu_custom_call" | custom-call | tf_op jit(solution)/shard_map/final/pallas_call | solution.py:346
  (106 shorter events, 40.4 us)
Async XLA Ops:
  3.9 20.5 %collective-permute-start.3 = (f32[4,4,128,128]{3,2,1,0:T(8,128)}, f32[4,4,128,128]{3,2,1,0:T(8,128)}, u32[]{:S(2)}, u32[]{:S(2)}) collective-permute-start(f32[4,4,128,128]{3,2,1,0:T(8,128)} %get-tuple-element.43), channel_id=1, source_target_pairs={{1,2},{3,4},{5,6},{7,8},{9,10},{11,12},{13,14},{15,16},{17,18},{19... | collective-permute-start | bytes 3145736 | tf_op jit(solution)/shard_map/ppermute | solution.py:284
  5.7 18.8 %collective-permute-start.2 = (f32[4,4,128,128]{3,2,1,0:T(8,128)}, f32[4,4,128,128]{3,2,1,0:T(8,128)}, u32[]{:S(2)}, u32[]{:S(2)}) collective-permute-start(f32[4,4,128,128]{3,2,1,0:T(8,128)} %get-tuple-element.44), channel_id=1, source_target_pairs={{0,1},{1,0},{2,3},{3,2},{4,5},{5,4},{6,7},{7,6},{8,9},{9,8},{10,11... | collective-permute-start | bytes 3145736 | tf_op jit(solution)/shard_map/ppermute | solution.py:284
  8.5 7.1 %collective-permute-start.1 = (s32[4,128,128]{2,1,0:T(8,128)}, s32[4,128,128]{2,1,0:T(8,128)S(1)}, u32[]{:S(2)}, u32[]{:S(2)}) collective-permute-start(s32[4,128,128]{2,1,0:T(8,128)} %get-tuple-element.51), channel_id=1, source_target_pairs={{1,2},{3,4},{5,6},{7,8},{9,10},{11,12},{13,14},{15,16},{17,18},{19... | collective-permute-start | bytes 786440 | tf_op jit(solution)/shard_map/ppermute | solution.py:284
  10.1 14.4 %collective-permute-start.5 = (f32[4,2,128,128]{3,2,1,0:T(8,128)}, f32[4,2,128,128]{3,2,1,0:T(8,128)S(1)}, u32[]{:S(2)}, u32[]{:S(2)}) collective-permute-start(f32[4,2,128,128]{3,2,1,0:T(8,128)} %get-tuple-element.41), channel_id=1, source_target_pairs={{1,2},{3,4},{5,6},{7,8},{9,10},{11,12},{13,14},{15,16},{17,18},{19... | collective-permute-start | bytes 1572872 | tf_op jit(solution)/shard_map/ppermute | solution.py:284
  10.8 13.7 %collective-permute-start.4 = (f32[4,2,128,128]{3,2,1,0:T(8,128)S(1)}, f32[4,2,128,128]{3,2,1,0:T(8,128)S(1)}, u32[]{:S(2)}, u32[]{:S(2)}) collective-permute-start(f32[4,2,128,128]{3,2,1,0:T(8,128)S(1)} %get-tuple-element.42), channel_id=1, source_target_pairs={{0,1},{1,0},{2,3},{3,2},{4,5},{5,4},{6,7},{7,6},{8,9},{9,8},{10,11... | collective-permute-start | bytes 1572872 | tf_op jit(solution)/shard_map/ppermute | solution.py:284
  15.6 8.8 %collective-permute-start = (s32[4,128,128]{2,1,0:T(8,128)}, s32[4,128,128]{2,1,0:T(8,128)S(1)}, u32[]{:S(2)}, u32[]{:S(2)}) collective-permute-start(s32[4,128,128]{2,1,0:T(8,128)} %get-tuple-element.52), channel_id=1, source_target_pairs={{0,1},{1,0},{2,3},{3,2},{4,5},{5,4},{6,7},{7,6},{8,9},{9,8},{10,11... | collective-permute-start | bytes 786440 | tf_op jit(solution)/shard_map/ppermute | solution.py:284
  58.1 9.7 %collective-permute-start.8 = (f32[4,13,16,128]{3,2,1,0:T(8,128)}, f32[4,13,16,128]{3,2,1,0:T(8,128)S(1)}, u32[]{:S(2)}, u32[]{:S(2)}) collective-permute-start(f32[4,13,16,128]{3,2,1,0:T(8,128)} %get-tuple-element.20), channel_id=1, source_target_pairs={{0,192},{32,224},{64,128},{96,160},{128,64},{160,96},{192,0},{224,... | collective-permute-start | bytes 1277960 | tf_op jit(solution)/shard_map/ppermute | solution.py:272
  59.8 11.2 %collective-permute-start.10 = (f32[4,13,16,128]{3,2,1,0:T(8,128)}, f32[4,13,16,128]{3,2,1,0:T(8,128)S(1)}, u32[]{:S(2)}, u32[]{:S(2)}) collective-permute-start(f32[4,13,16,128]{3,2,1,0:T(8,128)} %get-tuple-element.22), channel_id=1, source_target_pairs={{0,32},{32,0},{64,96},{96,64},{128,160},{160,128},{192,224},{224,1... | collective-permute-start | bytes 1277960 | tf_op jit(solution)/shard_map/ppermute | solution.py:272
  61.7 12.0 %collective-permute-start.6 = (f32[4,14,16,128]{3,2,1,0:T(8,128)}, f32[4,14,16,128]{3,2,1,0:T(8,128)S(1)}, u32[]{:S(2)}, u32[]{:S(2)}) collective-permute-start(f32[4,14,16,128]{3,2,1,0:T(8,128)} %get-tuple-element.18), channel_id=1, source_target_pairs={{0,64},{32,96},{64,0},{96,32},{128,192},{160,224},{192,128},{224,1... | collective-permute-start | bytes 1376264 | tf_op jit(solution)/shard_map/ppermute | solution.py:272
  69.0 7.4 %collective-permute-start.9 = (f32[2,13,16,128]{3,2,1,0:T(8,128)S(1)}, f32[2,13,16,128]{3,2,1,0:T(8,128)S(1)}, u32[]{:S(2)}, u32[]{:S(2)}) collective-permute-start(f32[2,13,16,128]{3,2,1,0:T(8,128)S(1)} %get-tuple-element.50), channel_id=1, source_target_pairs={{0,32},{32,0},{64,96},{96,64},{128,160},{160,128},{192,224},{224,1... | collective-permute-start | bytes 638984 | tf_op jit(solution)/shard_map/ppermute | solution.py:272
  72.1 9.7 %collective-permute-start.11 = (f32[2,13,16,128]{3,2,1,0:T(8,128)S(1)}, f32[2,13,16,128]{3,2,1,0:T(8,128)S(1)}, u32[]{:S(2)}, u32[]{:S(2)}) collective-permute-start(f32[2,13,16,128]{3,2,1,0:T(8,128)S(1)} %get-tuple-element.48), channel_id=1, source_target_pairs={{0,64},{32,96},{64,0},{96,32},{128,192},{160,224},{192,128},{224,1... | collective-permute-start | bytes 638984 | tf_op jit(solution)/shard_map/ppermute | solution.py:272
  73.8 7.1 %collective-permute-start.7 = (f32[2,14,16,128]{3,2,1,0:T(8,128)S(1)}, f32[2,14,16,128]{3,2,1,0:T(8,128)S(1)}, u32[]{:S(2)}, u32[]{:S(2)}) collective-permute-start(f32[2,14,16,128]{3,2,1,0:T(8,128)S(1)} %get-tuple-element.46), channel_id=1, source_target_pairs={{0,192},{32,224},{64,128},{96,160},{128,64},{160,96},{192,0},{224,... | collective-permute-start | bytes 688136 | tf_op jit(solution)/shard_map/ppermute | solution.py:272
  77.1 7.6 %collective-permute-start.13 = (f32[1,13,16,128]{3,2,1,0:T(8,128)S(1)}, f32[1,13,16,128]{3,2,1,0:T(8,128)S(1)}, u32[]{:S(2)}, u32[]{:S(2)}) collective-permute-start(f32[1,13,16,128]{3,2,1,0:T(8,128)S(1)} %get-tuple-element.57), channel_id=1, source_target_pairs={{0,64},{32,96},{64,0},{96,32},{128,192},{160,224},{192,128},{224,1... | collective-permute-start | bytes 319496 | tf_op jit(solution)/shard_map/ppermute | solution.py:272
  93.0 9.7 %collective-permute-start.29 = (f32[1,13,16,128]{3,2,1,0:T(8,128)}, f32[1,13,16,128]{3,2,1,0:T(8,128)S(1)}, u32[]{:S(2)}, u32[]{:S(2)}) collective-permute-start(f32[1,13,16,128]{3,2,1,0:T(8,128)} %get-tuple-element.26.refs_8_), channel_id=1, source_target_pairs={{0,192},{32,224},{64,128},{96,160},{128,64},{160,96},{192,0},{224,... | collective-permute-start | bytes 319496 | tf_op jit(solution)/shard_map/ppermute | solution.py:272
  97.9 8.2 %collective-permute-start.27 = (f32[2,13,16,128]{3,2,1,0:T(8,128)S(1)}, f32[2,13,16,128]{3,2,1,0:T(8,128)S(1)}, u32[]{:S(2)}, u32[]{:S(2)}) collective-permute-start(f32[2,13,16,128]{3,2,1,0:T(8,128)S(1)} %pad_maximum_fusion.4), channel_id=1, source_target_pairs={{0,32},{32,0},{64,96},{96,64},{128,160},{160,128},{192,224},{224,1... | collective-permute-start | bytes 638984 | tf_op jit(solution)/shard_map/ppermute | solution.py:272
  101.1 6.8 %collective-permute-start.24 = (f32[2,14,16,128]{3,2,1,0:T(8,128)S(1)}, f32[2,14,16,128]{3,2,1,0:T(8,128)S(1)}, u32[]{:S(2)}, u32[]{:S(2)}) collective-permute-start(f32[2,14,16,128]{3,2,1,0:T(8,128)S(1)} %pad_maximum_fusion.3), channel_id=1, source_target_pairs={{0,192},{32,224},{64,128},{96,160},{128,64},{160,96},{192,0},{224,... | collective-permute-start | bytes 688136 | tf_op jit(solution)/shard_map/ppermute | solution.py:272
  103.7 7.4 %collective-permute-start.30 = (f32[2,13,16,128]{3,2,1,0:T(8,128)S(1)}, f32[2,13,16,128]{3,2,1,0:T(8,128)S(1)}, u32[]{:S(2)}, u32[]{:S(2)}) collective-permute-start(f32[2,13,16,128]{3,2,1,0:T(8,128)S(1)} %pad_maximum_fusion.5), channel_id=1, source_target_pairs={{0,64},{32,96},{64,0},{96,32},{128,192},{160,224},{192,128},{224,1... | collective-permute-start | bytes 638984 | tf_op jit(solution)/shard_map/ppermute | solution.py:272
  107.0 66.8 %collective-permute-start.28 = (f32[4,13,16,128]{3,2,1,0:T(8,128)S(1)}, f32[4,13,16,128]{3,2,1,0:T(8,128)S(1)}, u32[]{:S(2)}, u32[]{:S(2)}) collective-permute-start(f32[4,13,16,128]{3,2,1,0:T(8,128)S(1)} %pad_maximum_fusion.1), channel_id=1, source_target_pairs={{0,192},{32,224},{64,128},{96,160},{128,64},{160,96},{192,0},{224,... | collective-permute-start | bytes 1277960 | tf_op jit(solution)/shard_map/ppermute | solution.py:272
  108.0 65.8 %collective-permute-start.25 = (f32[4,14,16,128]{3,2,1,0:T(8,128)S(1)}, f32[4,14,16,128]{3,2,1,0:T(8,128)S(1)}, u32[]{:S(2)}, u32[]{:S(2)}) collective-permute-start(f32[4,14,16,128]{3,2,1,0:T(8,128)S(1)} %pad_maximum_fusion), channel_id=1, source_target_pairs={{0,64},{32,96},{64,0},{96,32},{128,192},{160,224},{192,128},{224,1... | collective-permute-start | bytes 1376264 | tf_op jit(solution)/shard_map/ppermute | solution.py:272
  111.1 62.7 %collective-permute-start.31 = (f32[4,13,16,128]{3,2,1,0:T(8,128)S(1)}, f32[4,13,16,128]{3,2,1,0:T(8,128)S(1)}, u32[]{:S(2)}, u32[]{:S(2)}) collective-permute-start(f32[4,13,16,128]{3,2,1,0:T(8,128)S(1)} %pad_maximum_fusion.2), channel_id=1, source_target_pairs={{0,32},{32,0},{64,96},{96,64},{128,160},{160,128},{192,224},{224,1... | collective-permute-start | bytes 1277960 | tf_op jit(solution)/shard_map/ppermute | solution.py:272
  113.8 10.2 %collective-permute-start.16 = (f32[8,128]{1,0:T(8,128)S(1)}, f32[8,128]{1,0:T(8,128)S(1)}, u32[]{:S(2)}, u32[]{:S(2)}) collective-permute-start(f32[8,128]{1,0:T(8,128)S(1)} %add.94), channel_id=1, source_target_pairs={{0,2},{1,3},{2,0},{3,1},{4,6},{5,7},{6,4},{7,5},{8,10},{9,11},{10,... | collective-permute-start | bytes 12296 | tf_op jit(solution)/shard_map/ppermute | solution.py:336
  124.0 19.1 %collective-permute-start.17 = (f32[8,128]{1,0:T(8,128)S(1)}, f32[8,128]{1,0:T(8,128)S(1)}, u32[]{:S(2)}, u32[]{:S(2)}) collective-permute-start(f32[8,128]{1,0:T(8,128)S(1)} %add.95), channel_id=1, source_target_pairs={{0,4},{1,5},{2,6},{3,7},{4,0},{5,1},{6,2},{7,3},{8,12},{9,13},{10,... | collective-permute-start | bytes 12296 | tf_op jit(solution)/shard_map/ppermute | solution.py:336
  143.1 11.7 %collective-permute-start.18 = (f32[8,128]{1,0:T(8,128)S(1)}, f32[8,128]{1,0:T(8,128)S(1)}, u32[]{:S(2)}, u32[]{:S(2)}) collective-permute-start(f32[8,128]{1,0:T(8,128)S(1)} %add.96), channel_id=1, source_target_pairs={{0,8},{1,9},{2,10},{3,11},{4,12},{5,13},{6,14},{7,15},{8,0},{9,1},... | collective-permute-start | bytes 12296 | tf_op jit(solution)/shard_map/ppermute | solution.py:336
  154.8 8.2 %collective-permute-start.19 = (f32[8,128]{1,0:T(8,128)S(1)}, f32[8,128]{1,0:T(8,128)S(1)}, u32[]{:S(2)}, u32[]{:S(2)}) collective-permute-start(f32[8,128]{1,0:T(8,128)S(1)} %add.97), channel_id=1, source_target_pairs={{0,16},{1,17},{2,18},{3,19},{4,20},{5,21},{6,22},{7,23},{8,24},{9,... | collective-permute-start | bytes 12296 | tf_op jit(solution)/shard_map/ppermute | solution.py:336
  (26 other events, 416.2 us)

commit v2 on v1

v2 whole, which is shorter than its diff:
```python
import functools

import jax
import jax.numpy as jnp
from jax import lax
from jax.experimental import pallas as pl
from jax.experimental.pallas import tpu as pltpu
from jax.sharding import PartitionSpec as P

STEP = 0.3
HF = 3
HM = 1
NP = 8
EXT = NP + 2 * HF
N = 128
PAD = 8
CHUNK = 32
F32 = jnp.float32

GENS = (2, 6, 1)
ORDERS = ((0, 1, 2), (1, 2, 0), (2, 0, 1))
PARTS = ((0, 14), (14, 27), (27, 40))
ROWS = 16


def code_of(part, slot):
    order = ORDERS[part]
    bits = (slot >> 2 & 1, slot >> 1 & 1, slot & 1)
    code = 0
    for dim, bit in zip(order, bits):
        code ^= GENS[dim] * bit
    return code


def slot_of(part, code):
    return [code_of(part, slot) for slot in range(8)].index(code)


def part_of(plane, field):
    at = plane * 5 + field
    for part, (first, last) in enumerate(PARTS):
        if at < last:
            return part, at - first


def shifts():
    source = lax.broadcasted_iota(jnp.int32, (2 * N, 2 * N), 0)
    target = lax.broadcasted_iota(jnp.int32, (2 * N, 2 * N), 1)
    x = jnp.where(source >= N, source - N, source)
    ahead = (target < N) & (x == target + 1)
    behind = (target >= N) & (x == target - N - 1)
    return jnp.where(ahead | behind, 1.0, 0.0).astype(jnp.bfloat16)


def two_terms(v):
    high = v.astype(jnp.bfloat16)
    low = (v - high.astype(F32)).astype(jnp.bfloat16)
    return jnp.concatenate([high, low], axis=1)


def pick(classes, entries):
    bit0 = (classes & 1) != 0
    bit1 = (classes & 2) != 0
    bit2 = (classes & 4) != 0
    low = [jnp.where(bit0, entries[2 * i + 1], entries[2 * i]) for i in range(4)]
    mid = [jnp.where(bit1, low[2 * i + 1], low[2 * i]) for i in range(2)]
    return jnp.where(bit2, mid[1], mid[0])


def pack_kernel(where, labels, start, meas, side_a, side_b, ints, sem):
    odd = lax.rem(where[0], 2)
    high_f, high_m = NP - HF, NP - HM
    copies = []
    for at, (out, flip) in enumerate(((side_a, 1 - odd), (side_b, odd))):
        copies.append(pltpu.make_async_copy(labels.at[pl.ds(flip * high_f, HF)], ints.at[at], sem.at[at, 8]))
        for l in range(4):
            copies.append(
                pltpu.make_async_copy(
                    start.at[l, pl.ds(flip * high_f, HF)], out.at[pl.ds(l * HF, HF)], sem.at[at, l]
                )
            )
            copies.append(
                pltpu.make_async_copy(
                    meas.at[l, pl.ds(flip * high_m, HM)], out.at[pl.ds(4 * HF + l * HM, HM)], sem.at[at, 4 + l]
                )
            )
    for copy in copies:
        copy.start()
    for copy in copies:
        copy.wait()
    for at, out in enumerate((side_a, side_b)):
        out[4 * (HF + HM) : 4 * (HF + HM) + HF] = ints[at].astype(F32)


def solve_kernel(
    where, spectra, absorb_t, half_t, labels, illum, start, meas, side_a, side_b,
    fluence, coef_a, coef_b, edge_a, edge_b, *rest,
):
    outs = rest[:6]
    own, shared, lit, step, near, near2, fl, hd, wys, tmp, adj, ab, wes, wws, wzs, inv, mis, ms, sem = rest[6:]
    sends, keeps = outs[0::2], outs[1::2]
    gz = where[0]
    me = where[1]
    odd = lax.rem(gz, 2)
    whole = pl.ds(PAD, N)
    copies = [
        pltpu.make_async_copy(labels, own, sem.at[0]),
        pltpu.make_async_copy(start, fl.at[:, pl.ds(HF, NP), whole], sem.at[1]),
        pltpu.make_async_copy(meas, ms.at[:, pl.ds(HM, NP)], sem.at[2]),
    ]
    label_copies = []
    side_copies = []
    for at, (side, high) in enumerate(((side_a, 1 - odd), (side_b, odd))):
        f_at = high * (HF + NP)
        m_at = high * (HM + NP)
        label_copies.append(
            pltpu.make_async_copy(side.at[pl.ds(4 * (HF + HM), HF)], shared.at[pl.ds(high * HF, HF)], sem.at[3 + at])
        )
        for l in range(4):
            side_copies.append(
                pltpu.make_async_copy(
                    side.at[pl.ds(l * HF, HF)], fl.at[l, pl.ds(f_at, HF), whole], sem.at[5 + 8 * at + l]
                )
            )
            side_copies.append(
                pltpu.make_async_copy(
                    side.at[pl.ds(4 * HF + l * HM, HM)], ms.at[l, pl.ds(m_at, HM)], sem.at[9 + 8 * at + l]
                )
            )
    for copy in label_copies + copies + side_copies:
        copy.start()

    lit[...] = illum[...].astype(F32)
    step[...] = shifts()
    pad = jnp.zeros((PAD, N), F32)

    def inside(e):
        z = gz * NP + e - HF
        return jnp.where((z >= 0) & (z < 32 * NP), 1.0, 0.0).astype(F32)

    def clear(e, _):
        for l in range(4):
            for field in (fl, tmp, adj, hd):
                field[l, e, 0:PAD] = pad
                field[l, e, PAD + N : 2 * PAD + N] = pad
        return 0

    lax.fori_loop(0, EXT, clear, 0)

    def optics(classes, e, r):
        there = inside(e)
        flat = pl.ds(r, CHUNK)
        rows = pl.ds(PAD + r, CHUNK)
        for l in range(4):
            ab[l, e, flat] = pick(classes, [absorb_t[l, i] for i in range(8)])
            hd[l, e, rows] = pick(classes, [half_t[l, i] * there for i in range(8)])

    def optics_own(p, _):
        for c in range(N // CHUNK):
            optics(own[p, pl.ds(c * CHUNK, CHUNK)], p + HF, c * CHUNK)
        return 0

    def optics_shared(p, _):
        e = p + jnp.where(p < HF, 0, NP)
        for c in range(N // CHUNK):
            classes = shared[p, pl.ds(c * CHUNK, CHUNK)].astype(jnp.int32)
            optics(classes, e, c * CHUNK)
        return 0

    copies[0].wait()
    lax.fori_loop(0, NP, optics_own, 0)
    for copy in label_copies:
        copy.wait()
    lax.fori_loop(0, 2 * HF, optics_shared, 0)
    for copy in copies[1:] + side_copies:
        copy.wait()

    @pl.when(gz == 0)
    def _():
        fl[:, HF - 1] = jnp.zeros((4, N + 2 * PAD, N), F32)

    @pl.when(gz == 31)
    def _():
        fl[:, HF + NP] = jnp.zeros((4, N + 2 * PAD, N), F32)

    def spread(to, field, l, first, last):
        rows = field[l, first:last, PAD : PAD + N].reshape((last - first) * N, N)
        both = jnp.dot(two_terms(rows), step[...], preferred_element_type=F32)
        to[first:last] = both.reshape(last - first, N, 2 * N)

    def per_plane(first, last, fields, body):
        def outerloop(l, _):
            for to, field in zip((near, near2), fields):
                spread(to, field, l, first, last)

            def innerloop(e, _):
                for c in range(N // CHUNK):
                    body(l, e, c * CHUNK)
                return 0

            lax.fori_loop(first, last, innerloop, 0)
            return 0

        lax.fori_loop(0, 4, outerloop, 0)

    def moved(field, l, e, r):
        flat = pl.ds(r, CHUNK)
        here = pl.ds(PAD + r, CHUNK)
        north = pl.ds(PAD + r + 1, CHUNK)
        south = pl.ds(PAD + r - 1, CHUNK)
        return (
            wzs[l, e, flat] * field[l, e + 1, here]
            + wzs[l, e - 1, flat] * field[l, e - 1, here]
            + wys[l, e, here] * field[l, e, north]
            + wys[l, e, south] * field[l, e, south]
            + wes[l, e, flat] * near[e, flat, 0:N]
            + wws[l, e, flat] * near[e, flat, N : 2 * N]
        )

    for l in range(4):
        for c in range(N // CHUNK):
            here = pl.ds(PAD + c * CHUNK, CHUNK)
            wzs[l, 0, pl.ds(c * CHUNK, CHUNK)] = hd[l, 0, here] + hd[l, 1, here]

    def first(l, e, r):
        flat = pl.ds(r, CHUNK)
        here = pl.ds(PAD + r, CHUNK)
        north_rows = pl.ds(PAD + r + 1, CHUNK)
        south_rows = pl.ds(PAD + r - 1, CHUNK)
        h = hd[l, e, here]
        north = h + hd[l, e, north_rows]
        south = h + hd[l, e, south_rows]
        above = h + hd[l, e + 1, here]
        below = wzs[l, e - 1, flat]
        east = h + near2[e, flat, 0:N]
        west = h + near2[e, flat, N : 2 * N]
        if r == 0:
            wys[l, e, 0:PAD] = jnp.broadcast_to(h[0:1], (PAD, N))
        wys[l, e, here] = north
        wzs[l, e, flat] = above
        wes[l, e, flat] = east
        wws[l, e, flat] = west
        total = ab[l, e, flat] + above + below + north + south + east + west
        scale = inside(e) / total
        inv[l, e, flat] = scale
        flow = (
            above * fl[l, e + 1, here]
            + below * fl[l, e - 1, here]
            + north * fl[l, e, north_rows]
            + south * fl[l, e, south_rows]
            + east * near[e, flat, 0:N]
            + west * near[e, flat, N : 2 * N]
        )
        tmp[l, e, here] = (spectra[l, 5] * lit[flat] + flow) * scale

    per_plane(1, EXT - 1, (fl, hd), first)

    def second(l, e, r):
        flat = pl.ds(r, CHUNK)
        here = pl.ds(PAD + r, CHUNK)
        scale = inv[l, e, flat]
        f = (spectra[l, 5] * lit[flat] + moved(tmp, l, e, r)) * scale
        fl[l, e, here] = f
        absorb = ab[l, e, flat]
        misfit = absorb * f - ms[l, e - (HF - HM), flat]
        mis[l, e, flat] = misfit
        adj[l, e, here] = absorb * misfit * scale

    per_plane(2, EXT - 2, (tmp,), second)
    write = pltpu.make_async_copy(fl.at[:, pl.ds(HF, NP), whole], fluence, sem.at[0])
    write.start()
    for l in range(4):
        tmp[l, HF - 1] = jnp.zeros((N + 2 * PAD, N), F32)
        tmp[l, HF + NP] = jnp.zeros((N + 2 * PAD, N), F32)

    def third(l, e, r):
        flat = pl.ds(r, CHUNK)
        here = pl.ds(PAD + r, CHUNK)
        tmp[l, e, here] = (ab[l, e, flat] * mis[l, e, flat] + moved(adj, l, e, r)) * inv[l, e, flat]

    per_plane(HF, HF + NP, (adj,), third)

    def couple(l, e, r):
        flat = pl.ds(r, CHUNK)
        here = pl.ds(PAD + r, CHUNK)
        north = pl.ds(PAD + r + 1, CHUNK)
        south = pl.ds(PAD + r - 1, CHUNK)
        h = hd[l, e, here]
        f = fl[l, e, here]
        a = tmp[l, e, here]
        total = (
            wes[l, e, flat] * (near[e, flat, 0:N] - f) * (near2[e, flat, 0:N] - a)
            + wws[l, e, flat] * (near[e, flat, N : 2 * N] - f) * (near2[e, flat, N : 2 * N] - a)
            + wys[l, e, here] * (fl[l, e, north] - f) * (tmp[l, e, north] - a)
            + wys[l, e, south] * (fl[l, e, south] - f) * (tmp[l, e, south] - a)
            + wzs[l, e, flat] * (fl[l, e + 1, here] - f) * (tmp[l, e + 1, here] - a)
            + wzs[l, e - 1, flat] * (fl[l, e - 1, here] - f) * (tmp[l, e - 1, here] - a)
        )
        ab[l, e, flat] = 12.0 * h * h * total

    per_plane(HF, HF + NP, (fl, tmp), couple)

    for coef, edge, high in ((coef_a, edge_a, 1 - odd), (coef_b, edge_b, odd)):
        e = HF + high * (NP - 1)
        beyond = e + 2 * high - 1
        face = e + high - 1
        for l in range(4):
            for c in range(N // CHUNK):
                here = pl.ds(PAD + c * CHUNK, CHUNK)
                to = pl.ds(c * CHUNK, CHUNK)
                h = hd[l, e, here]
                edge[l, to] = tmp[l, e, here]
                coef[l, to] = (
                    spectra[l, 4] * 12.0 * h * h * wzs[l, face, to] * (fl[l, beyond, here] - fl[l, e, here])
                )

    for code in range(8):
        rows = pl.ds(pl.multiple_of(PAD + (me ^ code) * ROWS, 8), ROWS)
        flat = pl.ds(pl.multiple_of((me ^ code) * ROWS, 8), ROWS)
        for plane in range(NP):
            e = plane + HF
            common = [fl[l, e, rows] * (mis[l, e, flat] - tmp[l, e, rows]) for l in range(4)]
            paired = [ab[l, e, flat] for l in range(4)]
            for field in range(5):
                terms = common if field < 4 else paired
                value = spectra[0, field] * terms[0]
                for l in range(1, 4):
                    value = value + spectra[l, field] * terms[l]
                part, index = part_of(plane, field)
                slot = slot_of(part, code)
                if slot >= 4:
                    sends[part][slot - 4, index] = value
                else:
                    keeps[part][slot, index] = value
    write.wait()


def edge_kernel(where, coef_a, coef_b, edge_a, edge_b, send, keep):
    gz, me = where[0], where[1]
    there = jnp.where((gz > 0) & (gz < 31), 1.0, 0.0).astype(F32)
    for code in range(8):
        rows = pl.ds(pl.multiple_of((me ^ code) * ROWS, ROWS), ROWS)
        slot = slot_of(0, code)
        for side, (coef, edge) in enumerate(((coef_a, edge_a), (coef_b, edge_b))):
            value = coef[0, rows] * edge[0, rows]
            for l in range(1, 4):
                value = value + coef[l, rows] * edge[l, rows]
            if side:
                value = value * there
            if slot >= 4:
                send[slot - 4, side] = value
            else:
                keep[slot, side] = value


def squares_kernel(where, late_keep, late_recv, *refs):
    keeps, recvs, owns, sums = refs[:3], refs[3:6], refs[6:9], refs[9]
    odd = lax.rem(where[0], 2)
    total = [jnp.zeros((8, N), F32) for _ in range(5)]
    for plane in range(NP):
        for field in range(5):
            part, index = part_of(plane, field)
            value = keeps[part][0, index] + recvs[part][0, index]
            if field == 4 and plane in (0, NP - 1):
                side = 1 - odd if plane == 0 else odd
                value = value + (late_keep[0, side] + late_recv[0, side])
            owns[part][0, index] = value
            squared = value * value
            total[field] = total[field] + squared[:8] + squared[8:]
    lane = lax.broadcasted_iota(jnp.int32, (1, N), 1)
    row = jnp.zeros((1, N), F32)
    for field in range(5):
        whole = jnp.sum(jnp.sum(total[field], axis=0, keepdims=True), axis=1, keepdims=True)
        row = jnp.where(lane == field, whole, row)
    for target in range(32):
        sums[target] = row


def final_kernel(where, table, labels, *refs):
    pieces, conc, scat = refs[:12], refs[12], refs[13]
    me = where[1]
    cells = 32 * NP * N * N
    extra = PARTS[0][1]
    total = pieces[0][0, extra] + pieces[1][0, extra]
    for i in range(2):
        total = total + pieces[2][i, extra]
    for i in range(4):
        total = total + pieces[3][i, extra]
    factor = -STEP / jnp.sqrt(total / cells + 1e-06)
    factors = [jnp.broadcast_to(factor[:, c : c + 1], (ROWS, N)) for c in range(5)]
    for code in range(8):
        at = pl.multiple_of((me ^ code) * ROWS, ROWS)
        rows = pl.ds(at, ROWS)
        for plane in range(NP):
            classes = labels[plane, rows]
            for field in range(5):
                part, index = part_of(plane, field)
                slot = slot_of(part, code)
                own, one, two, four = pieces[4 * part : 4 * part + 4]
                if slot == 0:
                    grad = own[0, index]
                elif slot == 1:
                    grad = one[0, index]
                elif slot < 4:
                    grad = two[slot - 2, index]
                else:
                    grad = four[slot - 4, index]
                coeff = pick(classes, [table[i, field] for i in range(8)])
                value = coeff * jnp.exp(grad * factors[field])
                if field < 4:
                    conc[field, plane, rows] = value
                else:
                    scat[plane, rows] = value


VMEM = pl.BlockSpec(memory_space=pltpu.VMEM)
SMEM = pl.BlockSpec(memory_space=pltpu.SMEM)
ANY = pl.BlockSpec(memory_space=pl.ANY)


def swap(x, code):
    return lax.ppermute(x, "wl", [(i, i ^ code) for i in range(8)])


ON_CHIP = [(i, i ^ 1) for i in range(32)]
OFF_CHIP = [(i, (i + 1 if i % 2 else i - 1) % 32) for i in range(32)]


def beside(a, b):
    return lax.ppermute(a, "gz", ON_CHIP), lax.ppermute(b, "gz", OFF_CHIP)


def after(x, *others):
    return lax.optimization_barrier((x, *others))[0]


def shards(labels, label_table, spectra, illumination, fluence_start, measured):
    where = jnp.stack([lax.axis_index("gz"), lax.axis_index("wl")]).astype(jnp.int32)
    packed = 4 * (HF + HM) + HF
    side_a, side_b = pl.pallas_call(
        pack_kernel,
        out_shape=[jax.ShapeDtypeStruct((packed, N, N), F32)] * 2,
        in_specs=[SMEM] + [ANY] * 3,
        out_specs=[VMEM] * 2,
        scratch_shapes=[pltpu.VMEM((2, HF, N, N), jnp.int32), pltpu.SemaphoreType.DMA((2, 9))],
        name="pack",
    )(where, labels, fluence_start, measured)
    side_a, side_b = beside(side_a, side_b)

    absorb_t = spectra[:, 0, None] * label_table[None, :, 0]
    for c in range(1, 4):
        absorb_t = absorb_t + spectra[:, c, None] * label_table[None, :, c]
    half_t = 0.5 / (3.0 * (absorb_t + spectra[:, 4, None] * label_table[None, :, 4]))

    sizes = [last - first for first, last in PARTS]
    field = pltpu.VMEM((4, EXT, N + 2 * PAD, N), F32)
    plane = jax.ShapeDtypeStruct((4, N, N), F32)
    fluence, coef_a, coef_b, edge_a, edge_b, *out = pl.pallas_call(
        solve_kernel,
        out_shape=[jax.ShapeDtypeStruct((4, NP, N, N), F32)]
        + [plane] * 4
        + [jax.ShapeDtypeStruct((4, size, ROWS, N), F32) for size in sizes for _ in range(2)],
        in_specs=[SMEM] * 4 + [ANY] + [VMEM] + [ANY] * 4,
        out_specs=[ANY] + [VMEM] * 10,
        scratch_shapes=[
            pltpu.VMEM((NP, N, N), jnp.int32),
            pltpu.VMEM((2 * HF, N, N), F32),
            pltpu.VMEM((N, N), F32),
            pltpu.VMEM((2 * N, 2 * N), jnp.bfloat16),
        ]
        + [pltpu.VMEM((EXT, N, 2 * N), F32)] * 2
        + [field] * 5
        + [pltpu.VMEM((4, EXT, N, N), F32)] * 6
        + [pltpu.VMEM((4, NP + 2 * HM, N, N), F32), pltpu.SemaphoreType.DMA((21,))],
        compiler_params=pltpu.CompilerParams(vmem_limit_bytes=57 * 2**20),
        name="solve",
    )(where, spectra, absorb_t, half_t, labels, illumination, fluence_start, measured, side_a, side_b)
    sends = list(out[0::2])
    keeps = list(out[1::2])

    far_a, far_b = beside(edge_a, edge_b)
    for phase in range(2):
        recvs = [swap(sends[q], GENS[ORDERS[q][phase]]) for q in range(3)]
        half = keeps[0].shape[0] // 2
        sends = [keeps[q][half:] + recvs[q][half:] for q in range(3)]
        keeps = [keeps[q][:half] + recvs[q][:half] for q in range(3)]
        if phase == 0:
            far_a, far_b = lax.optimization_barrier((far_a, far_b, *sends))[:2]
    recvs = [swap(sends[q], GENS[ORDERS[q][2]]) for q in range(3)]

    late_send, late_keep = pl.pallas_call(
        edge_kernel,
        out_shape=[jax.ShapeDtypeStruct((4, 2, ROWS, N), F32)] * 2,
        in_specs=[SMEM] + [VMEM] * 4,
        out_specs=[VMEM] * 2,
        name="edge",
    )(where, coef_a, coef_b, far_a, far_b)
    for phase in range(2):
        late_recv = swap(late_send, GENS[ORDERS[0][phase]])
        half = late_keep.shape[0] // 2
        late_send = late_keep[half:] + late_recv[half:]
        late_keep = late_keep[:half] + late_recv[:half]
    late_recv = swap(late_send, GENS[ORDERS[0][2]])

    *owns, sums = pl.pallas_call(
        squares_kernel,
        out_shape=[jax.ShapeDtypeStruct((1, size, ROWS, N), F32) for size in sizes]
        + [jax.ShapeDtypeStruct((32, 1, N), F32)],
        in_specs=[SMEM] + [VMEM] * 8,
        out_specs=[VMEM] * 4,
        name="squares",
    )(where, late_keep, late_recv, *keeps, *recvs)

    steps = {q: [owns[q]] for q in (1, 2)}
    for phase in (2, 1, 0):
        for q in (1, 2):
            have = steps[q]
            mine = have[0] if len(have) == 1 else jnp.concatenate(have)
            have.append(swap(mine, GENS[ORDERS[q][phase]]))
    slab = jnp.sum(lax.all_to_all(sums, "gz", 0, 0), axis=0)
    steps[0] = [jnp.concatenate([owns[0], jnp.broadcast_to(slab[None, None], (1, 1, ROWS, N))], axis=1)]
    for phase in (2, 1, 0):
        have = steps[0]
        mine = have[0] if len(have) == 1 else jnp.concatenate(have)
        have.append(swap(mine, GENS[ORDERS[0][phase]]))
    pieces = steps[0] + steps[1] + steps[2]
    conc, scat = pl.pallas_call(
        final_kernel,
        out_shape=[jax.ShapeDtypeStruct((4, NP, N, N), F32), jax.ShapeDtypeStruct((NP, N, N), F32)],
        in_specs=[SMEM] * 2 + [VMEM] * 13,
        out_specs=[VMEM] * 2,
        compiler_params=pltpu.CompilerParams(vmem_limit_bytes=32 * 2**20),
        name="final",
    )(where, label_table, labels, *pieces)
    return fluence, conc, scat


def solution(mesh):
    in_specs = (
        P("gz", None, None),
        P(),
        P("wl", None),
        P(),
        P("wl", "gz", None, None),
        P("wl", "gz", None, None),
    )
    out_specs = (P("wl", "gz", None, None), P(None, "gz", None, None), P("gz", None, None))
    return jax.shard_map(shards, mesh=mesh, in_specs=in_specs, out_specs=out_specs, check_vma=False)
```

time: 178 us -> 157 us (0.88)
  starting transfers between devices: 92.6 us -> 40.3 us
  waiting for transfers between devices: 29.3 us -> 62.7 us
  local copies, waits for them, and re-layouts: 7.19 us -> 2.98 us
  other arithmetic: 9.29 us -> 11.7 us
    ppermute x11 -> x4, starting transfers between devices: 59.6 us -> 13.4 us  [beside(): return (lax.ppermute(a, 'gz', ON_CHIP), lax.ppermute(b, 'gz', OFF_CHIP))]
    ppermute x11 -> x4, waiting for transfers between devices: 7.62 us -> 29.8 us  [beside(): return (lax.ppermute(a, 'gz', ON_CHIP), lax.ppermute(b, 'gz', OFF_CHIP))]
    ppermute x21, starting transfers between devices: 33 us -> 21.2 us  [swap(): return lax.ppermute(x, 'wl', [(i, i ^ code) for i in range(8)])]
    all_to_all x0 -> x1, waiting for transfers between devices: none -> 8.87 us  [shards(): slab = jnp.sum(lax.all_to_all(sums, 'gz', 0, 0), axis=0)]
    pallas_call x1, Pallas kernels: 32.7 us -> 26.4 us  [shards(): pl.pallas_call(solve_kernel, out_shape=[jax.ShapeDtypeStruct((4, NP, N, N...]
    pallas_call x0 -> x2, Pallas kernels: none -> 6.06 us  [the longest x1 4.14 us: shards(): pl.pallas_call(pack_kernel, out_shape=[jax.ShapeDtypeStruct((packed, N, N...]
    all_to_all x0 -> x1, starting transfers between devices: none -> 5.76 us  [shards(): slab = jnp.sum(lax.all_to_all(sums, 'gz', 0, 0), axis=0)]
    dynamic_slice x3 -> x0, local copies, waits for them, and re-layouts: 4.96 us -> none  [halo(): b = lax.dynamic_slice_in_dim(x, jnp.where(odd == 0, 0, high), width, axis)]
  transfers between devices with their start and end apart: 32 -> 26, of which waited for: 14 -> 12; matrix products, arithmetic and copies ran while one was open for 6% -> 7% of each run, Pallas kernels for 0% -> 0%
where the time goes in v2:
time: 157 us; the launch traced here: 156 us
  waiting for transfers between devices  62.7 us (40%)
  starting transfers between devices  40.3 us (26%)
  Pallas kernels  37.8 us (24%)
  other arithmetic  11.7 us (7%)
  local copies, waits for them, and re-layouts  2.98 us (2%)
    ppermute x4, waiting for transfers between devices, beside(): return (lax.ppermute(a, 'gz', ON_CHIP), lax.ppermute(b, 'gz', OFF_CHIP))  29.8 us
    pallas_call x1, Pallas kernels, shards(): pl.pallas_call(solve_kernel, out_shape=[jax.ShapeDtypeStruct((4, NP, N, N...  26.4 us
    ppermute x21, waiting for transfers between devices, swap(): return lax.ppermute(x, 'wl', [(i, i ^ code) for i in range(8)])  24 us
    ppermute x21, starting transfers between devices, swap(): return lax.ppermute(x, 'wl', [(i, i ^ code) for i in range(8)])  21.2 us
    ppermute x4, starting transfers between devices, beside(): return (lax.ppermute(a, 'gz', ON_CHIP), lax.ppermute(b, 'gz', OFF_CHIP))  13.4 us
    all_to_all x1, waiting for transfers between devices, shards(): slab = jnp.sum(lax.all_to_all(sums, 'gz', 0, 0), axis=0)  8.87 us
    all_to_all x1, starting transfers between devices, shards(): slab = jnp.sum(lax.all_to_all(sums, 'gz', 0, 0), axis=0)  5.76 us
    pallas_call x1, Pallas kernels, shards(): pl.pallas_call(pack_kernel, out_shape=[jax.ShapeDtypeStruct((packed, N, N...  4.14 us
  transfers between devices with their start and end apart: 26, of which 12 were waited for; matrix products, arithmetic and copies ran while one was open for 7% of the time, Pallas kernels for 0%

profile of v2, /device:TPU:8, one launch (start us, length us, event | category | flops | bytes accessed | tf_op | source)
XLA Modules:
  0.0 156.3 jit_solution(11802130207743140691)
XLA Ops:
  1.3 4.1 %pack.1 = (f32[19,128,128]{2,1,0:T(8,128)}, f32[19,128,128]{2,1,0:T(8,128)}) custom-call(s32[2]{0:T(128)} %pad_add_fusion.where, s32[8,128,128]{2,1,0:T(8,128)} %labels.5, f32[4,8,128,128]{3,2,1,0:T(8,128)} %start.3, f32[4,8,128,128]{3,2,1,0:T(8,128)} %meas.3), custom_call_target="tpu_custom_call" | custom-call | tf_op jit(solution)/shard_map/pack/pallas_call | solution.py:440
  5.6 8.6 %collective-permute-start.1 = (f32[19,128,128]{2,1,0:T(8,128)}, f32[19,128,128]{2,1,0:T(8,128)S(1)}, u32[]{:S(2)}, u32[]{:S(2)}) collective-permute-start(f32[19,128,128]{2,1,0:T(8,128)} %get-tuple-element.27), channel_id=1, source_target_pairs={{0,31},{1,2},{2,1},{3,4},{4,3},{5,6},{6,5},{7,8},{8,7},{9,10},{10,... | collective-permute-start | bytes 3735560 | tf_op jit(solution)/shard_map/ppermute | solution.py:430
  15.4 26.9 %collective-permute-done.1.side_b = f32[19,128,128]{2,1,0:T(8,128)S(1)} collective-permute-done((f32[19,128,128]{2,1,0:T(8,128)}, f32[19,128,128]{2,1,0:T(8,128)S(1)}, u32[]{:S(2)}, u32[]{:S(2)}) %collective-permute-start.1) | collective-permute-done | bytes 1245216 | tf_op jit(solution)/shard_map/ppermute | solution.py:430
  43.3 26.4 %solve.1 = (f32[4,8,128,128]{3,2,1,0:T(8,128)}, f32[4,128,128]{2,1,0:T(8,128)}, f32[4,128,128]{2,1,0:T(8,128)}, f32[4,128,128]{2,1,0:T(8,128)}, f32[4,128,128]{2...) custom-call(s32[2]{0:T(128)} %pad_add_fusion.where, ...), custom_call_target="tpu_custom_call" | custom-call | tf_op jit(solution)/shard_map/solve/pallas_call | solution.py:458
  72.4 4.7 %collective-permute-start.3 = (f32[4,128,128]{2,1,0:T(8,128)}, f32[4,128,128]{2,1,0:T(8,128)S(1)}, u32[]{:S(2)}, u32[]{:S(2)}) collective-permute-start(f32[4,128,128]{2,1,0:T(8,128)} %get-tuple-element.32), channel_id=1, source_target_pairs={{0,31},{1,2},{2,1},{3,4},{4,3},{5,6},{6,5},{7,8},{8,7},{9,10},{10,... | collective-permute-start | bytes 786440 | tf_op jit(solution)/shard_map/ppermute | solution.py:430
  77.1 1.9 %collective-permute-start.4 = (f32[4,14,16,128]{3,2,1,0:T(8,128)}, f32[4,14,16,128]{3,2,1,0:T(8,128)S(1)}, u32[]{:S(2)}, u32[]{:S(2)}) collective-permute-start(f32[4,14,16,128]{3,2,1,0:T(8,128)} %get-tuple-element.34), channel_id=1, source_target_pairs={{0,64},{32,96},{64,0},{96,32},{128,192},{160,224},{192,128},{224,1... | collective-permute-start | bytes 1376264 | tf_op jit(solution)/shard_map/ppermute | solution.py:422
  80.1 1.7 %collective-permute-done.6 = f32[4,13,16,128]{3,2,1,0:T(8,128)S(1)} collective-permute-done((f32[4,13,16,128]{3,2,1,0:T(8,128)}, f32[4,13,16,128]{3,2,1,0:T(8,128)S(1)}, u32[]{:S(2)}, u32[]{:S(2)}) %collective-permute-start.6) | collective-permute-done | bytes 426016 | tf_op jit(solution)/shard_map/ppermute | solution.py:422
  82.8 3.0 %collective-permute-done.4 = f32[4,14,16,128]{3,2,1,0:T(8,128)S(1)} collective-permute-done((f32[4,14,16,128]{3,2,1,0:T(8,128)}, f32[4,14,16,128]{3,2,1,0:T(8,128)S(1)}, u32[]{:S(2)}, u32[]{:S(2)}) %collective-permute-start.4) | collective-permute-done | bytes 458784 | tf_op jit(solution)/shard_map/ppermute | solution.py:422
  85.9 2.9 %collective-permute-done.3.edge_b = f32[4,128,128]{2,1,0:T(8,128)S(1)} collective-permute-done((f32[4,128,128]{2,1,0:T(8,128)}, f32[4,128,128]{2,1,0:T(8,128)S(1)}, u32[]{:S(2)}, u32[]{:S(2)}) %collective-permute-start.3) | collective-permute-done | bytes 262176 | tf_op jit(solution)/shard_map/ppermute | solution.py:430
  89.4 1.9 %edge.1 = (f32[4,2,16,128]{3,2,1,0:T(8,128)}, f32[4,2,16,128]{3,2,1,0:T(8,128)}) custom-call(s32[2]{0:T(128)} %pad_add_fusion.where, f32[4,128,128]{2,1,0:T(8,128)} %get-tuple-element.29.coef_a, f32[4,128,128]{2,1,0:T(8,128)} %get-tuple-element.30.coef_b, f32[4,128,128]{2,1,0:T(8,128)} %copy-done.9, f32[4,128,128]{2,1,0:T(8,128)} %copy-done.10), custom_call_target="tpu_custom_call" | custom-call | tf_op jit(solution)/shard_map/edge/pallas_call | solution.py:491
  91.4 1.9 %collective-permute-start.7 = (f32[4,2,16,128]{3,2,1,0:T(8,128)}, f32[4,2,16,128]{3,2,1,0:T(8,128)S(1)}, u32[]{:S(2)}, u32[]{:S(2)}) collective-permute-start(f32[4,2,16,128]{3,2,1,0:T(8,128)} %get-tuple-element.42), channel_id=1, source_target_pairs={{0,64},{32,96},{64,0},{96,32},{128,192},{160,224},{192,128},{224,1... | collective-permute-start | bytes 196616 | tf_op jit(solution)/shard_map/ppermute | solution.py:422
  93.8 2.0 %collective-permute-done.7 = f32[4,2,16,128]{3,2,1,0:T(8,128)S(1)} collective-permute-done((f32[4,2,16,128]{3,2,1,0:T(8,128)}, f32[4,2,16,128]{3,2,1,0:T(8,128)S(1)}, u32[]{:S(2)}, u32[]{:S(2)}) %collective-permute-start.7) | collective-permute-done | bytes 65568 | tf_op jit(solution)/shard_map/ppermute | solution.py:422
  97.2 2.9 %collective-permute-done.11 = f32[2,13,16,128]{3,2,1,0:T(8,128)S(1)} collective-permute-done((f32[2,13,16,128]{3,2,1,0:T(8,128)S(1)}, f32[2,13,16,128]{3,2,1,0:T(8,128)S(1)}, u32[]{:S(2)}, u32[]{:S(2)}) %collective-permute-start.11) | collective-permute-done | bytes 213024 | tf_op jit(solution)/shard_map/ppermute | solution.py:422
  104.0 1.8 %collective-permute-start.9 = (f32[1,2,16,128]{3,2,1,0:T(8,128)S(1)}, f32[1,2,16,128]{3,2,1,0:T(8,128)S(1)}, u32[]{:S(2)}, u32[]{:S(2)}) collective-permute-start(f32[1,2,16,128]{3,2,1,0:T(8,128)S(1)} %get-tuple-element.75), channel_id=1, source_target_pairs={{0,32},{32,0},{64,96},{96,64},{128,160},{160,128},{192,224},{224,1... | collective-permute-start | bytes 49160 | tf_op jit(solution)/shard_map/ppermute | solution.py:422
  105.9 2.3 %collective-permute-done.9.late_recv = f32[1,2,16,128]{3,2,1,0:T(8,128)S(1)} collective-permute-done((f32[1,2,16,128]{3,2,1,0:T(8,128)S(1)}, f32[1,2,16,128]{3,2,1,0:T(8,128)S(1)}, u32[]{:S(2)}, u32[]{:S(2)}) %collective-permute-start.9) | collective-permute-done | bytes 16416 | tf_op jit(solution)/shard_map/ppermute | solution.py:422
  108.9 2.0 %squares.1 = (f32[1,14,16,128]{3,2,1,0:T(8,128)}, f32[1,13,16,128]{3,2,1,0:T(8,128)}, f32[1,13,16,128]{3,2,1,0:T(8,128)}, f32[32,1,128]{2,1,0:T(1,128)}) custom-call(s32[2]{0:T(128)} %pad_add_fusion.where, f32[1,2,16,128]{3,2,1,0:T(8,128)} %get-tuple-element.76.late_keep, f32[1,2,16,128]{3,2,1,0:T(8,128)} %copy-done.15, ...), custom_call_target="tpu_custom_call" | custom-call | tf_op jit(solution)/shard_map/squares/pallas_call | solution.py:505
  110.9 5.8 %all-to-all-start = ((f32[32,1,128]{2,1,0:T(1,128)}), f32[32,1,128]{2,1,0:T(1,128)S(1)}, u32[]{:S(2)}, u32[]{:S(2)}) async-start(f32[32,1,128]{2,1,0:T(1,128)} %get-tuple-element.44), calls=%async_computation | async-start | bytes 32768 | tf_op jit(solution)/shard_map/all_to_all | solution.py:520
  117.6 8.9 %all-to-all-done = f32[32,1,128]{2,1,0:T(1,128)S(1)} async-done(((f32[32,1,128]{2,1,0:T(1,128)}), f32[32,1,128]{2,1,0:T(1,128)S(1)}, u32[]{:S(2)}, u32[]{:S(2)}) %all-to-all-start) | async-done | bytes 16416 | tf_op jit(solution)/shard_map/all_to_all | solution.py:520
  131.1 2.3 %collective-permute-done.16.refs_1_ = f32[1,15,16,128]{3,2,1,0:T(8,128)S(1)} collective-permute-done((f32[1,15,16,128]{3,2,1,0:T(8,128)S(1)}, f32[1,15,16,128]{3,2,1,0:T(8,128)S(1)}, u32[]{:S(2)}, u32[]{:S(2)}) %collective-permute-start.16) | collective-permute-done | bytes 122912 | tf_op jit(solution)/shard_map/ppermute | solution.py:422
  135.3 2.8 %collective-permute-start.23 = (f32[2,13,16,128]{3,2,1,0:T(8,128)S(1)}, f32[2,13,16,128]{3,2,1,0:T(8,128)S(1)}, u32[]{:S(2)}, u32[]{:S(2)}) collective-permute-start(f32[2,13,16,128]{3,2,1,0:T(8,128)S(1)} %pad_maximum_fusion.5), channel_id=1, source_target_pairs={{0,64},{32,96},{64,0},{96,32},{128,192},{160,224},{192,128},{224,1... | collective-permute-start | bytes 638984 | tf_op jit(solution)/shard_map/ppermute | solution.py:422
  141.0 2.9 %collective-permute-start.18 = (f32[4,15,16,128]{3,2,1,0:T(8,128)S(1)}, f32[4,15,16,128]{3,2,1,0:T(8,128)S(1)}, u32[]{:S(2)}, u32[]{:S(2)}) collective-permute-start(f32[4,15,16,128]{3,2,1,0:T(8,128)S(1)} %pad_maximum_fusion), channel_id=1, source_target_pairs={{0,64},{32,96},{64,0},{96,32},{128,192},{160,224},{192,128},{224,1... | collective-permute-start | bytes 1474568 | tf_op jit(solution)/shard_map/ppermute | solution.py:422
  144.4 5.3 %collective-permute-done.21.refs_7_ = f32[4,13,16,128]{3,2,1,0:T(8,128)S(1)} collective-permute-done((f32[4,13,16,128]{3,2,1,0:T(8,128)S(1)}, f32[4,13,16,128]{3,2,1,0:T(8,128)S(1)}, u32[]{:S(2)}, u32[]{:S(2)}) %collective-permute-start.21) | collective-permute-done | bytes 426016 | tf_op jit(solution)/shard_map/ppermute | solution.py:422
  149.7 3.2 %collective-permute-done.24.refs_11_ = f32[4,13,16,128]{3,2,1,0:T(8,128)S(1)} collective-permute-done((f32[4,13,16,128]{3,2,1,0:T(8,128)S(1)}, f32[4,13,16,128]{3,2,1,0:T(8,128)S(1)}, u32[]{:S(2)}, u32[]{:S(2)}) %collective-permute-start.24) | collective-permute-done | bytes 426016 | tf_op jit(solution)/shard_map/ppermute | solution.py:422
  153.0 3.3 %final.1 = (f32[4,8,128,128]{3,2,1,0:T(8,128)}, f32[8,128,128]{2,1,0:T(8,128)}) custom-call(s32[2]{0:T(128)S(1)} %copy-done.4, f32[8,5]{1,0:T(8,128)S(1)} %copy-done.3, s32[8,128,128]{2,1,0:T(8,128)S(1)} %copy-done, f32[1,15,16,128]{3,2,1,0:T(8,128)S(1)} %pad_maximum_fusion.6.refs_0_, f32[1,15,16,128]{3,2,1,0:T(8,128)S(1)} %collective-permute-done.16.refs_1_, ...), custom_call_target="tpu_custom_call" | custom-call | tf_op jit(solution)/shard_map/final/pallas_call | solution.py:527
  (86 shorter events, 26.0 us)
Async XLA Ops:
  5.5 9.9 %collective-permute-start = (f32[19,128,128]{2,1,0:T(8,128)}, f32[19,128,128]{2,1,0:T(8,128)S(1)}, u32[]{:S(2)}, u32[]{:S(2)}) collective-permute-start(f32[19,128,128]{2,1,0:T(8,128)} %get-tuple-element.26), channel_id=1, source_target_pairs={{0,1},{1,0},{2,3},{3,2},{4,5},{5,4},{6,7},{7,6},{8,9},{9,8},{10,11... | collective-permute-start | bytes 3735560 | tf_op jit(solution)/shard_map/ppermute | solution.py:430
  5.6 36.7 %collective-permute-start.1 = (f32[19,128,128]{2,1,0:T(8,128)}, f32[19,128,128]{2,1,0:T(8,128)S(1)}, u32[]{:S(2)}, u32[]{:S(2)}) collective-permute-start(f32[19,128,128]{2,1,0:T(8,128)} %get-tuple-element.27), channel_id=1, source_target_pairs={{0,31},{1,2},{2,1},{3,4},{4,3},{5,6},{6,5},{7,8},{8,7},{9,10},{10,... | collective-permute-start | bytes 3735560 | tf_op jit(solution)/shard_map/ppermute | solution.py:430
  69.7 9.3 %collective-permute-start.5 = (f32[4,13,16,128]{3,2,1,0:T(8,128)}, f32[4,13,16,128]{3,2,1,0:T(8,128)S(1)}, u32[]{:S(2)}, u32[]{:S(2)}) collective-permute-start(f32[4,13,16,128]{3,2,1,0:T(8,128)} %get-tuple-element.36), channel_id=1, source_target_pairs={{0,192},{32,224},{64,128},{96,160},{128,64},{160,96},{192,0},{224,... | collective-permute-start | bytes 1277960 | tf_op jit(solution)/shard_map/ppermute | solution.py:422
  71.4 10.3 %collective-permute-start.6 = (f32[4,13,16,128]{3,2,1,0:T(8,128)}, f32[4,13,16,128]{3,2,1,0:T(8,128)S(1)}, u32[]{:S(2)}, u32[]{:S(2)}) collective-permute-start(f32[4,13,16,128]{3,2,1,0:T(8,128)} %get-tuple-element.38), channel_id=1, source_target_pairs={{0,32},{32,0},{64,96},{96,64},{128,160},{160,128},{192,224},{224,1... | collective-permute-start | bytes 1277960 | tf_op jit(solution)/shard_map/ppermute | solution.py:422
  72.4 13.4 %collective-permute-start.2 = (f32[4,128,128]{2,1,0:T(8,128)}, f32[4,128,128]{2,1,0:T(8,128)S(1)}, u32[]{:S(2)}, u32[]{:S(2)}) collective-permute-start(f32[4,128,128]{2,1,0:T(8,128)} %get-tuple-element.31), channel_id=1, source_target_pairs={{0,1},{1,0},{2,3},{3,2},{4,5},{5,4},{6,7},{7,6},{8,9},{9,8},{10,11... | collective-permute-start | bytes 786440 | tf_op jit(solution)/shard_map/ppermute | solution.py:430
  72.4 16.3 %collective-permute-start.3 = (f32[4,128,128]{2,1,0:T(8,128)}, f32[4,128,128]{2,1,0:T(8,128)S(1)}, u32[]{:S(2)}, u32[]{:S(2)}) collective-permute-start(f32[4,128,128]{2,1,0:T(8,128)} %get-tuple-element.32), channel_id=1, source_target_pairs={{0,31},{1,2},{2,1},{3,4},{4,3},{5,6},{6,5},{7,8},{8,7},{9,10},{10,... | collective-permute-start | bytes 786440 | tf_op jit(solution)/shard_map/ppermute | solution.py:430
  77.1 8.7 %collective-permute-start.4 = (f32[4,14,16,128]{3,2,1,0:T(8,128)}, f32[4,14,16,128]{3,2,1,0:T(8,128)S(1)}, u32[]{:S(2)}, u32[]{:S(2)}) collective-permute-start(f32[4,14,16,128]{3,2,1,0:T(8,128)} %get-tuple-element.34), channel_id=1, source_target_pairs={{0,64},{32,96},{64,0},{96,32},{128,192},{160,224},{192,128},{224,1... | collective-permute-start | bytes 1376264 | tf_op jit(solution)/shard_map/ppermute | solution.py:422
  93.2 6.8 %collective-permute-start.11 = (f32[2,13,16,128]{3,2,1,0:T(8,128)S(1)}, f32[2,13,16,128]{3,2,1,0:T(8,128)S(1)}, u32[]{:S(2)}, u32[]{:S(2)}) collective-permute-start(f32[2,13,16,128]{3,2,1,0:T(8,128)S(1)} %get-tuple-element.66), channel_id=1, source_target_pairs={{0,32},{32,0},{64,96},{96,64},{128,160},{160,128},{192,224},{224,1... | collective-permute-start | bytes 638984 | tf_op jit(solution)/shard_map/ppermute | solution.py:422
  93.2 8.1 %collective-permute-start.12 = (f32[2,13,16,128]{3,2,1,0:T(8,128)S(1)}, f32[2,13,16,128]{3,2,1,0:T(8,128)S(1)}, u32[]{:S(2)}, u32[]{:S(2)}) collective-permute-start(f32[2,13,16,128]{3,2,1,0:T(8,128)S(1)} %get-tuple-element.64), channel_id=1, source_target_pairs={{0,64},{32,96},{64,0},{96,32},{128,192},{160,224},{192,128},{224,1... | collective-permute-start | bytes 638984 | tf_op jit(solution)/shard_map/ppermute | solution.py:422
  93.4 9.2 %collective-permute-start.10 = (f32[2,14,16,128]{3,2,1,0:T(8,128)S(1)}, f32[2,14,16,128]{3,2,1,0:T(8,128)S(1)}, u32[]{:S(2)}, u32[]{:S(2)}) collective-permute-start(f32[2,14,16,128]{3,2,1,0:T(8,128)S(1)} %get-tuple-element.62), channel_id=1, source_target_pairs={{0,192},{32,224},{64,128},{96,160},{128,64},{160,96},{192,0},{224,... | collective-permute-start | bytes 688136 | tf_op jit(solution)/shard_map/ppermute | solution.py:422
  96.6 6.8 %collective-permute-start.8 = (f32[2,2,16,128]{3,2,1,0:T(8,128)S(1)}, f32[2,2,16,128]{3,2,1,0:T(8,128)S(1)}, u32[]{:S(2)}, u32[]{:S(2)}) collective-permute-start(f32[2,2,16,128]{3,2,1,0:T(8,128)S(1)} %get-tuple-element.74), channel_id=1, source_target_pairs={{0,192},{32,224},{64,128},{96,160},{128,64},{160,96},{192,0},{224,... | collective-permute-start | bytes 98312 | tf_op jit(solution)/shard_map/ppermute | solution.py:422
  100.7 7.5 %collective-permute-start.14 = (f32[1,13,16,128]{3,2,1,0:T(8,128)S(1)}, f32[1,13,16,128]{3,2,1,0:T(8,128)S(1)}, u32[]{:S(2)}, u32[]{:S(2)}) collective-permute-start(f32[1,13,16,128]{3,2,1,0:T(8,128)S(1)} %get-tuple-element.71), channel_id=1, source_target_pairs={{0,64},{32,96},{64,0},{96,32},{128,192},{160,224},{192,128},{224,1... | collective-permute-start | bytes 319496 | tf_op jit(solution)/shard_map/ppermute | solution.py:422
  102.0 6.2 %collective-permute-start.15 = (f32[1,13,16,128]{3,2,1,0:T(8,128)S(1)}, f32[1,13,16,128]{3,2,1,0:T(8,128)S(1)}, u32[]{:S(2)}, u32[]{:S(2)}) collective-permute-start(f32[1,13,16,128]{3,2,1,0:T(8,128)S(1)} %get-tuple-element.69), channel_id=1, source_target_pairs={{0,192},{32,224},{64,128},{96,160},{128,64},{160,96},{192,0},{224,... | collective-permute-start | bytes 319496 | tf_op jit(solution)/shard_map/ppermute | solution.py:422
  103.2 5.0 %collective-permute-start.13 = (f32[1,14,16,128]{3,2,1,0:T(8,128)S(1)}, f32[1,14,16,128]{3,2,1,0:T(8,128)S(1)}, u32[]{:S(2)}, u32[]{:S(2)}) collective-permute-start(f32[1,14,16,128]{3,2,1,0:T(8,128)S(1)} %get-tuple-element.67), channel_id=1, source_target_pairs={{0,32},{32,0},{64,96},{96,64},{128,160},{160,128},{192,224},{224,1... | collective-permute-start | bytes 344072 | tf_op jit(solution)/shard_map/ppermute | solution.py:422
  110.9 15.5 %all-to-all-start = ((f32[32,1,128]{2,1,0:T(1,128)}), f32[32,1,128]{2,1,0:T(1,128)S(1)}, u32[]{:S(2)}, u32[]{:S(2)}) async-start(f32[32,1,128]{2,1,0:T(1,128)} %get-tuple-element.44), calls=%async_computation | async-start | bytes 32768 | tf_op jit(solution)/shard_map/all_to_all | solution.py:520
  116.7 12.4 %collective-permute-start.19 = (f32[1,13,16,128]{3,2,1,0:T(8,128)}, f32[1,13,16,128]{3,2,1,0:T(8,128)S(1)}, u32[]{:S(2)}, u32[]{:S(2)}) collective-permute-start(f32[1,13,16,128]{3,2,1,0:T(8,128)} %get-tuple-element.45.refs_4_), channel_id=1, source_target_pairs={{0,64},{32,96},{64,0},{96,32},{128,192},{160,224},{192,128},{224,1... | collective-permute-start | bytes 319496 | tf_op jit(solution)/shard_map/ppermute | solution.py:422
  127.5 5.9 %collective-permute-start.16 = (f32[1,15,16,128]{3,2,1,0:T(8,128)S(1)}, f32[1,15,16,128]{3,2,1,0:T(8,128)S(1)}, u32[]{:S(2)}, u32[]{:S(2)}) collective-permute-start(f32[1,15,16,128]{3,2,1,0:T(8,128)S(1)} %pad_maximum_fusion.6.refs_0_), channel_id=1, source_target_pairs={{0,32},{32,0},{64,96},{96,64},{128,160},{160,128},{192,224},{224,1... | collective-permute-start | bytes 368648 | tf_op jit(solution)/shard_map/ppermute | solution.py:422
  128.2 6.2 %collective-permute-start.22 = (f32[1,13,16,128]{3,2,1,0:T(8,128)}, f32[1,13,16,128]{3,2,1,0:T(8,128)S(1)}, u32[]{:S(2)}, u32[]{:S(2)}) collective-permute-start(f32[1,13,16,128]{3,2,1,0:T(8,128)} %get-tuple-element.46.refs_8_), channel_id=1, source_target_pairs={{0,192},{32,224},{64,128},{96,160},{128,64},{160,96},{192,0},{224,... | collective-permute-start | bytes 319496 | tf_op jit(solution)/shard_map/ppermute | solution.py:422
  130.0 8.2 %collective-permute-start.20 = (f32[2,13,16,128]{3,2,1,0:T(8,128)S(1)}, f32[2,13,16,128]{3,2,1,0:T(8,128)S(1)}, u32[]{:S(2)}, u32[]{:S(2)}) collective-permute-start(f32[2,13,16,128]{3,2,1,0:T(8,128)S(1)} %pad_maximum_fusion.4), channel_id=1, source_target_pairs={{0,32},{32,0},{64,96},{96,64},{128,160},{160,128},{192,224},{224,1... | collective-permute-start | bytes 638984 | tf_op jit(solution)/shard_map/ppermute | solution.py:422
  134.3 6.7 %collective-permute-start.17 = (f32[2,15,16,128]{3,2,1,0:T(8,128)S(1)}, f32[2,15,16,128]{3,2,1,0:T(8,128)S(1)}, u32[]{:S(2)}, u32[]{:S(2)}) collective-permute-start(f32[2,15,16,128]{3,2,1,0:T(8,128)S(1)} %pad_maximum_fusion.3), channel_id=1, source_target_pairs={{0,192},{32,224},{64,128},{96,160},{128,64},{160,96},{192,0},{224,... | collective-permute-start | bytes 737288 | tf_op jit(solution)/shard_map/ppermute | solution.py:422
  135.3 8.6 %collective-permute-start.23 = (f32[2,13,16,128]{3,2,1,0:T(8,128)S(1)}, f32[2,13,16,128]{3,2,1,0:T(8,128)S(1)}, u32[]{:S(2)}, u32[]{:S(2)}) collective-permute-start(f32[2,13,16,128]{3,2,1,0:T(8,128)S(1)} %pad_maximum_fusion.5), channel_id=1, source_target_pairs={{0,64},{32,96},{64,0},{96,32},{128,192},{160,224},{192,128},{224,1... | collective-permute-start | bytes 638984 | tf_op jit(solution)/shard_map/ppermute | solution.py:422
  139.1 10.6 %collective-permute-start.21 = (f32[4,13,16,128]{3,2,1,0:T(8,128)S(1)}, f32[4,13,16,128]{3,2,1,0:T(8,128)S(1)}, u32[]{:S(2)}, u32[]{:S(2)}) collective-permute-start(f32[4,13,16,128]{3,2,1,0:T(8,128)S(1)} %pad_maximum_fusion.1), channel_id=1, source_target_pairs={{0,192},{32,224},{64,128},{96,160},{128,64},{160,96},{192,0},{224,... | collective-permute-start | bytes 1277960 | tf_op jit(solution)/shard_map/ppermute | solution.py:422
  141.0 11.9 %collective-permute-start.18 = (f32[4,15,16,128]{3,2,1,0:T(8,128)S(1)}, f32[4,15,16,128]{3,2,1,0:T(8,128)S(1)}, u32[]{:S(2)}, u32[]{:S(2)}) collective-permute-start(f32[4,15,16,128]{3,2,1,0:T(8,128)S(1)} %pad_maximum_fusion), channel_id=1, source_target_pairs={{0,64},{32,96},{64,0},{96,32},{128,192},{160,224},{192,128},{224,1... | collective-permute-start | bytes 1474568 | tf_op jit(solution)/shard_map/ppermute | solution.py:422
  144.0 8.9 %collective-permute-start.24 = (f32[4,13,16,128]{3,2,1,0:T(8,128)S(1)}, f32[4,13,16,128]{3,2,1,0:T(8,128)S(1)}, u32[]{:S(2)}, u32[]{:S(2)}) collective-permute-start(f32[4,13,16,128]{3,2,1,0:T(8,128)S(1)} %pad_maximum_fusion.2), channel_id=1, source_target_pairs={{0,32},{32,0},{64,96},{96,64},{128,160},{160,128},{192,224},{224,1... | collective-permute-start | bytes 1277960 | tf_op jit(solution)/shard_map/ppermute | solution.py:422
  (18 other events, 227.2 us)

commit v3 on v2

--- a/solution.py
+++ b/solution.py
@@ -67,37 +67,34 @@
     return jnp.where(bit2, mid[1], mid[0])
 
 
-def pack_kernel(where, labels, start, meas, side_a, side_b, ints, sem):
-    odd = lax.rem(where[0], 2)
-    high_f, high_m = NP - HF, NP - HM
-    copies = []
-    for at, (out, flip) in enumerate(((side_a, 1 - odd), (side_b, odd))):
-        copies.append(pltpu.make_async_copy(labels.at[pl.ds(flip * high_f, HF)], ints.at[at], sem.at[at, 8]))
-        for l in range(4):
-            copies.append(
-                pltpu.make_async_copy(
-                    start.at[l, pl.ds(flip * high_f, HF)], out.at[pl.ds(l * HF, HF)], sem.at[at, l]
-                )
+def pack_kernel(high, labels, start, meas, *rest):
+    *outs, ints, sem = rest
+    bulk, extra = outs[0], outs[-1]
+    at = 4 * HF if len(outs) == 1 else 0
+    flip = high[0]
+    copies = [pltpu.make_async_copy(labels.at[pl.ds(flip * (NP - HF), HF)], ints, sem.at[8])]
+    for l in range(4):
+        copies.append(
+            pltpu.make_async_copy(start.at[l, pl.ds(flip * (NP - HF), HF)], bulk.at[pl.ds(l * HF, HF)], sem.at[l])
+        )
+        copies.append(
+            pltpu.make_async_copy(
+                meas.at[l, pl.ds(flip * (NP - HM), HM)], extra.at[pl.ds(at + l * HM, HM)], sem.at[4 + l]
             )
-            copies.append(
-                pltpu.make_async_copy(
-                    meas.at[l, pl.ds(flip * high_m, HM)], out.at[pl.ds(4 * HF + l * HM, HM)], sem.at[at, 4 + l]
-                )
-            )
+        )
     for copy in copies:
         copy.start()
     for copy in copies:
         copy.wait()
-    for at, out in enumerate((side_a, side_b)):
-        out[4 * (HF + HM) : 4 * (HF + HM) + HF] = ints[at].astype(F32)
+    extra[at + 4 * HM : at + 4 * HM + HF] = ints[...].astype(F32)
 
 
 def solve_kernel(
-    where, spectra, absorb_t, half_t, labels, illum, start, meas, side_a, side_b,
+    where, spectra, absorb_t, half_t, labels, illum, start, meas, side_a, bulk_b, straight_b, turned_b,
     fluence, coef_a, coef_b, edge_a, edge_b, *rest,
 ):
     outs = rest[:6]
-    own, shared, lit, step, near, near2, fl, hd, wys, tmp, adj, ab, wes, wws, wzs, inv, mis, ms, sem = rest[6:]
+    own, shared, lit, step, near, near2, fl, hd, wys, tmp, adj, ab, wes, wws, wzs, inv, ms, sem = rest[6:]
     sends, keeps = outs[0::2], outs[1::2]
     gz = where[0]
     me = where[1]
@@ -108,26 +105,48 @@
         pltpu.make_async_copy(start, fl.at[:, pl.ds(HF, NP), whole], sem.at[1]),
         pltpu.make_async_copy(meas, ms.at[:, pl.ds(HM, NP)], sem.at[2]),
     ]
-    label_copies = []
-    side_copies = []
-    for at, (side, high) in enumerate(((side_a, 1 - odd), (side_b, odd))):
-        f_at = high * (HF + NP)
-        m_at = high * (HM + NP)
-        label_copies.append(
-            pltpu.make_async_copy(side.at[pl.ds(4 * (HF + HM), HF)], shared.at[pl.ds(high * HF, HF)], sem.at[3 + at])
+
+    def extras(side, at, high, number):
+        first = 3 + 5 * number
+        return [
+            pltpu.make_async_copy(
+                side.at[pl.ds(at + 4 * HM, HF)], shared.at[pl.ds(high * HF, HF)], sem.at[first]
+            )
+        ] + [
+            pltpu.make_async_copy(
+                side.at[pl.ds(at + l * HM, HM)], ms.at[l, pl.ds(high * (HM + NP), HM)], sem.at[first + 1 + l]
+            )
+            for l in range(4)
+        ]
+
+    extras_a = extras(side_a, 4 * HF, 1 - odd, 0)
+    extras_b = extras(straight_b, 0, odd, 1)
+    label_copies = [extras_a[0], extras_b[0]]
+    meas_copies = [copies[2]] + extras_a[1:] + extras_b[1:]
+    fluence_copies = [copies[1]] + [
+        pltpu.make_async_copy(
+            side.at[pl.ds(l * HF, HF)],
+            fl.at[l, pl.ds(high * (HF + NP), HF), whole],
+            sem.at[13 + 4 * number + l],
         )
-        for l in range(4):
-            side_copies.append(
-                pltpu.make_async_copy(
-                    side.at[pl.ds(l * HF, HF)], fl.at[l, pl.ds(f_at, HF), whole], sem.at[5 + 8 * at + l]
-                )
-            )
-            side_copies.append(
-                pltpu.make_async_copy(
-                    side.at[pl.ds(4 * HF + l * HM, HM)], ms.at[l, pl.ds(m_at, HM)], sem.at[9 + 8 * at + l]
-                )
-            )
-    for copy in label_copies + copies + side_copies:
+        for number, (side, high) in enumerate(((side_a, 1 - odd), (bulk_b, odd)))
+        for l in range(4)
+    ]
+    turned = (lax.rem(gz, 8) == 0) | (lax.rem(gz, 8) == 7)
+    copies[0].start()
+    extras_a[0].start()
+
+    @pl.when(turned)
+    def _():
+        for copy in extras(turned_b, 0, odd, 1):
+            copy.start()
+
+    @pl.when(jnp.logical_not(turned))
+    def _():
+        for copy in extras_b:
+            copy.start()
+
+    for copy in fluence_copies + [copies[2]] + extras_a[1:]:
         copy.start()
 
     lit[...] = illum[...].astype(F32)
@@ -172,7 +191,7 @@
     for copy in label_copies:
         copy.wait()
     lax.fori_loop(0, 2 * HF, optics_shared, 0)
-    for copy in copies[1:] + side_copies:
+    for copy in fluence_copies:
         copy.wait()
 
     @pl.when(gz == 0)
@@ -263,9 +282,11 @@
         fl[l, e, here] = f
         absorb = ab[l, e, flat]
         misfit = absorb * f - ms[l, e - (HF - HM), flat]
-        mis[l, e, flat] = misfit
+        ms[l, e - (HF - HM), flat] = misfit
         adj[l, e, here] = absorb * misfit * scale
 
+    for copy in meas_copies:
+        copy.wait()
     per_plane(2, EXT - 2, (tmp,), second)
     write = pltpu.make_async_copy(fl.at[:, pl.ds(HF, NP), whole], fluence, sem.at[0])
     write.start()
@@ -276,7 +297,7 @@
     def third(l, e, r):
         flat = pl.ds(r, CHUNK)
         here = pl.ds(PAD + r, CHUNK)
-        tmp[l, e, here] = (ab[l, e, flat] * mis[l, e, flat] + moved(adj, l, e, r)) * inv[l, e, flat]
+        tmp[l, e, here] = (ab[l, e, flat] * ms[l, e - (HF - HM), flat] + moved(adj, l, e, r)) * inv[l, e, flat]
 
     per_plane(HF, HF + NP, (adj,), third)
 
@@ -319,7 +340,7 @@
         flat = pl.ds(pl.multiple_of((me ^ code) * ROWS, 8), ROWS)
         for plane in range(NP):
             e = plane + HF
-            common = [fl[l, e, rows] * (mis[l, e, flat] - tmp[l, e, rows]) for l in range(4)]
+            common = [fl[l, e, rows] * (ms[l, e - (HF - HM), flat] - tmp[l, e, rows]) for l in range(4)]
             paired = [ab[l, e, flat] for l in range(4)]
             for field in range(5):
                 terms = common if field < 4 else paired
@@ -377,7 +398,7 @@
 
 
 def final_kernel(where, table, labels, *refs):
-    pieces, conc, scat = refs[:12], refs[12], refs[13]
+    pieces, (conc, scat, done, sem) = refs[:12], refs[12:]
     me = where[1]
     cells = 32 * NP * N * N
     extra = PARTS[0][1]
@@ -388,10 +409,10 @@
         total = total + pieces[3][i, extra]
     factor = -STEP / jnp.sqrt(total / cells + 1e-06)
     factors = [jnp.broadcast_to(factor[:, c : c + 1], (ROWS, N)) for c in range(5)]
-    for code in range(8):
-        at = pl.multiple_of((me ^ code) * ROWS, ROWS)
-        rows = pl.ds(at, ROWS)
-        for plane in range(NP):
+    copies = []
+    for plane in range(NP):
+        for code in range(8):
+            rows = pl.ds(pl.multiple_of((me ^ code) * ROWS, ROWS), ROWS)
             classes = labels[plane, rows]
             for field in range(5):
                 part, index = part_of(plane, field)
@@ -406,11 +427,13 @@
                 else:
                     grad = four[slot - 4, index]
                 coeff = pick(classes, [table[i, field] for i in range(8)])
-                value = coeff * jnp.exp(grad * factors[field])
-                if field < 4:
-                    conc[field, plane, rows] = value
-                else:
-                    scat[plane, rows] = value
+                done[field, plane, rows] = coeff * jnp.exp(grad * factors[field])
+        copies.append(pltpu.make_async_copy(done.at[0:4, plane], conc.at[:, plane], sem.at[plane, 0]))
+        copies.append(pltpu.make_async_copy(done.at[4, plane], scat.at[plane], sem.at[plane, 1]))
+        copies[-2].start()
+        copies[-1].start()
+    for copy in copies:
+        copy.wait()
 
 
 VMEM = pl.BlockSpec(memory_space=pltpu.VMEM)
@@ -424,28 +447,43 @@
 
 ON_CHIP = [(i, i ^ 1) for i in range(32)]
 OFF_CHIP = [(i, (i + 1 if i % 2 else i - 1) % 32) for i in range(32)]
+AROUND = [(i, i - 7 if i % 8 == 7 else i + 7 if i % 8 == 0 else j) for i, j in OFF_CHIP]
+ALONG = [(i, i + 8) for i in (0, 8, 16)] + [(i, i - 8) for i in (15, 23, 31)]
 
 
 def beside(a, b):
     return lax.ppermute(a, "gz", ON_CHIP), lax.ppermute(b, "gz", OFF_CHIP)
 
 
-def after(x, *others):
-    return lax.optimization_barrier((x, *others))[0]
-
-
 def shards(labels, label_table, spectra, illumination, fluence_start, measured):
     where = jnp.stack([lax.axis_index("gz"), lax.axis_index("wl")]).astype(jnp.int32)
-    packed = 4 * (HF + HM) + HF
-    side_a, side_b = pl.pallas_call(
-        pack_kernel,
-        out_shape=[jax.ShapeDtypeStruct((packed, N, N), F32)] * 2,
-        in_specs=[SMEM] + [ANY] * 3,
-        out_specs=[VMEM] * 2,
-        scratch_shapes=[pltpu.VMEM((2, HF, N, N), jnp.int32), pltpu.SemaphoreType.DMA((2, 9))],
-        name="pack",
-    )(where, labels, fluence_start, measured)
-    side_a, side_b = beside(side_a, side_b)
+    odd = lax.rem(where[:1], 2)
+    small = pltpu.CompilerParams(vmem_limit_bytes=12 * 2**20)
+
+    def in_hbm(x):
+        return pltpu.with_memory_space_constraint(x, pltpu.HBM)
+
+    def in_vmem(x):
+        return pltpu.with_memory_space_constraint(x, pltpu.VMEM)
+
+    def pack(high, *planes):
+        return pl.pallas_call(
+            pack_kernel,
+            out_shape=[jax.ShapeDtypeStruct((count, N, N), F32) for count in planes],
+            in_specs=[SMEM] + [ANY] * 3,
+            out_specs=[VMEM] * len(planes),
+            scratch_shapes=[pltpu.VMEM((HF, N, N), jnp.int32), pltpu.SemaphoreType.DMA((9,))],
+            compiler_params=small,
+            name="pack",
+        )(high, *map(in_hbm, (labels, fluence_start, measured)))
+
+    bulk_b, extra_b = pack(odd, 4 * HF, 4 * HM + HF)
+    (side_a,) = pack(1 - odd, 4 * HF + 4 * HM + HF)
+    bulk_b = lax.ppermute(bulk_b, "gz", OFF_CHIP)
+    straight_b = lax.ppermute(extra_b, "gz", AROUND)
+    side_a = lax.ppermute(side_a, "gz", ON_CHIP)
+    turned_b = lax.ppermute(straight_b, "gz", ALONG)
+    side_a, bulk_b, straight_b, turned_b = map(in_vmem, (side_a, bulk_b, straight_b, turned_b))
 
     absorb_t = spectra[:, 0, None] * label_table[None, :, 0]
     for c in range(1, 4):
@@ -460,7 +498,7 @@
         out_shape=[jax.ShapeDtypeStruct((4, NP, N, N), F32)]
         + [plane] * 4
         + [jax.ShapeDtypeStruct((4, size, ROWS, N), F32) for size in sizes for _ in range(2)],
-        in_specs=[SMEM] * 4 + [ANY] + [VMEM] + [ANY] * 4,
+        in_specs=[SMEM] * 4 + [ANY] + [VMEM] + [ANY] * 6,
         out_specs=[ANY] + [VMEM] * 10,
         scratch_shapes=[
             pltpu.VMEM((NP, N, N), jnp.int32),
@@ -470,11 +508,12 @@
         ]
         + [pltpu.VMEM((EXT, N, 2 * N), F32)] * 2
         + [field] * 5
-        + [pltpu.VMEM((4, EXT, N, N), F32)] * 6
+        + [pltpu.VMEM((4, EXT, N, N), F32)] * 5
         + [pltpu.VMEM((4, NP + 2 * HM, N, N), F32), pltpu.SemaphoreType.DMA((21,))],
-        compiler_params=pltpu.CompilerParams(vmem_limit_bytes=57 * 2**20),
+        compiler_params=pltpu.CompilerParams(vmem_limit_bytes=52 * 2**20),
         name="solve",
-    )(where, spectra, absorb_t, half_t, labels, illumination, fluence_start, measured, side_a, side_b)
+    )(where, spectra, absorb_t, half_t, labels, illumination,
+      *map(in_hbm, (fluence_start, measured)), side_a, bulk_b, straight_b, turned_b)
     sends = list(out[0::2])
     keeps = list(out[1::2])
 
@@ -493,6 +532,7 @@
         out_shape=[jax.ShapeDtypeStruct((4, 2, ROWS, N), F32)] * 2,
         in_specs=[SMEM] + [VMEM] * 4,
         out_specs=[VMEM] * 2,
+        compiler_params=small,
         name="edge",
     )(where, coef_a, coef_b, far_a, far_b)
     for phase in range(2):
@@ -508,6 +548,7 @@
         + [jax.ShapeDtypeStruct((32, 1, N), F32)],
         in_specs=[SMEM] + [VMEM] * 8,
         out_specs=[VMEM] * 4,
+        compiler_params=small,
         name="squares",
     )(where, late_keep, late_recv, *keeps, *recvs)
 
@@ -528,7 +569,8 @@
         final_kernel,
         out_shape=[jax.ShapeDtypeStruct((4, NP, N, N), F32), jax.ShapeDtypeStruct((NP, N, N), F32)],
         in_specs=[SMEM] * 2 + [VMEM] * 13,
-        out_specs=[VMEM] * 2,
+        out_specs=[ANY] * 2,
+        scratch_shapes=[pltpu.VMEM((5, NP, N, N), F32), pltpu.SemaphoreType.DMA((NP, 2))],
         compiler_params=pltpu.CompilerParams(vmem_limit_bytes=32 * 2**20),
         name="final",
     )(where, label_table, labels, *pieces)

time: 157 us -> 143 us (0.911)
  waiting for transfers between devices: 62.7 us -> 40 us
  starting transfers between devices: 40.3 us -> 61.6 us
  other arithmetic: 11.7 us -> 3.82 us
  Pallas kernels: 37.8 us -> 35.3 us
  local copies, waits for them, and re-layouts: 2.98 us -> 0.54 us
    ppermute x4 -> x2, waiting for transfers between devices: 29.8 us -> 0.32 us  [beside(): return (lax.ppermute(a, 'gz', ON_CHIP), lax.ppermute(b, 'gz', OFF_CHIP))]
    ppermute x0 -> x4, starting transfers between devices: none -> 17.4 us  [the longest x1 8.55 us: shards(): turned_b = lax.ppermute(straight_b, 'gz', ALONG)]
    ppermute x21, starting transfers between devices: 21.2 us -> 34.1 us  [swap(): return lax.ppermute(x, 'wl', [(i, i ^ code) for i in range(8)])]
    ppermute x4 -> x2, starting transfers between devices: 13.4 us -> 2.06 us  [beside(): return (lax.ppermute(a, 'gz', ON_CHIP), lax.ppermute(b, 'gz', OFF_CHIP))]
    ppermute x0 -> x4, waiting for transfers between devices: none -> 7.98 us  [the longest x1 6.05 us: shards(): bulk_b = lax.ppermute(bulk_b, 'gz', OFF_CHIP)]
    concatenate x6, other arithmetic: 3.73 us -> 0.16 us  [shards(): mine = have[0] if len(have) == 1 else jnp.concatenate(have)]
    unnamed x32 -> x14, local copies, waits for them, and re-layouts: 2.47 us -> 0.04 us
    all_to_all x1, waiting for transfers between devices: 8.87 us -> 6.53 us  [shards(): slab = jnp.sum(lax.all_to_all(sums, 'gz', 0, 0), axis=0)]
  transfers between devices with their start and end apart: 26 -> 28, of which waited for: 12 -> 14; matrix products, arithmetic and copies ran while one was open for 7% -> 3% of each run, Pallas kernels for 0% -> 2%
where the time goes in v3:
time: 143 us; the launch traced here: 142 us
  starting transfers between devices  61.6 us (43%)
  waiting for transfers between devices  40 us (28%)
  Pallas kernels  35.3 us (25%)
  other arithmetic  3.82 us (3%)
    ppermute x21, starting transfers between devices, swap(): return lax.ppermute(x, 'wl', [(i, i ^ code) for i in range(8)])  34.1 us
    pallas_call x1, Pallas kernels, shards(): pl.pallas_call(solve_kernel, out_shape=[jax.ShapeDtypeStruct((4, NP, N, N...  26.8 us
    ppermute x21, waiting for transfers between devices, swap(): return lax.ppermute(x, 'wl', [(i, i ^ code) for i in range(8)])  25.2 us
    ppermute x1, starting transfers between devices, shards(): turned_b = lax.ppermute(straight_b, 'gz', ALONG)  8.55 us
    all_to_all x1, starting transfers between devices, shards(): slab = jnp.sum(lax.all_to_all(sums, 'gz', 0, 0), axis=0)  8.05 us
    all_to_all x1, waiting for transfers between devices, shards(): slab = jnp.sum(lax.all_to_all(sums, 'gz', 0, 0), axis=0)  6.53 us
    ppermute x1, waiting for transfers between devices, shards(): bulk_b = lax.ppermute(bulk_b, 'gz', OFF_CHIP)  6.05 us
    ppermute x1, starting transfers between devices, shards(): bulk_b = lax.ppermute(bulk_b, 'gz', OFF_CHIP)  5.84 us
  transfers between devices with their start and end apart: 28, of which 14 were waited for; matrix products, arithmetic and copies ran while one was open for 3% of the time, Pallas kernels for 2%

profile of v3, /device:TPU:8, one launch (start us, length us, event | category | flops | bytes accessed | tf_op | source)
XLA Modules:
  0.0 142.3 jit_solution(12486618596984412085)
XLA Ops:
  2.2 2.5 %pack.3 = (f32[12,128,128]{2,1,0:T(8,128)}, f32[7,128,128]{2,1,0:T(8,128)}) custom-call(s32[1]{0:T(128)S(6)} %rem.18.high, s32[8,128,128]{2,1,0:T(8,128)} %labels.7, f32[4,8,128,128]{3,2,1,0:T(8,128)} %start.5, f32[4,8,128,128]{3,2,1,0:T(8,128)} %meas.5), custom_call_target="tpu_custom_call" | custom-call | tf_op jit(solution)/shard_map/pack/pallas_call | solution.py:470
  4.7 2.9 %collective-permute-start.2 = (f32[7,128,128]{2,1,0:T(8,128)}, f32[7,128,128]{2,1,0:T(8,128)}, u32[]{:S(2)}, u32[]{:S(2)}) collective-permute-start(f32[7,128,128]{2,1,0:T(8,128)} %get-tuple-element.27), channel_id=1, source_target_pairs={{0,7},{1,2},{2,1},{3,4},{4,3},{5,6},{6,5},{7,0},{8,15},{9,10},{10,... | collective-permute-start | bytes 1376264 | tf_op jit(solution)/shard_map/ppermute | solution.py:483
  7.6 5.8 %collective-permute-start.1 = (f32[12,128,128]{2,1,0:T(8,128)}, f32[12,128,128]{2,1,0:T(8,128)S(1)}, u32[]{:S(2)}, u32[]{:S(2)}) collective-permute-start(f32[12,128,128]{2,1,0:T(8,128)} %get-tuple-element.26), channel_id=1, source_target_pairs={{0,31},{1,2},{2,1},{3,4},{4,3},{5,6},{6,5},{7,8},{8,7},{9,10},{10,... | collective-permute-start | bytes 2359304 | tf_op jit(solution)/shard_map/ppermute | solution.py:482
  13.5 1.9 %collective-permute-done.2.straight_b = f32[7,128,128]{2,1,0:T(8,128)} collective-permute-done((f32[7,128,128]{2,1,0:T(8,128)}, f32[7,128,128]{2,1,0:T(8,128)}, u32[]{:S(2)}, u32[]{:S(2)}) %collective-permute-start.2) | collective-permute-done | bytes 458784 | tf_op jit(solution)/shard_map/ppermute | solution.py:483
  15.4 8.5 %collective-permute-start.3 = (f32[7,128,128]{2,1,0:T(8,128)}, f32[7,128,128]{2,1,0:T(8,128)S(1)}, u32[]{:S(2)}, u32[]{:S(2)}) collective-permute-start(f32[7,128,128]{2,1,0:T(8,128)} %collective-permute-done.2.straight_b), channel_id=1, source_target_pairs={{0,8},{8,16},{16,24},{15,7},{23,15},{31,23},{32,40},{40,48},{48,56... | collective-permute-start | bytes 1376264 | tf_op jit(solution)/shard_map/ppermute | solution.py:485
  25.7 6.0 %collective-permute-done.1.bulk_b = f32[12,128,128]{2,1,0:T(8,128)S(1)} collective-permute-done((f32[12,128,128]{2,1,0:T(8,128)}, f32[12,128,128]{2,1,0:T(8,128)S(1)}, u32[]{:S(2)}, u32[]{:S(2)}) %collective-permute-start.1) | collective-permute-done | bytes 786464 | tf_op jit(solution)/shard_map/ppermute | solution.py:482
  31.8 26.8 %solve.1 = (f32[4,8,128,128]{3,2,1,0:T(8,128)}, f32[4,128,128]{2,1,0:T(8,128)}, f32[4,128,128]{2,1,0:T(8,128)}, f32[4,128,128]{2,1,0:T(8,128)}, f32[4,128,128]{2...) custom-call(s32[2]{0:T(128)} %pad_add_fusion.where, ...), custom_call_target="tpu_custom_call" | custom-call | tf_op jit(solution)/shard_map/solve/pallas_call | solution.py:496
  60.3 4.2 %collective-permute-start.8 = (f32[4,13,16,128]{3,2,1,0:T(8,128)}, f32[4,13,16,128]{3,2,1,0:T(8,128)S(1)}, u32[]{:S(2)}, u32[]{:S(2)}) collective-permute-start(f32[4,13,16,128]{3,2,1,0:T(8,128)} %get-tuple-element.38), channel_id=1, source_target_pairs={{0,32},{32,0},{64,96},{96,64},{128,160},{160,128},{192,224},{224,1... | collective-permute-start | bytes 1277960 | tf_op jit(solution)/shard_map/ppermute | solution.py:445
  64.5 2.1 %collective-permute-start.5 = (f32[4,128,128]{2,1,0:T(8,128)}, f32[4,128,128]{2,1,0:T(8,128)S(1)}, u32[]{:S(2)}, u32[]{:S(2)}) collective-permute-start(f32[4,128,128]{2,1,0:T(8,128)} %get-tuple-element.32), channel_id=1, source_target_pairs={{0,31},{1,2},{2,1},{3,4},{4,3},{5,6},{6,5},{7,8},{8,7},{9,10},{10,... | collective-permute-start | bytes 786440 | tf_op jit(solution)/shard_map/ppermute | solution.py:455
  66.6 1.9 %collective-permute-start.6 = (f32[4,14,16,128]{3,2,1,0:T(8,128)}, f32[4,14,16,128]{3,2,1,0:T(8,128)S(1)}, u32[]{:S(2)}, u32[]{:S(2)}) collective-permute-start(f32[4,14,16,128]{3,2,1,0:T(8,128)} %get-tuple-element.34), channel_id=1, source_target_pairs={{0,64},{32,96},{64,0},{96,32},{128,192},{160,224},{192,128},{224,1... | collective-permute-start | bytes 1376264 | tf_op jit(solution)/shard_map/ppermute | solution.py:445
  71.9 5.9 %collective-permute-done.6 = f32[4,14,16,128]{3,2,1,0:T(8,128)S(1)} collective-permute-done((f32[4,14,16,128]{3,2,1,0:T(8,128)}, f32[4,14,16,128]{3,2,1,0:T(8,128)S(1)}, u32[]{:S(2)}, u32[]{:S(2)}) %collective-permute-start.6) | collective-permute-done | bytes 458784 | tf_op jit(solution)/shard_map/ppermute | solution.py:445
  78.8 2.0 %collective-permute-start.9 = (f32[4,2,16,128]{3,2,1,0:T(8,128)S(1)}, f32[4,2,16,128]{3,2,1,0:T(8,128)S(1)}, u32[]{:S(2)}, u32[]{:S(2)}) collective-permute-start(f32[4,2,16,128]{3,2,1,0:T(8,128)S(1)} %get-tuple-element.42), channel_id=1, source_target_pairs={{0,64},{32,96},{64,0},{96,32},{128,192},{160,224},{192,128},{224,1... | collective-permute-start | bytes 196616 | tf_op jit(solution)/shard_map/ppermute | solution.py:445
  83.7 3.1 %collective-permute-done.13 = f32[2,13,16,128]{3,2,1,0:T(8,128)S(1)} collective-permute-done((f32[2,13,16,128]{3,2,1,0:T(8,128)S(1)}, f32[2,13,16,128]{3,2,1,0:T(8,128)S(1)}, u32[]{:S(2)}, u32[]{:S(2)}) %collective-permute-start.13) | collective-permute-done | bytes 213024 | tf_op jit(solution)/shard_map/ppermute | solution.py:445
  90.6 3.3 %collective-permute-done.11.late_recv = f32[1,2,16,128]{3,2,1,0:T(8,128)S(1)} collective-permute-done((f32[1,2,16,128]{3,2,1,0:T(8,128)S(1)}, f32[1,2,16,128]{3,2,1,0:T(8,128)S(1)}, u32[]{:S(2)}, u32[]{:S(2)}) %collective-permute-start.11) | collective-permute-done | bytes 16416 | tf_op jit(solution)/shard_map/ppermute | solution.py:445
  95.2 8.0 %all-to-all-start = ((f32[32,1,128]{2,1,0:T(1,128)}), f32[32,1,128]{2,1,0:T(1,128)S(1)}, u32[]{:S(2)}, u32[]{:S(2)}) async-start(f32[32,1,128]{2,1,0:T(1,128)} %get-tuple-element.44), calls=%async_computation | async-start | bytes 32768 | tf_op jit(solution)/shard_map/all_to_all | solution.py:561
  103.3 3.2 %collective-permute-start.21 = (f32[1,13,16,128]{3,2,1,0:T(8,128)S(1)}, f32[1,13,16,128]{3,2,1,0:T(8,128)S(1)}, u32[]{:S(2)}, u32[]{:S(2)}) collective-permute-start(f32[1,13,16,128]{3,2,1,0:T(8,128)S(1)} %get-tuple-element.45.refs_4_), channel_id=1, source_target_pairs={{0,64},{32,96},{64,0},{96,32},{128,192},{160,224},{192,128},{224,1... | collective-permute-start | bytes 319496 | tf_op jit(solution)/shard_map/ppermute | solution.py:445
  106.5 6.5 %all-to-all-done = f32[32,1,128]{2,1,0:T(1,128)S(1)} async-done(((f32[32,1,128]{2,1,0:T(1,128)}), f32[32,1,128]{2,1,0:T(1,128)S(1)}, u32[]{:S(2)}, u32[]{:S(2)}) %all-to-all-start) | async-done | bytes 16416 | tf_op jit(solution)/shard_map/all_to_all | solution.py:561
  114.3 2.0 %collective-permute-start.24 = (f32[1,13,16,128]{3,2,1,0:T(8,128)S(1)}, f32[1,13,16,128]{3,2,1,0:T(8,128)S(1)}, u32[]{:S(2)}, u32[]{:S(2)}) collective-permute-start(f32[1,13,16,128]{3,2,1,0:T(8,128)S(1)} %get-tuple-element.46.refs_8_), channel_id=1, source_target_pairs={{0,192},{32,224},{64,128},{96,160},{128,64},{160,96},{192,0},{224,... | collective-permute-start | bytes 319496 | tf_op jit(solution)/shard_map/ppermute | solution.py:445
  118.3 3.2 %collective-permute-start.19 = (f32[2,15,16,128]{3,2,1,0:T(8,128)S(1)}, f32[2,15,16,128]{3,2,1,0:T(8,128)S(1)}, u32[]{:S(2)}, u32[]{:S(2)}) collective-permute-start(f32[2,15,16,128]{3,2,1,0:T(8,128)S(1)} %pad_maximum_fusion.3), channel_id=1, source_target_pairs={{0,192},{32,224},{64,128},{96,160},{128,64},{160,96},{192,0},{224,... | collective-permute-start | bytes 737288 | tf_op jit(solution)/shard_map/ppermute | solution.py:445
  123.4 2.0 %collective-permute-start.23 = (f32[4,13,16,128]{3,2,1,0:T(8,128)S(1)}, f32[4,13,16,128]{3,2,1,0:T(8,128)S(1)}, u32[]{:S(2)}, u32[]{:S(2)}) collective-permute-start(f32[4,13,16,128]{3,2,1,0:T(8,128)S(1)} %pad_maximum_fusion.1), channel_id=1, source_target_pairs={{0,192},{32,224},{64,128},{96,160},{128,64},{160,96},{192,0},{224,... | collective-permute-start | bytes 1277960 | tf_op jit(solution)/shard_map/ppermute | solution.py:445
  126.5 4.7 %collective-permute-start.20 = (f32[4,15,16,128]{3,2,1,0:T(8,128)S(1)}, f32[4,15,16,128]{3,2,1,0:T(8,128)S(1)}, u32[]{:S(2)}, u32[]{:S(2)}) collective-permute-start(f32[4,15,16,128]{3,2,1,0:T(8,128)S(1)} %pad_maximum_fusion), channel_id=1, source_target_pairs={{0,64},{32,96},{64,0},{96,32},{128,192},{160,224},{192,128},{224,1... | collective-permute-start | bytes 1474568 | tf_op jit(solution)/shard_map/ppermute | solution.py:445
  132.4 2.4 %collective-permute-done.23.refs_7_ = f32[4,13,16,128]{3,2,1,0:T(8,128)S(1)} collective-permute-done((f32[4,13,16,128]{3,2,1,0:T(8,128)S(1)}, f32[4,13,16,128]{3,2,1,0:T(8,128)S(1)}, u32[]{:S(2)}, u32[]{:S(2)}) %collective-permute-start.23) | collective-permute-done | bytes 426016 | tf_op jit(solution)/shard_map/ppermute | solution.py:445
  134.8 4.6 %collective-permute-done.26.refs_11_ = f32[4,13,16,128]{3,2,1,0:T(8,128)S(1)} collective-permute-done((f32[4,13,16,128]{3,2,1,0:T(8,128)S(1)}, f32[4,13,16,128]{3,2,1,0:T(8,128)S(1)}, u32[]{:S(2)}, u32[]{:S(2)}) %collective-permute-start.26) | collective-permute-done | bytes 426016 | tf_op jit(solution)/shard_map/ppermute | solution.py:445
  139.4 2.7 %final.1 = (f32[4,8,128,128]{3,2,1,0:T(8,128)}, f32[8,128,128]{2,1,0:T(8,128)}) custom-call(s32[2]{0:T(128)S(1)} %copy-done.4, f32[8,5]{1,0:T(8,128)S(1)} %copy-done.3, s32[8,128,128]{2,1,0:T(8,128)S(1)} %copy-done, f32[1,15,16,128]{3,2,1,0:T(8,128)S(1)} %pad_maximum_fusion.6.refs_0_, f32[1,15,16,128]{3,2,1,0:T(8,128)S(1)} %collective-permute-done.18.refs_1_, ...), custom_call_target="tpu_custom_call" | custom-call | tf_op jit(solution)/shard_map/final/pallas_call | solution.py:568
  (73 shorter events, 24.9 us)
Async XLA Ops:
  2.1 29.6 %collective-permute-start = (f32[19,128,128]{2,1,0:T(8,128)S(1)}, f32[19,128,128]{2,1,0:T(8,128)S(1)}, u32[]{:S(2)}, u32[]{:S(2)}) collective-permute-start(f32[19,128,128]{2,1,0:T(8,128)S(1)} %pack.2), channel_id=1, source_target_pairs={{0,1},{1,0},{2,3},{3,2},{4,5},{5,4},{6,7},{7,6},{8,9},{9,8},{10,11... | collective-permute-start | bytes 3735560 | tf_op jit(solution)/shard_map/ppermute | solution.py:484
  4.7 10.7 %collective-permute-start.2 = (f32[7,128,128]{2,1,0:T(8,128)}, f32[7,128,128]{2,1,0:T(8,128)}, u32[]{:S(2)}, u32[]{:S(2)}) collective-permute-start(f32[7,128,128]{2,1,0:T(8,128)} %get-tuple-element.27), channel_id=1, source_target_pairs={{0,7},{1,2},{2,1},{3,4},{4,3},{5,6},{6,5},{7,0},{8,15},{9,10},{10,... | collective-permute-start | bytes 1376264 | tf_op jit(solution)/shard_map/ppermute | solution.py:483
  7.6 24.1 %collective-permute-start.1 = (f32[12,128,128]{2,1,0:T(8,128)}, f32[12,128,128]{2,1,0:T(8,128)S(1)}, u32[]{:S(2)}, u32[]{:S(2)}) collective-permute-start(f32[12,128,128]{2,1,0:T(8,128)} %get-tuple-element.26), channel_id=1, source_target_pairs={{0,31},{1,2},{2,1},{3,4},{4,3},{5,6},{6,5},{7,8},{8,7},{9,10},{10,... | collective-permute-start | bytes 2359304 | tf_op jit(solution)/shard_map/ppermute | solution.py:482
  15.4 16.4 %collective-permute-start.3 = (f32[7,128,128]{2,1,0:T(8,128)}, f32[7,128,128]{2,1,0:T(8,128)S(1)}, u32[]{:S(2)}, u32[]{:S(2)}) collective-permute-start(f32[7,128,128]{2,1,0:T(8,128)} %collective-permute-done.2.straight_b), channel_id=1, source_target_pairs={{0,8},{8,16},{16,24},{15,7},{23,15},{31,23},{32,40},{40,48},{48,56... | collective-permute-start | bytes 1376264 | tf_op jit(solution)/shard_map/ppermute | solution.py:485
  58.6 9.9 %collective-permute-start.7 = (f32[4,13,16,128]{3,2,1,0:T(8,128)}, f32[4,13,16,128]{3,2,1,0:T(8,128)S(1)}, u32[]{:S(2)}, u32[]{:S(2)}) collective-permute-start(f32[4,13,16,128]{3,2,1,0:T(8,128)} %get-tuple-element.36), channel_id=1, source_target_pairs={{0,192},{32,224},{64,128},{96,160},{128,64},{160,96},{192,0},{224,... | collective-permute-start | bytes 1277960 | tf_op jit(solution)/shard_map/ppermute | solution.py:445
  60.3 10.6 %collective-permute-start.8 = (f32[4,13,16,128]{3,2,1,0:T(8,128)}, f32[4,13,16,128]{3,2,1,0:T(8,128)S(1)}, u32[]{:S(2)}, u32[]{:S(2)}) collective-permute-start(f32[4,13,16,128]{3,2,1,0:T(8,128)} %get-tuple-element.38), channel_id=1, source_target_pairs={{0,32},{32,0},{64,96},{96,64},{128,160},{160,128},{192,224},{224,1... | collective-permute-start | bytes 1277960 | tf_op jit(solution)/shard_map/ppermute | solution.py:445
  64.5 13.4 %collective-permute-start.4 = (f32[4,128,128]{2,1,0:T(8,128)}, f32[4,128,128]{2,1,0:T(8,128)S(1)}, u32[]{:S(2)}, u32[]{:S(2)}) collective-permute-start(f32[4,128,128]{2,1,0:T(8,128)} %get-tuple-element.31), channel_id=1, source_target_pairs={{0,1},{1,0},{2,3},{3,2},{4,5},{5,4},{6,7},{7,6},{8,9},{9,8},{10,11... | collective-permute-start | bytes 786440 | tf_op jit(solution)/shard_map/ppermute | solution.py:455
  64.5 13.7 %collective-permute-start.5 = (f32[4,128,128]{2,1,0:T(8,128)}, f32[4,128,128]{2,1,0:T(8,128)S(1)}, u32[]{:S(2)}, u32[]{:S(2)}) collective-permute-start(f32[4,128,128]{2,1,0:T(8,128)} %get-tuple-element.32), channel_id=1, source_target_pairs={{0,31},{1,2},{2,1},{3,4},{4,3},{5,6},{6,5},{7,8},{8,7},{9,10},{10,... | collective-permute-start | bytes 786440 | tf_op jit(solution)/shard_map/ppermute | solution.py:455
  66.6 11.2 %collective-permute-start.6 = (f32[4,14,16,128]{3,2,1,0:T(8,128)}, f32[4,14,16,128]{3,2,1,0:T(8,128)S(1)}, u32[]{:S(2)}, u32[]{:S(2)}) collective-permute-start(f32[4,14,16,128]{3,2,1,0:T(8,128)} %get-tuple-element.34), channel_id=1, source_target_pairs={{0,64},{32,96},{64,0},{96,32},{128,192},{160,224},{192,128},{224,1... | collective-permute-start | bytes 1376264 | tf_op jit(solution)/shard_map/ppermute | solution.py:445
  80.8 6.1 %collective-permute-start.13 = (f32[2,13,16,128]{3,2,1,0:T(8,128)S(1)}, f32[2,13,16,128]{3,2,1,0:T(8,128)S(1)}, u32[]{:S(2)}, u32[]{:S(2)}) collective-permute-start(f32[2,13,16,128]{3,2,1,0:T(8,128)S(1)} %get-tuple-element.66), channel_id=1, source_target_pairs={{0,32},{32,0},{64,96},{96,64},{128,160},{160,128},{192,224},{224,1... | collective-permute-start | bytes 638984 | tf_op jit(solution)/shard_map/ppermute | solution.py:445
  81.1 7.0 %collective-permute-start.14 = (f32[2,13,16,128]{3,2,1,0:T(8,128)S(1)}, f32[2,13,16,128]{3,2,1,0:T(8,128)S(1)}, u32[]{:S(2)}, u32[]{:S(2)}) collective-permute-start(f32[2,13,16,128]{3,2,1,0:T(8,128)S(1)} %get-tuple-element.64), channel_id=1, source_target_pairs={{0,64},{32,96},{64,0},{96,32},{128,192},{160,224},{192,128},{224,1... | collective-permute-start | bytes 638984 | tf_op jit(solution)/shard_map/ppermute | solution.py:445
  81.2 7.2 %collective-permute-start.12 = (f32[2,14,16,128]{3,2,1,0:T(8,128)S(1)}, f32[2,14,16,128]{3,2,1,0:T(8,128)S(1)}, u32[]{:S(2)}, u32[]{:S(2)}) collective-permute-start(f32[2,14,16,128]{3,2,1,0:T(8,128)S(1)} %get-tuple-element.62), channel_id=1, source_target_pairs={{0,192},{32,224},{64,128},{96,160},{128,64},{160,96},{192,0},{224,... | collective-permute-start | bytes 688136 | tf_op jit(solution)/shard_map/ppermute | solution.py:445
  83.2 6.9 %collective-permute-start.10 = (f32[2,2,16,128]{3,2,1,0:T(8,128)S(1)}, f32[2,2,16,128]{3,2,1,0:T(8,128)S(1)}, u32[]{:S(2)}, u32[]{:S(2)}) collective-permute-start(f32[2,2,16,128]{3,2,1,0:T(8,128)S(1)} %get-tuple-element.74), channel_id=1, source_target_pairs={{0,192},{32,224},{64,128},{96,160},{128,64},{160,96},{192,0},{224,... | collective-permute-start | bytes 98312 | tf_op jit(solution)/shard_map/ppermute | solution.py:445
  86.9 7.0 %collective-permute-start.16 = (f32[1,13,16,128]{3,2,1,0:T(8,128)S(1)}, f32[1,13,16,128]{3,2,1,0:T(8,128)S(1)}, u32[]{:S(2)}, u32[]{:S(2)}) collective-permute-start(f32[1,13,16,128]{3,2,1,0:T(8,128)S(1)} %get-tuple-element.71), channel_id=1, source_target_pairs={{0,64},{32,96},{64,0},{96,32},{128,192},{160,224},{192,128},{224,1... | collective-permute-start | bytes 319496 | tf_op jit(solution)/shard_map/ppermute | solution.py:445
  88.1 5.9 %collective-permute-start.17 = (f32[1,13,16,128]{3,2,1,0:T(8,128)S(1)}, f32[1,13,16,128]{3,2,1,0:T(8,128)S(1)}, u32[]{:S(2)}, u32[]{:S(2)}) collective-permute-start(f32[1,13,16,128]{3,2,1,0:T(8,128)S(1)} %get-tuple-element.69), channel_id=1, source_target_pairs={{0,192},{32,224},{64,128},{96,160},{128,64},{160,96},{192,0},{224,... | collective-permute-start | bytes 319496 | tf_op jit(solution)/shard_map/ppermute | solution.py:445
  95.2 17.8 %all-to-all-start = ((f32[32,1,128]{2,1,0:T(1,128)}), f32[32,1,128]{2,1,0:T(1,128)S(1)}, u32[]{:S(2)}, u32[]{:S(2)}) async-start(f32[32,1,128]{2,1,0:T(1,128)} %get-tuple-element.44), calls=%async_computation | async-start | bytes 32768 | tf_op jit(solution)/shard_map/all_to_all | solution.py:561
  103.3 13.0 %collective-permute-start.21 = (f32[1,13,16,128]{3,2,1,0:T(8,128)S(1)}, f32[1,13,16,128]{3,2,1,0:T(8,128)S(1)}, u32[]{:S(2)}, u32[]{:S(2)}) collective-permute-start(f32[1,13,16,128]{3,2,1,0:T(8,128)S(1)} %get-tuple-element.45.refs_4_), channel_id=1, source_target_pairs={{0,64},{32,96},{64,0},{96,32},{128,192},{160,224},{192,128},{224,1... | collective-permute-start | bytes 319496 | tf_op jit(solution)/shard_map/ppermute | solution.py:445
  114.3 7.2 %collective-permute-start.24 = (f32[1,13,16,128]{3,2,1,0:T(8,128)S(1)}, f32[1,13,16,128]{3,2,1,0:T(8,128)S(1)}, u32[]{:S(2)}, u32[]{:S(2)}) collective-permute-start(f32[1,13,16,128]{3,2,1,0:T(8,128)S(1)} %get-tuple-element.46.refs_8_), channel_id=1, source_target_pairs={{0,192},{32,224},{64,128},{96,160},{128,64},{160,96},{192,0},{224,... | collective-permute-start | bytes 319496 | tf_op jit(solution)/shard_map/ppermute | solution.py:445
  116.3 7.1 %collective-permute-start.22 = (f32[2,13,16,128]{3,2,1,0:T(8,128)S(1)}, f32[2,13,16,128]{3,2,1,0:T(8,128)S(1)}, u32[]{:S(2)}, u32[]{:S(2)}) collective-permute-start(f32[2,13,16,128]{3,2,1,0:T(8,128)S(1)} %pad_maximum_fusion.4), channel_id=1, source_target_pairs={{0,32},{32,0},{64,96},{96,64},{128,160},{160,128},{192,224},{224,1... | collective-permute-start | bytes 638984 | tf_op jit(solution)/shard_map/ppermute | solution.py:445
  118.3 8.1 %collective-permute-start.19 = (f32[2,15,16,128]{3,2,1,0:T(8,128)S(1)}, f32[2,15,16,128]{3,2,1,0:T(8,128)S(1)}, u32[]{:S(2)}, u32[]{:S(2)}) collective-permute-start(f32[2,15,16,128]{3,2,1,0:T(8,128)S(1)} %pad_maximum_fusion.3), channel_id=1, source_target_pairs={{0,192},{32,224},{64,128},{96,160},{128,64},{160,96},{192,0},{224,... | collective-permute-start | bytes 737288 | tf_op jit(solution)/shard_map/ppermute | solution.py:445
  121.5 9.7 %collective-permute-start.25 = (f32[2,13,16,128]{3,2,1,0:T(8,128)S(1)}, f32[2,13,16,128]{3,2,1,0:T(8,128)S(1)}, u32[]{:S(2)}, u32[]{:S(2)}) collective-permute-start(f32[2,13,16,128]{3,2,1,0:T(8,128)S(1)} %pad_maximum_fusion.5), channel_id=1, source_target_pairs={{0,64},{32,96},{64,0},{96,32},{128,192},{160,224},{192,128},{224,1... | collective-permute-start | bytes 638984 | tf_op jit(solution)/shard_map/ppermute | solution.py:445
  123.4 11.4 %collective-permute-start.23 = (f32[4,13,16,128]{3,2,1,0:T(8,128)S(1)}, f32[4,13,16,128]{3,2,1,0:T(8,128)S(1)}, u32[]{:S(2)}, u32[]{:S(2)}) collective-permute-start(f32[4,13,16,128]{3,2,1,0:T(8,128)S(1)} %pad_maximum_fusion.1), channel_id=1, source_target_pairs={{0,192},{32,224},{64,128},{96,160},{128,64},{160,96},{192,0},{224,... | collective-permute-start | bytes 1277960 | tf_op jit(solution)/shard_map/ppermute | solution.py:445
  126.5 12.9 %collective-permute-start.20 = (f32[4,15,16,128]{3,2,1,0:T(8,128)S(1)}, f32[4,15,16,128]{3,2,1,0:T(8,128)S(1)}, u32[]{:S(2)}, u32[]{:S(2)}) collective-permute-start(f32[4,15,16,128]{3,2,1,0:T(8,128)S(1)} %pad_maximum_fusion), channel_id=1, source_target_pairs={{0,64},{32,96},{64,0},{96,32},{128,192},{160,224},{192,128},{224,1... | collective-permute-start | bytes 1474568 | tf_op jit(solution)/shard_map/ppermute | solution.py:445
  131.2 8.2 %collective-permute-start.26 = (f32[4,13,16,128]{3,2,1,0:T(8,128)S(1)}, f32[4,13,16,128]{3,2,1,0:T(8,128)S(1)}, u32[]{:S(2)}, u32[]{:S(2)}) collective-permute-start(f32[4,13,16,128]{3,2,1,0:T(8,128)S(1)} %pad_maximum_fusion.2), channel_id=1, source_target_pairs={{0,32},{32,0},{64,96},{96,64},{128,160},{160,128},{192,224},{224,1... | collective-permute-start | bytes 1277960 | tf_op jit(solution)/shard_map/ppermute | solution.py:445
  (11 other events, 168.5 us)

commit v4 on v3

--- a/solution.py
+++ b/solution.py
@@ -89,68 +89,9 @@
     extra[at + 4 * HM : at + 4 * HM + HF] = ints[...].astype(F32)
 
 
-def solve_kernel(
-    where, spectra, absorb_t, half_t, labels, illum, start, meas, side_a, bulk_b, straight_b, turned_b,
-    fluence, coef_a, coef_b, edge_a, edge_b, *rest,
-):
-    outs = rest[:6]
-    own, shared, lit, step, near, near2, fl, hd, wys, tmp, adj, ab, wes, wws, wzs, inv, ms, sem = rest[6:]
-    sends, keeps = outs[0::2], outs[1::2]
+def stages(where, spectra, absorb_t, half_t, lit, step, near, near2, state):
+    fl, hd, wys, tmp, adj, ab, wes, wws, wzs, inv, ms = state
     gz = where[0]
-    me = where[1]
-    odd = lax.rem(gz, 2)
-    whole = pl.ds(PAD, N)
-    copies = [
-        pltpu.make_async_copy(labels, own, sem.at[0]),
-        pltpu.make_async_copy(start, fl.at[:, pl.ds(HF, NP), whole], sem.at[1]),
-        pltpu.make_async_copy(meas, ms.at[:, pl.ds(HM, NP)], sem.at[2]),
-    ]
-
-    def extras(side, at, high, number):
-        first = 3 + 5 * number
-        return [
-            pltpu.make_async_copy(
-                side.at[pl.ds(at + 4 * HM, HF)], shared.at[pl.ds(high * HF, HF)], sem.at[first]
-            )
-        ] + [
-            pltpu.make_async_copy(
-                side.at[pl.ds(at + l * HM, HM)], ms.at[l, pl.ds(high * (HM + NP), HM)], sem.at[first + 1 + l]
-            )
-            for l in range(4)
-        ]
-
-    extras_a = extras(side_a, 4 * HF, 1 - odd, 0)
-    extras_b = extras(straight_b, 0, odd, 1)
-    label_copies = [extras_a[0], extras_b[0]]
-    meas_copies = [copies[2]] + extras_a[1:] + extras_b[1:]
-    fluence_copies = [copies[1]] + [
-        pltpu.make_async_copy(
-            side.at[pl.ds(l * HF, HF)],
-            fl.at[l, pl.ds(high * (HF + NP), HF), whole],
-            sem.at[13 + 4 * number + l],
-        )
-        for number, (side, high) in enumerate(((side_a, 1 - odd), (bulk_b, odd)))
-        for l in range(4)
-    ]
-    turned = (lax.rem(gz, 8) == 0) | (lax.rem(gz, 8) == 7)
-    copies[0].start()
-    extras_a[0].start()
-
-    @pl.when(turned)
-    def _():
-        for copy in extras(turned_b, 0, odd, 1):
-            copy.start()
-
-    @pl.when(jnp.logical_not(turned))
-    def _():
-        for copy in extras_b:
-            copy.start()
-
-    for copy in fluence_copies + [copies[2]] + extras_a[1:]:
-        copy.start()
-
-    lit[...] = illum[...].astype(F32)
-    step[...] = shifts()
     pad = jnp.zeros((PAD, N), F32)
 
     def inside(e):
@@ -163,8 +104,6 @@
                 field[l, e, 0:PAD] = pad
                 field[l, e, PAD + N : 2 * PAD + N] = pad
         return 0
-
-    lax.fori_loop(0, EXT, clear, 0)
 
     def optics(classes, e, r):
         there = inside(e)
@@ -174,53 +113,36 @@
             ab[l, e, flat] = pick(classes, [absorb_t[l, i] for i in range(8)])
             hd[l, e, rows] = pick(classes, [half_t[l, i] * there for i in range(8)])
 
-    def optics_own(p, _):
-        for c in range(N // CHUNK):
-            optics(own[p, pl.ds(c * CHUNK, CHUNK)], p + HF, c * CHUNK)
-        return 0
-
-    def optics_shared(p, _):
-        e = p + jnp.where(p < HF, 0, NP)
-        for c in range(N // CHUNK):
-            classes = shared[p, pl.ds(c * CHUNK, CHUNK)].astype(jnp.int32)
-            optics(classes, e, c * CHUNK)
-        return 0
-
-    copies[0].wait()
-    lax.fori_loop(0, NP, optics_own, 0)
-    for copy in label_copies:
-        copy.wait()
-    lax.fori_loop(0, 2 * HF, optics_shared, 0)
-    for copy in fluence_copies:
-        copy.wait()
-
-    @pl.when(gz == 0)
-    def _():
-        fl[:, HF - 1] = jnp.zeros((4, N + 2 * PAD, N), F32)
-
-    @pl.when(gz == 31)
-    def _():
-        fl[:, HF + NP] = jnp.zeros((4, N + 2 * PAD, N), F32)
-
-    def spread(to, field, l, first, last):
-        rows = field[l, first:last, PAD : PAD + N].reshape((last - first) * N, N)
-        both = jnp.dot(two_terms(rows), step[...], preferred_element_type=F32)
-        to[first:last] = both.reshape(last - first, N, 2 * N)
-
-    def per_plane(first, last, fields, body):
+    def per_plane(ranges, fields, body):
+        def spread(to, field, l):
+            parts = [field[l, a:b, PAD : PAD + N].reshape((b - a) * N, N) for a, b in ranges]
+            rows = parts[0] if len(parts) == 1 else jnp.concatenate(parts)
+            both = jnp.dot(two_terms(rows), step[...], preferred_element_type=F32)
+            at = 0
+            for a, b in ranges:
+                to[a:b] = both[at : at + (b - a) * N].reshape(b - a, N, 2 * N)
+                at += (b - a) * N
+
         def outerloop(l, _):
             for to, field in zip((near, near2), fields):
-                spread(to, field, l, first, last)
+                spread(to, field, l)
 
             def innerloop(e, _):
                 for c in range(N // CHUNK):
                     body(l, e, c * CHUNK)
                 return 0
 
-            lax.fori_loop(first, last, innerloop, 0)
+            for a, b in ranges:
+                lax.fori_loop(a, b, innerloop, 0)
             return 0
 
         lax.fori_loop(0, 4, outerloop, 0)
+
+    def face(e):
+        for l in range(4):
+            for c in range(N // CHUNK):
+                here = pl.ds(PAD + c * CHUNK, CHUNK)
+                wzs[l, e, pl.ds(c * CHUNK, CHUNK)] = hd[l, e, here] + hd[l, e + 1, here]
 
     def moved(field, l, e, r):
         flat = pl.ds(r, CHUNK)
@@ -235,11 +157,6 @@
             + wes[l, e, flat] * near[e, flat, 0:N]
             + wws[l, e, flat] * near[e, flat, N : 2 * N]
         )
-
-    for l in range(4):
-        for c in range(N // CHUNK):
-            here = pl.ds(PAD + c * CHUNK, CHUNK)
-            wzs[l, 0, pl.ds(c * CHUNK, CHUNK)] = hd[l, 0, here] + hd[l, 1, here]
 
     def first(l, e, r):
         flat = pl.ds(r, CHUNK)
@@ -272,8 +189,6 @@
         )
         tmp[l, e, here] = (spectra[l, 5] * lit[flat] + flow) * scale
 
-    per_plane(1, EXT - 1, (fl, hd), first)
-
     def second(l, e, r):
         flat = pl.ds(r, CHUNK)
         here = pl.ds(PAD + r, CHUNK)
@@ -285,21 +200,10 @@
         ms[l, e - (HF - HM), flat] = misfit
         adj[l, e, here] = absorb * misfit * scale
 
-    for copy in meas_copies:
-        copy.wait()
-    per_plane(2, EXT - 2, (tmp,), second)
-    write = pltpu.make_async_copy(fl.at[:, pl.ds(HF, NP), whole], fluence, sem.at[0])
-    write.start()
-    for l in range(4):
-        tmp[l, HF - 1] = jnp.zeros((N + 2 * PAD, N), F32)
-        tmp[l, HF + NP] = jnp.zeros((N + 2 * PAD, N), F32)
-
     def third(l, e, r):
         flat = pl.ds(r, CHUNK)
         here = pl.ds(PAD + r, CHUNK)
         tmp[l, e, here] = (ab[l, e, flat] * ms[l, e - (HF - HM), flat] + moved(adj, l, e, r)) * inv[l, e, flat]
-
-    per_plane(HF, HF + NP, (adj,), third)
 
     def couple(l, e, r):
         flat = pl.ds(r, CHUNK)
@@ -319,7 +223,136 @@
         )
         ab[l, e, flat] = 12.0 * h * h * total
 
-    per_plane(HF, HF + NP, (fl, tmp), couple)
+    return inside, clear, optics, per_plane, face, first, second, third, couple
+
+
+def inner_kernel(where, spectra, absorb_t, half_t, labels, illum, start, meas, *rest):
+    state, (own, lit, step, near, near2, sem) = rest[:11], rest[11:]
+    fl, hd, wys, tmp, adj, ab, wes, wws, wzs, inv, ms = state
+    _, clear, optics, per_plane, face, first, second, third, _ = stages(
+        where, spectra, absorb_t, half_t, lit, step, near, near2, state
+    )
+    copies = [
+        pltpu.make_async_copy(labels, own, sem.at[0]),
+        pltpu.make_async_copy(start, fl.at[:, pl.ds(HF, NP), pl.ds(PAD, N)], sem.at[1]),
+        pltpu.make_async_copy(meas, ms.at[:, pl.ds(HM, NP)], sem.at[2]),
+    ]
+    for copy in copies:
+        copy.start()
+    lit[...] = illum[...].astype(F32)
+    step[...] = shifts()
+    lax.fori_loop(0, EXT, clear, 0)
+
+    def optics_own(p, _):
+        for c in range(N // CHUNK):
+            optics(own[p, pl.ds(c * CHUNK, CHUNK)], p + HF, c * CHUNK)
+        return 0
+
+    copies[0].wait()
+    lax.fori_loop(0, NP, optics_own, 0)
+    face(HF)
+    copies[1].wait()
+    per_plane(((HF + 1, HF + NP - 1),), (fl, hd), first)
+    copies[2].wait()
+    per_plane(((HF + 2, HF + NP - 2),), (tmp,), second)
+    per_plane(((HF + 3, HF + NP - 3),), (adj,), third)
+
+
+def solve_kernel(
+    where, spectra, absorb_t, half_t, illum, side_a, bulk_b, straight_b, turned_b, *rest,
+):
+    fluence, coef_a, coef_b, edge_a, edge_b, *rest = rest[11:]
+    outs, state = rest[:6], rest[6:17]
+    shared, lit, step, near, near2, sem = rest[17:]
+    fl, hd, wys, tmp, adj, ab, wes, wws, wzs, inv, ms = state
+    sends, keeps = outs[0::2], outs[1::2]
+    inside, _, optics, per_plane, face, first, second, third, couple = stages(
+        where, spectra, absorb_t, half_t, lit, step, near, near2, state
+    )
+    gz = where[0]
+    me = where[1]
+    odd = lax.rem(gz, 2)
+    whole = pl.ds(PAD, N)
+
+    def extras(side, at, high, number):
+        first = 3 + 5 * number
+        return [
+            pltpu.make_async_copy(
+                side.at[pl.ds(at + 4 * HM, HF)], shared.at[pl.ds(high * HF, HF)], sem.at[first]
+            )
+        ] + [
+            pltpu.make_async_copy(
+                side.at[pl.ds(at + l * HM, HM)], ms.at[l, pl.ds(high * (HM + NP), HM)], sem.at[first + 1 + l]
+            )
+            for l in range(4)
+        ]
+
+    extras_a = extras(side_a, 4 * HF, 1 - odd, 0)
+    extras_b = extras(straight_b, 0, odd, 1)
+    label_copies = [extras_a[0], extras_b[0]]
+    meas_copies = extras_a[1:] + extras_b[1:]
+    fluence_copies = [
+        pltpu.make_async_copy(
+            side.at[pl.ds(l * HF, HF)],
+            fl.at[l, pl.ds(high * (HF + NP), HF), whole],
+            sem.at[13 + 4 * number + l],
+        )
+        for number, (side, high) in enumerate(((side_a, 1 - odd), (bulk_b, odd)))
+        for l in range(4)
+    ]
+    turned = (lax.rem(gz, 8) == 0) | (lax.rem(gz, 8) == 7)
+    extras_a[0].start()
+
+    @pl.when(turned)
+    def _():
+        for copy in extras(turned_b, 0, odd, 1):
+            copy.start()
+
+    @pl.when(jnp.logical_not(turned))
+    def _():
+        for copy in extras_b:
+            copy.start()
+
+    for copy in fluence_copies + extras_a[1:]:
+        copy.start()
+
+    lit[...] = illum[...].astype(F32)
+    step[...] = shifts()
+
+    def optics_shared(p, _):
+        e = p + jnp.where(p < HF, 0, NP)
+        for c in range(N // CHUNK):
+            classes = shared[p, pl.ds(c * CHUNK, CHUNK)].astype(jnp.int32)
+            optics(classes, e, c * CHUNK)
+        return 0
+
+    for copy in label_copies:
+        copy.wait()
+    lax.fori_loop(0, 2 * HF, optics_shared, 0)
+    for copy in fluence_copies:
+        copy.wait()
+
+    @pl.when(gz == 0)
+    def _():
+        fl[:, HF - 1] = jnp.zeros((4, N + 2 * PAD, N), F32)
+
+    @pl.when(gz == 31)
+    def _():
+        fl[:, HF + NP] = jnp.zeros((4, N + 2 * PAD, N), F32)
+
+    face(0)
+    last = HF + NP
+    per_plane(((1, HF + 1), (last - 1, EXT - 1)), (fl, hd), first)
+    for copy in meas_copies:
+        copy.wait()
+    per_plane(((2, HF + 2), (last - 2, EXT - 2)), (tmp,), second)
+    write = pltpu.make_async_copy(fl.at[:, pl.ds(HF, NP), whole], fluence, sem.at[0])
+    write.start()
+    for l in range(4):
+        tmp[l, HF - 1] = jnp.zeros((N + 2 * PAD, N), F32)
+        tmp[l, last] = jnp.zeros((N + 2 * PAD, N), F32)
+    per_plane(((HF, HF + 3), (last - 3, last)), (adj,), third)
+    per_plane(((HF, last),), (fl, tmp), couple)
 
     for coef, edge, high in ((coef_a, edge_a, 1 - odd), (coef_b, edge_b, odd)):
         e = HF + high * (NP - 1)
@@ -491,29 +524,41 @@
     half_t = 0.5 / (3.0 * (absorb_t + spectra[:, 4, None] * label_table[None, :, 4]))
 
     sizes = [last - first for first, last in PARTS]
-    field = pltpu.VMEM((4, EXT, N + 2 * PAD, N), F32)
     plane = jax.ShapeDtypeStruct((4, N, N), F32)
+    held = (
+        [pltpu.VMEM((4, EXT, N + 2 * PAD, N), F32)] * 5
+        + [pltpu.VMEM((4, EXT, N, N), F32)] * 5
+        + [pltpu.VMEM((4, NP + 2 * HM, N, N), F32)]
+    )
+    work = [
+        pltpu.VMEM((N, N), F32),
+        pltpu.VMEM((2 * N, 2 * N), jnp.bfloat16),
+        pltpu.VMEM((EXT, N, 2 * N), F32),
+        pltpu.VMEM((EXT, N, 2 * N), F32),
+    ]
+    state = pl.pallas_call(
+        inner_kernel,
+        out_shape=held,
+        in_specs=[SMEM] * 4 + [ANY] + [VMEM] + [ANY] * 2,
+        out_specs=[VMEM] * 11,
+        scratch_shapes=[pltpu.VMEM((NP, N, N), jnp.int32)] + work + [pltpu.SemaphoreType.DMA((3,))],
+        compiler_params=small,
+        name="inner",
+    )(where, spectra, absorb_t, half_t, in_hbm(labels), illumination, *map(in_hbm, (fluence_start, measured)))
     fluence, coef_a, coef_b, edge_a, edge_b, *out = pl.pallas_call(
         solve_kernel,
         out_shape=[jax.ShapeDtypeStruct((4, NP, N, N), F32)]
         + [plane] * 4
-        + [jax.ShapeDtypeStruct((4, size, ROWS, N), F32) for size in sizes for _ in range(2)],
-        in_specs=[SMEM] * 4 + [ANY] + [VMEM] + [ANY] * 6,
-        out_specs=[ANY] + [VMEM] * 10,
-        scratch_shapes=[
-            pltpu.VMEM((NP, N, N), jnp.int32),
-            pltpu.VMEM((2 * HF, N, N), F32),
-            pltpu.VMEM((N, N), F32),
-            pltpu.VMEM((2 * N, 2 * N), jnp.bfloat16),
-        ]
-        + [pltpu.VMEM((EXT, N, 2 * N), F32)] * 2
-        + [field] * 5
-        + [pltpu.VMEM((4, EXT, N, N), F32)] * 5
-        + [pltpu.VMEM((4, NP + 2 * HM, N, N), F32), pltpu.SemaphoreType.DMA((21,))],
-        compiler_params=pltpu.CompilerParams(vmem_limit_bytes=52 * 2**20),
+        + [jax.ShapeDtypeStruct((4, size, ROWS, N), F32) for size in sizes for _ in range(2)]
+        + held,
+        in_specs=[SMEM] * 4 + [VMEM] + [ANY] * 4 + [VMEM] * 11,
+        out_specs=[ANY] + [VMEM] * 21,
+        input_output_aliases={9 + i: 11 + i for i in range(11)},
+        scratch_shapes=[pltpu.VMEM((2 * HF, N, N), F32)] + work + [pltpu.SemaphoreType.DMA((21,))],
+        compiler_params=small,
         name="solve",
-    )(where, spectra, absorb_t, half_t, labels, illumination,
-      *map(in_hbm, (fluence_start, measured)), side_a, bulk_b, straight_b, turned_b)
+    )(where, spectra, absorb_t, half_t, illumination, side_a, bulk_b, straight_b, turned_b, *map(in_vmem, state))
+    out = out[:6]
     sends = list(out[0::2])
     keeps = list(out[1::2])
 

time: 143 us -> 137 us (0.958)
  waiting for transfers between devices: 40 us -> 33.2 us
  Pallas kernels: 35.3 us -> 39 us
  starting transfers between devices: 61.6 us -> 59.2 us
    pallas_call x0 -> x1, Pallas kernels: none -> 9.75 us  [shards(): pl.pallas_call(inner_kernel, out_shape=held, in_specs=[SMEM] * 4 + [ANY]...]
    pallas_call x1, Pallas kernels: 26.8 us -> 20.7 us  [shards(): pl.pallas_call(solve_kernel, out_shape=[jax.ShapeDtypeStruct((4, NP, N, N...]
    ppermute x1, waiting for transfers between devices: 6.05 us -> 0.01 us  [shards(): bulk_b = lax.ppermute(bulk_b, 'gz', OFF_CHIP)]
    ppermute x2, starting transfers between devices: 2.06 us -> 6.62 us  [beside(): return (lax.ppermute(a, 'gz', ON_CHIP), lax.ppermute(b, 'gz', OFF_CHIP))]
    all_to_all x1, starting transfers between devices: 8.05 us -> 4.32 us  [shards(): slab = jnp.sum(lax.all_to_all(sums, 'gz', 0, 0), axis=0)]
    ppermute x21, starting transfers between devices: 34.1 us -> 30.8 us  [swap(): return lax.ppermute(x, 'wl', [(i, i ^ code) for i in range(8)])]
  transfers between devices with their start and end apart: 28 -> 28, of which waited for: 14 -> 10; matrix products, arithmetic and copies ran while one was open for 3% -> 3% of each run, Pallas kernels for 2% -> 9%
where the time goes in v4:
time: 137 us
  starting transfers between devices  59.2 us (43%)
  Pallas kernels  39 us (28%)
  waiting for transfers between devices  33.2 us (24%)
  other arithmetic  3.77 us (3%)
    ppermute x21, starting transfers between devices, swap(): return lax.ppermute(x, 'wl', [(i, i ^ code) for i in range(8)])  30.8 us
    ppermute x21, waiting for transfers between devices, swap(): return lax.ppermute(x, 'wl', [(i, i ^ code) for i in range(8)])  24.5 us
    pallas_call x1, Pallas kernels, shards(): pl.pallas_call(solve_kernel, out_shape=[jax.ShapeDtypeStruct((4, NP, N, N...  20.7 us
    pallas_call x1, Pallas kernels, shards(): pl.pallas_call(inner_kernel, out_shape=held, in_specs=[SMEM] * 4 + [ANY]...  9.75 us
    ppermute x1, starting transfers between devices, shards(): turned_b = lax.ppermute(straight_b, 'gz', ALONG)  8.55 us
    all_to_all x1, waiting for transfers between devices, shards(): slab = jnp.sum(lax.all_to_all(sums, 'gz', 0, 0), axis=0)  6.76 us
    ppermute x2, starting transfers between devices, beside(): return (lax.ppermute(a, 'gz', ON_CHIP), lax.ppermute(b, 'gz', OFF_CHIP))  6.62 us
    ppermute x1, starting transfers between devices, shards(): bulk_b = lax.ppermute(bulk_b, 'gz', OFF_CHIP)  5.84 us
  transfers between devices with their start and end apart: 28, of which 10 were waited for; matrix products, arithmetic and copies ran while one was open for 3% of the time, Pallas kernels for 9%

profile of v4, /device:TPU:8, one launch (start us, length us, event | category | flops | bytes accessed | tf_op | source)
XLA Modules:
  0.0 136.8 jit_solution(6726425524226152018)
XLA Ops:
  2.2 2.5 %pack.3 = (f32[12,128,128]{2,1,0:T(8,128)}, f32[7,128,128]{2,1,0:T(8,128)}) custom-call(s32[1]{0:T(128)S(6)} %rem.18.high, s32[8,128,128]{2,1,0:T(8,128)} %labels.7, f32[4,8,128,128]{3,2,1,0:T(8,128)} %start.5, f32[4,8,128,128]{3,2,1,0:T(8,128)} %meas.5), custom_call_target="tpu_custom_call" | custom-call | tf_op jit(solution)/shard_map/pack/pallas_call | solution.py:503
  4.7 2.9 %collective-permute-start.2 = (f32[7,128,128]{2,1,0:T(8,128)}, f32[7,128,128]{2,1,0:T(8,128)}, u32[]{:S(2)}, u32[]{:S(2)}) collective-permute-start(f32[7,128,128]{2,1,0:T(8,128)} %get-tuple-element.38), channel_id=1, source_target_pairs={{0,7},{1,2},{2,1},{3,4},{4,3},{5,6},{6,5},{7,0},{8,15},{9,10},{10,... | collective-permute-start | bytes 1376264 | tf_op jit(solution)/shard_map/ppermute | solution.py:516
  7.6 5.8 %collective-permute-start.1 = (f32[12,128,128]{2,1,0:T(8,128)}, f32[12,128,128]{2,1,0:T(8,128)S(1)}, u32[]{:S(2)}, u32[]{:S(2)}) collective-permute-start(f32[12,128,128]{2,1,0:T(8,128)} %get-tuple-element.37), channel_id=1, source_target_pairs={{0,31},{1,2},{2,1},{3,4},{4,3},{5,6},{6,5},{7,8},{8,7},{9,10},{10,... | collective-permute-start | bytes 2359304 | tf_op jit(solution)/shard_map/ppermute | solution.py:515
  13.5 1.9 %collective-permute-done.2.straight_b = f32[7,128,128]{2,1,0:T(8,128)} collective-permute-done((f32[7,128,128]{2,1,0:T(8,128)}, f32[7,128,128]{2,1,0:T(8,128)}, u32[]{:S(2)}, u32[]{:S(2)}) %collective-permute-start.2) | collective-permute-done | bytes 458784 | tf_op jit(solution)/shard_map/ppermute | solution.py:516
  15.4 8.5 %collective-permute-start.3 = (f32[7,128,128]{2,1,0:T(8,128)}, f32[7,128,128]{2,1,0:T(8,128)S(1)}, u32[]{:S(2)}, u32[]{:S(2)}) collective-permute-start(f32[7,128,128]{2,1,0:T(8,128)} %collective-permute-done.2.straight_b), channel_id=1, source_target_pairs={{0,8},{8,16},{16,24},{15,7},{23,15},{31,23},{32,40},{40,48},{48,56... | collective-permute-start | bytes 1376264 | tf_op jit(solution)/shard_map/ppermute | solution.py:518
  24.7 9.7 %inner.1 = (f32[4,14,144,128]{3,2,1,0:T(8,128)S(1)}, f32[4,14,144,128]{3,2,1,0:T(8,128)S(1)}, f32[4,14,144,128]{3,2,1,0:T(8,128)S(1)}, f32[4,14,144,128]{3,2,1,0...) custom-call(s32[2]{0:T(128)S(1)} %pad_add_fusion.where, ...), custom_call_target="tpu_custom_call" | custom-call | tf_op jit(solution)/shard_map/inner/pallas_call | solution.py:539
  34.5 20.7 %solve.1 = (f32[4,8,128,128]{3,2,1,0:T(8,128)}, f32[4,128,128]{2,1,0:T(8,128)}, f32[4,128,128]{2,1,0:T(8,128)}, f32[4,128,128]{2,1,0:T(8,128)}, f32[4,128,128]{2...) custom-call(s32[2]{0:T(128)} %copy-done.8, ...), custom_call_target="tpu_custom_call", output_to_operand_aliasing={{11}: (9, {}), {12}: (10, {}), {13}: (11, {}), {14}: (12, {... | custom-call | tf_op jit(solution)/shard_map/solve/pallas_call | solution.py:548
  58.5 6.6 %collective-permute-start.5 = (f32[4,128,128]{2,1,0:T(8,128)}, f32[4,128,128]{2,1,0:T(8,128)S(1)}, u32[]{:S(2)}, u32[]{:S(2)}) collective-permute-start(f32[4,128,128]{2,1,0:T(8,128)} %get-tuple-element.54), channel_id=1, source_target_pairs={{0,31},{1,2},{2,1},{3,4},{4,3},{5,6},{6,5},{7,8},{8,7},{9,10},{10,... | collective-permute-start | bytes 786440 | tf_op jit(solution)/shard_map/ppermute | solution.py:488
  65.1 1.9 %collective-permute-start.6 = (f32[4,14,16,128]{3,2,1,0:T(8,128)}, f32[4,14,16,128]{3,2,1,0:T(8,128)S(1)}, u32[]{:S(2)}, u32[]{:S(2)}) collective-permute-start(f32[4,14,16,128]{3,2,1,0:T(8,128)} %get-tuple-element.56), channel_id=1, source_target_pairs={{0,64},{32,96},{64,0},{96,32},{128,192},{160,224},{192,128},{224,1... | collective-permute-start | bytes 1376264 | tf_op jit(solution)/shard_map/ppermute | solution.py:478
  69.2 6.8 %collective-permute-done.6 = f32[4,14,16,128]{3,2,1,0:T(8,128)S(1)} collective-permute-done((f32[4,14,16,128]{3,2,1,0:T(8,128)}, f32[4,14,16,128]{3,2,1,0:T(8,128)S(1)}, u32[]{:S(2)}, u32[]{:S(2)}) %collective-permute-start.6) | collective-permute-done | bytes 458784 | tf_op jit(solution)/shard_map/ppermute | solution.py:478
  77.8 2.5 %collective-permute-start.9 = (f32[4,2,16,128]{3,2,1,0:T(8,128)S(1)}, f32[4,2,16,128]{3,2,1,0:T(8,128)S(1)}, u32[]{:S(2)}, u32[]{:S(2)}) collective-permute-start(f32[4,2,16,128]{3,2,1,0:T(8,128)S(1)} %get-tuple-element.64), channel_id=1, source_target_pairs={{0,64},{32,96},{64,0},{96,32},{128,192},{160,224},{192,128},{224,1... | collective-permute-start | bytes 196616 | tf_op jit(solution)/shard_map/ppermute | solution.py:478
  83.2 2.9 %collective-permute-done.13 = f32[2,13,16,128]{3,2,1,0:T(8,128)S(1)} collective-permute-done((f32[2,13,16,128]{3,2,1,0:T(8,128)S(1)}, f32[2,13,16,128]{3,2,1,0:T(8,128)S(1)}, u32[]{:S(2)}, u32[]{:S(2)}) %collective-permute-start.13) | collective-permute-done | bytes 213024 | tf_op jit(solution)/shard_map/ppermute | solution.py:478
  90.3 2.8 %collective-permute-done.11.late_recv = f32[1,2,16,128]{3,2,1,0:T(8,128)S(1)} collective-permute-done((f32[1,2,16,128]{3,2,1,0:T(8,128)S(1)}, f32[1,2,16,128]{3,2,1,0:T(8,128)S(1)}, u32[]{:S(2)}, u32[]{:S(2)}) %collective-permute-start.11) | collective-permute-done | bytes 16416 | tf_op jit(solution)/shard_map/ppermute | solution.py:478
  94.4 4.3 %all-to-all-start = ((f32[32,1,128]{2,1,0:T(1,128)}), f32[32,1,128]{2,1,0:T(1,128)S(1)}, u32[]{:S(2)}, u32[]{:S(2)}) async-start(f32[32,1,128]{2,1,0:T(1,128)} %get-tuple-element.66), calls=%async_computation | async-start | bytes 32768 | tf_op jit(solution)/shard_map/all_to_all | solution.py:606
  98.7 2.9 %collective-permute-start.21 = (f32[1,13,16,128]{3,2,1,0:T(8,128)S(1)}, f32[1,13,16,128]{3,2,1,0:T(8,128)S(1)}, u32[]{:S(2)}, u32[]{:S(2)}) collective-permute-start(f32[1,13,16,128]{3,2,1,0:T(8,128)S(1)} %get-tuple-element.67.refs_4_), channel_id=1, source_target_pairs={{0,64},{32,96},{64,0},{96,32},{128,192},{160,224},{192,128},{224,1... | collective-permute-start | bytes 319496 | tf_op jit(solution)/shard_map/ppermute | solution.py:478
  101.7 6.8 %all-to-all-done = f32[32,1,128]{2,1,0:T(1,128)S(1)} async-done(((f32[32,1,128]{2,1,0:T(1,128)}), f32[32,1,128]{2,1,0:T(1,128)S(1)}, u32[]{:S(2)}, u32[]{:S(2)}) %all-to-all-start) | async-done | bytes 16416 | tf_op jit(solution)/shard_map/all_to_all | solution.py:606
  112.1 2.2 %collective-permute-done.18.refs_1_ = f32[1,15,16,128]{3,2,1,0:T(8,128)S(1)} collective-permute-done((f32[1,15,16,128]{3,2,1,0:T(8,128)S(1)}, f32[1,15,16,128]{3,2,1,0:T(8,128)S(1)}, u32[]{:S(2)}, u32[]{:S(2)}) %collective-permute-start.18) | collective-permute-done | bytes 122912 | tf_op jit(solution)/shard_map/ppermute | solution.py:478
  114.3 2.0 %collective-permute-start.19 = (f32[2,15,16,128]{3,2,1,0:T(8,128)S(1)}, f32[2,15,16,128]{3,2,1,0:T(8,128)S(1)}, u32[]{:S(2)}, u32[]{:S(2)}) collective-permute-start(f32[2,15,16,128]{3,2,1,0:T(8,128)S(1)} %pad_maximum_fusion.3), channel_id=1, source_target_pairs={{0,192},{32,224},{64,128},{96,160},{128,64},{160,96},{192,0},{224,... | collective-permute-start | bytes 737288 | tf_op jit(solution)/shard_map/ppermute | solution.py:478
  116.3 2.2 %collective-permute-start.25 = (f32[2,13,16,128]{3,2,1,0:T(8,128)S(1)}, f32[2,13,16,128]{3,2,1,0:T(8,128)S(1)}, u32[]{:S(2)}, u32[]{:S(2)}) collective-permute-start(f32[2,13,16,128]{3,2,1,0:T(8,128)S(1)} %pad_maximum_fusion.5), channel_id=1, source_target_pairs={{0,64},{32,96},{64,0},{96,32},{128,192},{160,224},{192,128},{224,1... | collective-permute-start | bytes 638984 | tf_op jit(solution)/shard_map/ppermute | solution.py:478
  118.6 1.8 %collective-permute-start.23 = (f32[4,13,16,128]{3,2,1,0:T(8,128)S(1)}, f32[4,13,16,128]{3,2,1,0:T(8,128)S(1)}, u32[]{:S(2)}, u32[]{:S(2)}) collective-permute-start(f32[4,13,16,128]{3,2,1,0:T(8,128)S(1)} %pad_maximum_fusion.1), channel_id=1, source_target_pairs={{0,192},{32,224},{64,128},{96,160},{128,64},{160,96},{192,0},{224,... | collective-permute-start | bytes 1277960 | tf_op jit(solution)/shard_map/ppermute | solution.py:478
  121.4 4.3 %collective-permute-start.20 = (f32[4,15,16,128]{3,2,1,0:T(8,128)S(1)}, f32[4,15,16,128]{3,2,1,0:T(8,128)S(1)}, u32[]{:S(2)}, u32[]{:S(2)}) collective-permute-start(f32[4,15,16,128]{3,2,1,0:T(8,128)S(1)} %pad_maximum_fusion), channel_id=1, source_target_pairs={{0,64},{32,96},{64,0},{96,32},{128,192},{160,224},{192,128},{224,1... | collective-permute-start | bytes 1474568 | tf_op jit(solution)/shard_map/ppermute | solution.py:478
  126.8 3.0 %collective-permute-done.23.refs_7_ = f32[4,13,16,128]{3,2,1,0:T(8,128)S(1)} collective-permute-done((f32[4,13,16,128]{3,2,1,0:T(8,128)S(1)}, f32[4,13,16,128]{3,2,1,0:T(8,128)S(1)}, u32[]{:S(2)}, u32[]{:S(2)}) %collective-permute-start.23) | collective-permute-done | bytes 426016 | tf_op jit(solution)/shard_map/ppermute | solution.py:478
  129.8 4.1 %collective-permute-done.26.refs_11_ = f32[4,13,16,128]{3,2,1,0:T(8,128)S(1)} collective-permute-done((f32[4,13,16,128]{3,2,1,0:T(8,128)S(1)}, f32[4,13,16,128]{3,2,1,0:T(8,128)S(1)}, u32[]{:S(2)}, u32[]{:S(2)}) %collective-permute-start.26) | collective-permute-done | bytes 426016 | tf_op jit(solution)/shard_map/ppermute | solution.py:478
  133.9 2.7 %final.1 = (f32[4,8,128,128]{3,2,1,0:T(8,128)}, f32[8,128,128]{2,1,0:T(8,128)}) custom-call(s32[2]{0:T(128)S(1)} %copy-done.9, f32[8,5]{1,0:T(8,128)S(1)} %copy-done.4, s32[8,128,128]{2,1,0:T(8,128)S(1)} %copy-done, f32[1,15,16,128]{3,2,1,0:T(8,128)S(1)} %pad_maximum_fusion.6.refs_0_, f32[1,15,16,128]{3,2,1,0:T(8,128)S(1)} %collective-permute-done.18.refs_1_, ...), custom_call_target="tpu_custom_call" | custom-call | tf_op jit(solution)/shard_map/final/pallas_call | solution.py:613
  (80 shorter events, 23.7 us)
Async XLA Ops:
  2.1 32.3 %collective-permute-start = (f32[19,128,128]{2,1,0:T(8,128)S(1)}, f32[19,128,128]{2,1,0:T(8,128)S(1)}, u32[]{:S(2)}, u32[]{:S(2)}) collective-permute-start(f32[19,128,128]{2,1,0:T(8,128)S(1)} %pack.2), channel_id=1, source_target_pairs={{0,1},{1,0},{2,3},{3,2},{4,5},{5,4},{6,7},{7,6},{8,9},{9,8},{10,11... | collective-permute-start | bytes 3735560 | tf_op jit(solution)/shard_map/ppermute | solution.py:517
  4.7 10.7 %collective-permute-start.2 = (f32[7,128,128]{2,1,0:T(8,128)}, f32[7,128,128]{2,1,0:T(8,128)}, u32[]{:S(2)}, u32[]{:S(2)}) collective-permute-start(f32[7,128,128]{2,1,0:T(8,128)} %get-tuple-element.38), channel_id=1, source_target_pairs={{0,7},{1,2},{2,1},{3,4},{4,3},{5,6},{6,5},{7,0},{8,15},{9,10},{10,... | collective-permute-start | bytes 1376264 | tf_op jit(solution)/shard_map/ppermute | solution.py:516
  7.6 26.8 %collective-permute-start.1 = (f32[12,128,128]{2,1,0:T(8,128)}, f32[12,128,128]{2,1,0:T(8,128)S(1)}, u32[]{:S(2)}, u32[]{:S(2)}) collective-permute-start(f32[12,128,128]{2,1,0:T(8,128)} %get-tuple-element.37), channel_id=1, source_target_pairs={{0,31},{1,2},{2,1},{3,4},{4,3},{5,6},{6,5},{7,8},{8,7},{9,10},{10,... | collective-permute-start | bytes 2359304 | tf_op jit(solution)/shard_map/ppermute | solution.py:515
  15.4 19.0 %collective-permute-start.3 = (f32[7,128,128]{2,1,0:T(8,128)}, f32[7,128,128]{2,1,0:T(8,128)S(1)}, u32[]{:S(2)}, u32[]{:S(2)}) collective-permute-start(f32[7,128,128]{2,1,0:T(8,128)} %collective-permute-done.2.straight_b), channel_id=1, source_target_pairs={{0,8},{8,16},{16,24},{15,7},{23,15},{31,23},{32,40},{40,48},{48,56... | collective-permute-start | bytes 1376264 | tf_op jit(solution)/shard_map/ppermute | solution.py:518
  55.2 11.7 %collective-permute-start.7 = (f32[4,13,16,128]{3,2,1,0:T(8,128)}, f32[4,13,16,128]{3,2,1,0:T(8,128)S(1)}, u32[]{:S(2)}, u32[]{:S(2)}) collective-permute-start(f32[4,13,16,128]{3,2,1,0:T(8,128)} %get-tuple-element.58), channel_id=1, source_target_pairs={{0,192},{32,224},{64,128},{96,160},{128,64},{160,96},{192,0},{224,... | collective-permute-start | bytes 1277960 | tf_op jit(solution)/shard_map/ppermute | solution.py:478
  56.9 11.2 %collective-permute-start.8 = (f32[4,13,16,128]{3,2,1,0:T(8,128)}, f32[4,13,16,128]{3,2,1,0:T(8,128)S(1)}, u32[]{:S(2)}, u32[]{:S(2)}) collective-permute-start(f32[4,13,16,128]{3,2,1,0:T(8,128)} %get-tuple-element.60), channel_id=1, source_target_pairs={{0,32},{32,0},{64,96},{96,64},{128,160},{160,128},{192,224},{224,1... | collective-permute-start | bytes 1277960 | tf_op jit(solution)/shard_map/ppermute | solution.py:478
  58.5 18.6 %collective-permute-start.4 = (f32[4,128,128]{2,1,0:T(8,128)}, f32[4,128,128]{2,1,0:T(8,128)S(1)}, u32[]{:S(2)}, u32[]{:S(2)}) collective-permute-start(f32[4,128,128]{2,1,0:T(8,128)} %get-tuple-element.53), channel_id=1, source_target_pairs={{0,1},{1,0},{2,3},{3,2},{4,5},{5,4},{6,7},{7,6},{8,9},{9,8},{10,11... | collective-permute-start | bytes 786440 | tf_op jit(solution)/shard_map/ppermute | solution.py:488
  58.5 18.6 %collective-permute-start.5 = (f32[4,128,128]{2,1,0:T(8,128)}, f32[4,128,128]{2,1,0:T(8,128)S(1)}, u32[]{:S(2)}, u32[]{:S(2)}) collective-permute-start(f32[4,128,128]{2,1,0:T(8,128)} %get-tuple-element.54), channel_id=1, source_target_pairs={{0,31},{1,2},{2,1},{3,4},{4,3},{5,6},{6,5},{7,8},{8,7},{9,10},{10,... | collective-permute-start | bytes 786440 | tf_op jit(solution)/shard_map/ppermute | solution.py:488
  65.1 10.9 %collective-permute-start.6 = (f32[4,14,16,128]{3,2,1,0:T(8,128)}, f32[4,14,16,128]{3,2,1,0:T(8,128)S(1)}, u32[]{:S(2)}, u32[]{:S(2)}) collective-permute-start(f32[4,14,16,128]{3,2,1,0:T(8,128)} %get-tuple-element.56), channel_id=1, source_target_pairs={{0,64},{32,96},{64,0},{96,32},{128,192},{160,224},{192,128},{224,1... | collective-permute-start | bytes 1376264 | tf_op jit(solution)/shard_map/ppermute | solution.py:478
  80.2 5.8 %collective-permute-start.13 = (f32[2,13,16,128]{3,2,1,0:T(8,128)S(1)}, f32[2,13,16,128]{3,2,1,0:T(8,128)S(1)}, u32[]{:S(2)}, u32[]{:S(2)}) collective-permute-start(f32[2,13,16,128]{3,2,1,0:T(8,128)S(1)} %get-tuple-element.88), channel_id=1, source_target_pairs={{0,32},{32,0},{64,96},{96,64},{128,160},{160,128},{192,224},{224,1... | collective-permute-start | bytes 638984 | tf_op jit(solution)/shard_map/ppermute | solution.py:478
  80.2 6.2 %collective-permute-start.14 = (f32[2,13,16,128]{3,2,1,0:T(8,128)S(1)}, f32[2,13,16,128]{3,2,1,0:T(8,128)S(1)}, u32[]{:S(2)}, u32[]{:S(2)}) collective-permute-start(f32[2,13,16,128]{3,2,1,0:T(8,128)S(1)} %get-tuple-element.86), channel_id=1, source_target_pairs={{0,64},{32,96},{64,0},{96,32},{128,192},{160,224},{192,128},{224,1... | collective-permute-start | bytes 638984 | tf_op jit(solution)/shard_map/ppermute | solution.py:478
  80.4 7.6 %collective-permute-start.12 = (f32[2,14,16,128]{3,2,1,0:T(8,128)S(1)}, f32[2,14,16,128]{3,2,1,0:T(8,128)S(1)}, u32[]{:S(2)}, u32[]{:S(2)}) collective-permute-start(f32[2,14,16,128]{3,2,1,0:T(8,128)S(1)} %get-tuple-element.84), channel_id=1, source_target_pairs={{0,192},{32,224},{64,128},{96,160},{128,64},{160,96},{192,0},{224,... | collective-permute-start | bytes 688136 | tf_op jit(solution)/shard_map/ppermute | solution.py:478
  82.5 6.0 %collective-permute-start.10 = (f32[2,2,16,128]{3,2,1,0:T(8,128)S(1)}, f32[2,2,16,128]{3,2,1,0:T(8,128)S(1)}, u32[]{:S(2)}, u32[]{:S(2)}) collective-permute-start(f32[2,2,16,128]{3,2,1,0:T(8,128)S(1)} %get-tuple-element.96), channel_id=1, source_target_pairs={{0,192},{32,224},{64,128},{96,160},{128,64},{160,96},{192,0},{224,... | collective-permute-start | bytes 98312 | tf_op jit(solution)/shard_map/ppermute | solution.py:478
  86.1 7.0 %collective-permute-start.16 = (f32[1,13,16,128]{3,2,1,0:T(8,128)S(1)}, f32[1,13,16,128]{3,2,1,0:T(8,128)S(1)}, u32[]{:S(2)}, u32[]{:S(2)}) collective-permute-start(f32[1,13,16,128]{3,2,1,0:T(8,128)S(1)} %get-tuple-element.93), channel_id=1, source_target_pairs={{0,64},{32,96},{64,0},{96,32},{128,192},{160,224},{192,128},{224,1... | collective-permute-start | bytes 319496 | tf_op jit(solution)/shard_map/ppermute | solution.py:478
  86.5 6.6 %collective-permute-start.17 = (f32[1,13,16,128]{3,2,1,0:T(8,128)S(1)}, f32[1,13,16,128]{3,2,1,0:T(8,128)S(1)}, u32[]{:S(2)}, u32[]{:S(2)}) collective-permute-start(f32[1,13,16,128]{3,2,1,0:T(8,128)S(1)} %get-tuple-element.91), channel_id=1, source_target_pairs={{0,192},{32,224},{64,128},{96,160},{128,64},{160,96},{192,0},{224,... | collective-permute-start | bytes 319496 | tf_op jit(solution)/shard_map/ppermute | solution.py:478
  94.4 14.0 %all-to-all-start = ((f32[32,1,128]{2,1,0:T(1,128)}), f32[32,1,128]{2,1,0:T(1,128)S(1)}, u32[]{:S(2)}, u32[]{:S(2)}) async-start(f32[32,1,128]{2,1,0:T(1,128)} %get-tuple-element.66), calls=%async_computation | async-start | bytes 32768 | tf_op jit(solution)/shard_map/all_to_all | solution.py:606
  98.7 12.4 %collective-permute-start.21 = (f32[1,13,16,128]{3,2,1,0:T(8,128)S(1)}, f32[1,13,16,128]{3,2,1,0:T(8,128)S(1)}, u32[]{:S(2)}, u32[]{:S(2)}) collective-permute-start(f32[1,13,16,128]{3,2,1,0:T(8,128)S(1)} %get-tuple-element.67.refs_4_), channel_id=1, source_target_pairs={{0,64},{32,96},{64,0},{96,32},{128,192},{160,224},{192,128},{224,1... | collective-permute-start | bytes 319496 | tf_op jit(solution)/shard_map/ppermute | solution.py:478
  109.7 6.6 %collective-permute-start.24 = (f32[1,13,16,128]{3,2,1,0:T(8,128)S(1)}, f32[1,13,16,128]{3,2,1,0:T(8,128)S(1)}, u32[]{:S(2)}, u32[]{:S(2)}) collective-permute-start(f32[1,13,16,128]{3,2,1,0:T(8,128)S(1)} %get-tuple-element.68.refs_8_), channel_id=1, source_target_pairs={{0,192},{32,224},{64,128},{96,160},{128,64},{160,96},{192,0},{224,... | collective-permute-start | bytes 319496 | tf_op jit(solution)/shard_map/ppermute | solution.py:478
  111.1 7.5 %collective-permute-start.22 = (f32[2,13,16,128]{3,2,1,0:T(8,128)S(1)}, f32[2,13,16,128]{3,2,1,0:T(8,128)S(1)}, u32[]{:S(2)}, u32[]{:S(2)}) collective-permute-start(f32[2,13,16,128]{3,2,1,0:T(8,128)S(1)} %pad_maximum_fusion.4), channel_id=1, source_target_pairs={{0,32},{32,0},{64,96},{96,64},{128,160},{160,128},{192,224},{224,1... | collective-permute-start | bytes 638984 | tf_op jit(solution)/shard_map/ppermute | solution.py:478
  114.3 7.0 %collective-permute-start.19 = (f32[2,15,16,128]{3,2,1,0:T(8,128)S(1)}, f32[2,15,16,128]{3,2,1,0:T(8,128)S(1)}, u32[]{:S(2)}, u32[]{:S(2)}) collective-permute-start(f32[2,15,16,128]{3,2,1,0:T(8,128)S(1)} %pad_maximum_fusion.3), channel_id=1, source_target_pairs={{0,192},{32,224},{64,128},{96,160},{128,64},{160,96},{192,0},{224,... | collective-permute-start | bytes 737288 | tf_op jit(solution)/shard_map/ppermute | solution.py:478
  116.3 9.3 %collective-permute-start.25 = (f32[2,13,16,128]{3,2,1,0:T(8,128)S(1)}, f32[2,13,16,128]{3,2,1,0:T(8,128)S(1)}, u32[]{:S(2)}, u32[]{:S(2)}) collective-permute-start(f32[2,13,16,128]{3,2,1,0:T(8,128)S(1)} %pad_maximum_fusion.5), channel_id=1, source_target_pairs={{0,64},{32,96},{64,0},{96,32},{128,192},{160,224},{192,128},{224,1... | collective-permute-start | bytes 638984 | tf_op jit(solution)/shard_map/ppermute | solution.py:478
  118.6 11.2 %collective-permute-start.23 = (f32[4,13,16,128]{3,2,1,0:T(8,128)S(1)}, f32[4,13,16,128]{3,2,1,0:T(8,128)S(1)}, u32[]{:S(2)}, u32[]{:S(2)}) collective-permute-start(f32[4,13,16,128]{3,2,1,0:T(8,128)S(1)} %pad_maximum_fusion.1), channel_id=1, source_target_pairs={{0,192},{32,224},{64,128},{96,160},{128,64},{160,96},{192,0},{224,... | collective-permute-start | bytes 1277960 | tf_op jit(solution)/shard_map/ppermute | solution.py:478
  121.4 12.6 %collective-permute-start.20 = (f32[4,15,16,128]{3,2,1,0:T(8,128)S(1)}, f32[4,15,16,128]{3,2,1,0:T(8,128)S(1)}, u32[]{:S(2)}, u32[]{:S(2)}) collective-permute-start(f32[4,15,16,128]{3,2,1,0:T(8,128)S(1)} %pad_maximum_fusion), channel_id=1, source_target_pairs={{0,64},{32,96},{64,0},{96,32},{128,192},{160,224},{192,128},{224,1... | collective-permute-start | bytes 1474568 | tf_op jit(solution)/shard_map/ppermute | solution.py:478
  125.7 8.2 %collective-permute-start.26 = (f32[4,13,16,128]{3,2,1,0:T(8,128)S(1)}, f32[4,13,16,128]{3,2,1,0:T(8,128)S(1)}, u32[]{:S(2)}, u32[]{:S(2)}) collective-permute-start(f32[4,13,16,128]{3,2,1,0:T(8,128)S(1)} %pad_maximum_fusion.2), channel_id=1, source_target_pairs={{0,32},{32,0},{64,96},{96,64},{128,160},{160,128},{192,224},{224,1... | collective-permute-start | bytes 1277960 | tf_op jit(solution)/shard_map/ppermute | solution.py:478
  (14 other events, 238.8 us)

commit v5 on v4

--- a/solution.py
+++ b/solution.py
@@ -12,6 +12,8 @@
 HM = 1
 NP = 8
 EXT = NP + 2 * HF
+TOTAL = 4 * (HF + HM) + HF
+BULK = 4 * HF + 2 * HM
 N = 128
 PAD = 8
 CHUNK = 32
@@ -67,26 +69,36 @@
     return jnp.where(bit2, mid[1], mid[0])
 
 
-def pack_kernel(high, labels, start, meas, *rest):
-    *outs, ints, sem = rest
-    bulk, extra = outs[0], outs[-1]
-    at = 4 * HF if len(outs) == 1 else 0
-    flip = high[0]
-    copies = [pltpu.make_async_copy(labels.at[pl.ds(flip * (NP - HF), HF)], ints, sem.at[8])]
-    for l in range(4):
+def pack_kernel(where, labels, start, meas, bulk_b, extra_b, side_a, ints, sem):
+    odd = lax.rem(where[0], 2)
+    copies = []
+    for side, flip in enumerate((odd, 1 - odd)):
+
+        def place(at, count):
+            if side == 1:
+                return side_a.at[pl.ds(at, count)]
+            return bulk_b.at[pl.ds(at, count)] if at < BULK else extra_b.at[pl.ds(at - BULK, count)]
+
         copies.append(
-            pltpu.make_async_copy(start.at[l, pl.ds(flip * (NP - HF), HF)], bulk.at[pl.ds(l * HF, HF)], sem.at[l])
+            pltpu.make_async_copy(labels.at[pl.ds(flip * (NP - HF), HF)], ints.at[side], sem.at[side, 8])
         )
-        copies.append(
-            pltpu.make_async_copy(
-                meas.at[l, pl.ds(flip * (NP - HM), HM)], extra.at[pl.ds(at + l * HM, HM)], sem.at[4 + l]
+        for l in range(4):
+            copies.append(
+                pltpu.make_async_copy(
+                    start.at[l, pl.ds(flip * (NP - HF), HF)], place(l * HF, HF), sem.at[side, l]
+                )
             )
-        )
+            copies.append(
+                pltpu.make_async_copy(
+                    meas.at[l, pl.ds(flip * (NP - HM), HM)], place(4 * HF + l * HM, HM), sem.at[side, 4 + l]
+                )
+            )
     for copy in copies:
         copy.start()
     for copy in copies:
         copy.wait()
-    extra[at + 4 * HM : at + 4 * HM + HF] = ints[...].astype(F32)
+    extra_b[TOTAL - HF - BULK : TOTAL - BULK] = ints[0].astype(F32)
+    side_a[TOTAL - HF : TOTAL] = ints[1].astype(F32)
 
 
 def stages(where, spectra, absorb_t, half_t, lit, step, near, near2, state):
@@ -274,46 +286,51 @@
     odd = lax.rem(gz, 2)
     whole = pl.ds(PAD, N)
 
-    def extras(side, at, high, number):
-        first = 3 + 5 * number
-        return [
+    def incoming(bulk, extra, high, number):
+        def piece(at, count):
+            return bulk.at[pl.ds(at, count)] if at < BULK else extra.at[pl.ds(at - BULK, count)]
+
+        first = 3 + 9 * number
+        lights = [
             pltpu.make_async_copy(
-                side.at[pl.ds(at + 4 * HM, HF)], shared.at[pl.ds(high * HF, HF)], sem.at[first]
-            )
-        ] + [
-            pltpu.make_async_copy(
-                side.at[pl.ds(at + l * HM, HM)], ms.at[l, pl.ds(high * (HM + NP), HM)], sem.at[first + 1 + l]
+                piece(l * HF, HF), fl.at[l, pl.ds(high * (HF + NP), HF), whole], sem.at[first + l]
             )
             for l in range(4)
         ]
-
-    extras_a = extras(side_a, 4 * HF, 1 - odd, 0)
-    extras_b = extras(straight_b, 0, odd, 1)
-    label_copies = [extras_a[0], extras_b[0]]
-    meas_copies = extras_a[1:] + extras_b[1:]
-    fluence_copies = [
-        pltpu.make_async_copy(
-            side.at[pl.ds(l * HF, HF)],
-            fl.at[l, pl.ds(high * (HF + NP), HF), whole],
-            sem.at[13 + 4 * number + l],
+        pressures = [
+            pltpu.make_async_copy(
+                piece(4 * HF + l * HM, HM), ms.at[l, pl.ds(high * (HM + NP), HM)], sem.at[first + 4 + l]
+            )
+            for l in range(4)
+        ]
+        classes = pltpu.make_async_copy(
+            piece(TOTAL - HF, HF), shared.at[pl.ds(high * HF, HF)], sem.at[first + 8]
         )
-        for number, (side, high) in enumerate(((side_a, 1 - odd), (bulk_b, odd)))
-        for l in range(4)
-    ]
+        return lights, pressures, classes
+
+    rest_a = side_a.at[pl.ds(BULK, TOTAL - BULK)]
+    lights_a, pressures_a, classes_a = incoming(side_a, rest_a, 1 - odd, 0)
+    lights_b, pressures_b, classes_b = incoming(bulk_b, straight_b, odd, 1)
+    _, turned_pressures, turned_classes = incoming(bulk_b, turned_b, odd, 1)
+    label_copies = [classes_a, classes_b]
+    meas_copies = pressures_a + pressures_b
+    fluence_copies = lights_a + lights_b
     turned = (lax.rem(gz, 8) == 0) | (lax.rem(gz, 8) == 7)
-    extras_a[0].start()
+    classes_a.start()
 
     @pl.when(turned)
     def _():
-        for copy in extras(turned_b, 0, odd, 1):
+        turned_classes.start()
+        for copy in turned_pressures[2:]:
             copy.start()
 
     @pl.when(jnp.logical_not(turned))
     def _():
-        for copy in extras_b:
+        classes_b.start()
+        for copy in pressures_b[2:]:
             copy.start()
 
-    for copy in fluence_copies + extras_a[1:]:
+    for copy in fluence_copies + pressures_a + pressures_b[:2]:
         copy.start()
 
     lit[...] = illum[...].astype(F32)
@@ -490,7 +507,6 @@
 
 def shards(labels, label_table, spectra, illumination, fluence_start, measured):
     where = jnp.stack([lax.axis_index("gz"), lax.axis_index("wl")]).astype(jnp.int32)
-    odd = lax.rem(where[:1], 2)
     small = pltpu.CompilerParams(vmem_limit_bytes=12 * 2**20)
 
     def in_hbm(x):
@@ -499,19 +515,15 @@
     def in_vmem(x):
         return pltpu.with_memory_space_constraint(x, pltpu.VMEM)
 
-    def pack(high, *planes):
-        return pl.pallas_call(
-            pack_kernel,
-            out_shape=[jax.ShapeDtypeStruct((count, N, N), F32) for count in planes],
-            in_specs=[SMEM] + [ANY] * 3,
-            out_specs=[VMEM] * len(planes),
-            scratch_shapes=[pltpu.VMEM((HF, N, N), jnp.int32), pltpu.SemaphoreType.DMA((9,))],
-            compiler_params=small,
-            name="pack",
-        )(high, *map(in_hbm, (labels, fluence_start, measured)))
-
-    bulk_b, extra_b = pack(odd, 4 * HF, 4 * HM + HF)
-    (side_a,) = pack(1 - odd, 4 * HF + 4 * HM + HF)
+    bulk_b, extra_b, side_a = pl.pallas_call(
+        pack_kernel,
+        out_shape=[pltpu.VMEM((count, N, N), F32) for count in (BULK, TOTAL - BULK, TOTAL)],
+        in_specs=[SMEM] + [ANY] * 3,
+        out_specs=[VMEM] * 3,
+        scratch_shapes=[pltpu.VMEM((2, HF, N, N), jnp.int32), pltpu.SemaphoreType.DMA((2, 9))],
+        compiler_params=small,
+        name="pack",
+    )(where, *map(in_hbm, (labels, fluence_start, measured)))
     bulk_b = lax.ppermute(bulk_b, "gz", OFF_CHIP)
     straight_b = lax.ppermute(extra_b, "gz", AROUND)
     side_a = lax.ppermute(side_a, "gz", ON_CHIP)
@@ -524,7 +536,6 @@
     half_t = 0.5 / (3.0 * (absorb_t + spectra[:, 4, None] * label_table[None, :, 4]))
 
     sizes = [last - first for first, last in PARTS]
-    plane = jax.ShapeDtypeStruct((4, N, N), F32)
     held = (
         [pltpu.VMEM((4, EXT, N + 2 * PAD, N), F32)] * 5
         + [pltpu.VMEM((4, EXT, N, N), F32)] * 5
@@ -548,8 +559,8 @@
     fluence, coef_a, coef_b, edge_a, edge_b, *out = pl.pallas_call(
         solve_kernel,
         out_shape=[jax.ShapeDtypeStruct((4, NP, N, N), F32)]
-        + [plane] * 4
-        + [jax.ShapeDtypeStruct((4, size, ROWS, N), F32) for size in sizes for _ in range(2)]
+        + [pltpu.VMEM((4, N, N), F32)] * 4
+        + [pltpu.VMEM((4, size, ROWS, N), F32) for size in sizes for _ in range(2)]
         + held,
         in_specs=[SMEM] * 4 + [VMEM] + [ANY] * 4 + [VMEM] * 11,
         out_specs=[ANY] + [VMEM] * 21,

time: 137 us -> 137 us (level)
  waiting for transfers between devices: 33.2 us -> 52.4 us
  starting transfers between devices: 59.2 us -> 45.9 us
  Pallas kernels: 39 us -> 35.7 us
  other arithmetic: 3.77 us -> 0.65 us
    ppermute x1, waiting for transfers between devices: 1.93 us -> 14.9 us  [shards(): straight_b = lax.ppermute(extra_b, 'gz', AROUND)]
    ppermute x1, starting transfers between devices: 8.55 us -> 1.3 us  [shards(): turned_b = lax.ppermute(straight_b, 'gz', ALONG)]
    ppermute x2, starting transfers between devices: 6.62 us -> 1.6 us  [beside(): return (lax.ppermute(a, 'gz', ON_CHIP), lax.ppermute(b, 'gz', OFF_CHIP))]
    ppermute x2, waiting for transfers between devices: 0.01 us -> 3.27 us  [beside(): return (lax.ppermute(a, 'gz', ON_CHIP), lax.ppermute(b, 'gz', OFF_CHIP))]
    ppermute x21, waiting for transfers between devices: 24.5 us -> 27.7 us  [swap(): return lax.ppermute(x, 'wl', [(i, i ^ code) for i in range(8)])]
    add x3, other arithmetic: 3.3 us -> 0.17 us  [shards(): keeps = [keeps[q][:half] + recvs[q][:half] for q in range(3)]]
    ppermute x1, starting transfers between devices: 2.94 us -> 0.01 us  [shards(): straight_b = lax.ppermute(extra_b, 'gz', AROUND)]
    ppermute x1, starting transfers between devices: 5.84 us -> 8.6 us  [shards(): bulk_b = lax.ppermute(bulk_b, 'gz', OFF_CHIP)]
  transfers between devices with their start and end apart: 28 -> 28, of which waited for: 10 -> 13; matrix products, arithmetic and copies ran while one was open for 3% -> 1% of each run, Pallas kernels for 9% -> 7%
where the time goes in v5:
time: 137 us; the launch traced here: 136 us
  waiting for transfers between devices  52.4 us (38%)
  starting transfers between devices  45.9 us (34%)
  Pallas kernels  35.7 us (26%)
    ppermute x21, starting transfers between devices, swap(): return lax.ppermute(x, 'wl', [(i, i ^ code) for i in range(8)])  29.6 us
    ppermute x21, waiting for transfers between devices, swap(): return lax.ppermute(x, 'wl', [(i, i ^ code) for i in range(8)])  27.7 us
    pallas_call x1, Pallas kernels, shards(): pl.pallas_call(solve_kernel, out_shape=[jax.ShapeDtypeStruct((4, NP, N, N...  18.9 us
    ppermute x1, waiting for transfers between devices, shards(): straight_b = lax.ppermute(extra_b, 'gz', AROUND)  14.9 us
    pallas_call x1, Pallas kernels, shards(): pl.pallas_call(inner_kernel, out_shape=held, in_specs=[SMEM] * 4 + [ANY]...  9.75 us
    ppermute x1, starting transfers between devices, shards(): bulk_b = lax.ppermute(bulk_b, 'gz', OFF_CHIP)  8.6 us
    all_to_all x1, waiting for transfers between devices, shards(): slab = jnp.sum(lax.all_to_all(sums, 'gz', 0, 0), axis=0)  6.56 us
    all_to_all x1, starting transfers between devices, shards(): slab = jnp.sum(lax.all_to_all(sums, 'gz', 0, 0), axis=0)  4.66 us
  transfers between devices with their start and end apart: 28, of which 13 were waited for; matrix products, arithmetic and copies ran while one was open for 1% of the time, Pallas kernels for 7%

profile of v5, /device:TPU:8, one launch (start us, length us, event | category | flops | bytes accessed | tf_op | source)
XLA Modules:
  0.0 136.3 jit_solution(11796198157959987367)
XLA Ops:
  0.7 2.5 %pack.1 = (f32[14,128,128]{2,1,0:T(8,128)S(1)}, f32[5,128,128]{2,1,0:T(8,128)S(1)}, f32[19,128,128]{2,1,0:T(8,128)S(1)}) custom-call(s32[2]{0:T(128)S(1)} %pad_add_fusion.where, s32[8,128,128]{2,1,0:T(8,128)} %labels.5, f32[4,8,128,128]{3,2,1,0:T(8,128)} %start.3, f32[4,8,128,128]{3,2,1,0:T(8,128)} %meas.3), custom_call_target="tpu_custom_call" | custom-call | tf_op jit(solution)/shard_map/pack/pallas_call | solution.py:518
  3.3 8.6 %collective-permute-start.1 = (f32[14,128,128]{2,1,0:T(8,128)S(1)}, f32[14,128,128]{2,1,0:T(8,128)S(1)}, u32[]{:S(2)}, u32[]{:S(2)}) collective-permute-start(f32[14,128,128]{2,1,0:T(8,128)S(1)} %get-tuple-element.39), channel_id=1, source_target_pairs={{0,31},{1,2},{2,1},{3,4},{4,3},{5,6},{6,5},{7,8},{8,7},{9,10},{10,... | collective-permute-start | bytes 2752520 | tf_op jit(solution)/shard_map/ppermute | solution.py:527
  12.2 14.9 %collective-permute-done.2.straight_b = f32[5,128,128]{2,1,0:T(8,128)S(1)} collective-permute-done((f32[5,128,128]{2,1,0:T(8,128)S(1)}, f32[5,128,128]{2,1,0:T(8,128)S(1)}, u32[]{:S(2)}, u32[]{:S(2)}) %collective-permute-start.2) | collective-permute-done | bytes 327712 | tf_op jit(solution)/shard_map/ppermute | solution.py:528
  28.8 9.7 %inner.1 = (f32[4,14,144,128]{3,2,1,0:T(8,128)S(1)}, f32[4,14,144,128]{3,2,1,0:T(8,128)S(1)}, f32[4,14,144,128]{3,2,1,0:T(8,128)S(1)}, f32[4,14,144,128]{3,2,1,0...) custom-call(s32[2]{0:T(128)S(1)} %pad_add_fusion.where, ...), custom_call_target="tpu_custom_call" | custom-call | tf_op jit(solution)/shard_map/inner/pallas_call | solution.py:550
  38.6 18.9 %solve.1 = (f32[4,8,128,128]{3,2,1,0:T(8,128)}, f32[4,128,128]{2,1,0:T(8,128)S(1)}, f32[4,128,128]{2,1,0:T(8,128)S(1)}, f32[4,128,128]{2,1,0:T(8,128)S(1)}, f32[...) custom-call(s32[2]{0:T(128)} %copy-done.6, ...), custom_call_target="tpu_custom_call", output_to_operand_aliasing={{11}: (9, {}), {12}: (10, {}), {13}: (11, {}), {14}: (12, {... | custom-call | tf_op jit(solution)/shard_map/solve/pallas_call | solution.py:559
  60.8 1.9 %collective-permute-start.6 = (f32[4,14,16,128]{3,2,1,0:T(8,128)S(1)}, f32[4,14,16,128]{3,2,1,0:T(8,128)S(1)}, u32[]{:S(2)}, u32[]{:S(2)}) collective-permute-start(f32[4,14,16,128]{3,2,1,0:T(8,128)S(1)} %get-tuple-element.58), channel_id=1, source_target_pairs={{0,64},{32,96},{64,0},{96,32},{128,192},{160,224},{192,128},{224,1... | collective-permute-start | bytes 1376264 | tf_op jit(solution)/shard_map/ppermute | solution.py:495
  62.7 3.1 %collective-permute-done.7 = f32[4,13,16,128]{3,2,1,0:T(8,128)S(1)} collective-permute-done((f32[4,13,16,128]{3,2,1,0:T(8,128)S(1)}, f32[4,13,16,128]{3,2,1,0:T(8,128)S(1)}, u32[]{:S(2)}, u32[]{:S(2)}) %collective-permute-start.7) | collective-permute-done | bytes 426016 | tf_op jit(solution)/shard_map/ppermute | solution.py:495
  65.8 3.6 %collective-permute-done.8 = f32[4,13,16,128]{3,2,1,0:T(8,128)S(1)} collective-permute-done((f32[4,13,16,128]{3,2,1,0:T(8,128)S(1)}, f32[4,13,16,128]{3,2,1,0:T(8,128)S(1)}, u32[]{:S(2)}, u32[]{:S(2)}) %collective-permute-start.8) | collective-permute-done | bytes 426016 | tf_op jit(solution)/shard_map/ppermute | solution.py:495
  69.5 2.8 %collective-permute-done.6 = f32[4,14,16,128]{3,2,1,0:T(8,128)S(1)} collective-permute-done((f32[4,14,16,128]{3,2,1,0:T(8,128)S(1)}, f32[4,14,16,128]{3,2,1,0:T(8,128)S(1)}, u32[]{:S(2)}, u32[]{:S(2)}) %collective-permute-start.6) | collective-permute-done | bytes 458784 | tf_op jit(solution)/shard_map/ppermute | solution.py:495
  72.4 3.3 %collective-permute-done.5.edge_b = f32[4,128,128]{2,1,0:T(8,128)S(1)} collective-permute-done((f32[4,128,128]{2,1,0:T(8,128)S(1)}, f32[4,128,128]{2,1,0:T(8,128)S(1)}, u32[]{:S(2)}, u32[]{:S(2)}) %collective-permute-start.5) | collective-permute-done | bytes 262176 | tf_op jit(solution)/shard_map/ppermute | solution.py:505
  76.3 2.0 %collective-permute-start.9 = (f32[4,2,16,128]{3,2,1,0:T(8,128)S(1)}, f32[4,2,16,128]{3,2,1,0:T(8,128)S(1)}, u32[]{:S(2)}, u32[]{:S(2)}) collective-permute-start(f32[4,2,16,128]{3,2,1,0:T(8,128)S(1)} %get-tuple-element.66), channel_id=1, source_target_pairs={{0,64},{32,96},{64,0},{96,32},{128,192},{160,224},{192,128},{224,1... | collective-permute-start | bytes 196616 | tf_op jit(solution)/shard_map/ppermute | solution.py:495
  78.8 2.1 %collective-permute-done.9 = f32[4,2,16,128]{3,2,1,0:T(8,128)S(1)} collective-permute-done((f32[4,2,16,128]{3,2,1,0:T(8,128)S(1)}, f32[4,2,16,128]{3,2,1,0:T(8,128)S(1)}, u32[]{:S(2)}, u32[]{:S(2)}) %collective-permute-start.9) | collective-permute-done | bytes 65568 | tf_op jit(solution)/shard_map/ppermute | solution.py:495
  81.2 3.4 %collective-permute-done.13 = f32[2,13,16,128]{3,2,1,0:T(8,128)S(1)} collective-permute-done((f32[2,13,16,128]{3,2,1,0:T(8,128)S(1)}, f32[2,13,16,128]{3,2,1,0:T(8,128)S(1)}, u32[]{:S(2)}, u32[]{:S(2)}) %collective-permute-start.13) | collective-permute-done | bytes 213024 | tf_op jit(solution)/shard_map/ppermute | solution.py:495
  87.9 3.5 %collective-permute-done.11.late_recv = f32[1,2,16,128]{3,2,1,0:T(8,128)S(1)} collective-permute-done((f32[1,2,16,128]{3,2,1,0:T(8,128)S(1)}, f32[1,2,16,128]{3,2,1,0:T(8,128)S(1)}, u32[]{:S(2)}, u32[]{:S(2)}) %collective-permute-start.11) | collective-permute-done | bytes 16416 | tf_op jit(solution)/shard_map/ppermute | solution.py:495
  92.7 4.7 %all-to-all-start = ((f32[32,1,128]{2,1,0:T(1,128)}), f32[32,1,128]{2,1,0:T(1,128)S(1)}, u32[]{:S(2)}, u32[]{:S(2)}) async-start(f32[32,1,128]{2,1,0:T(1,128)} %get-tuple-element.68), calls=%async_computation | async-start | bytes 32768 | tf_op jit(solution)/shard_map/all_to_all | solution.py:617
  97.3 3.1 %collective-permute-start.21 = (f32[1,13,16,128]{3,2,1,0:T(8,128)S(1)}, f32[1,13,16,128]{3,2,1,0:T(8,128)S(1)}, u32[]{:S(2)}, u32[]{:S(2)}) collective-permute-start(f32[1,13,16,128]{3,2,1,0:T(8,128)S(1)} %get-tuple-element.69.refs_4_), channel_id=1, source_target_pairs={{0,64},{32,96},{64,0},{96,32},{128,192},{160,224},{192,128},{224,1... | collective-permute-start | bytes 319496 | tf_op jit(solution)/shard_map/ppermute | solution.py:495
  100.5 6.6 %all-to-all-done = f32[32,1,128]{2,1,0:T(1,128)S(1)} async-done(((f32[32,1,128]{2,1,0:T(1,128)}), f32[32,1,128]{2,1,0:T(1,128)S(1)}, u32[]{:S(2)}, u32[]{:S(2)}) %all-to-all-start) | async-done | bytes 16416 | tf_op jit(solution)/shard_map/all_to_all | solution.py:617
  112.5 2.9 %collective-permute-start.19 = (f32[2,15,16,128]{3,2,1,0:T(8,128)S(1)}, f32[2,15,16,128]{3,2,1,0:T(8,128)S(1)}, u32[]{:S(2)}, u32[]{:S(2)}) collective-permute-start(f32[2,15,16,128]{3,2,1,0:T(8,128)S(1)} %pad_maximum_fusion.3), channel_id=1, source_target_pairs={{0,192},{32,224},{64,128},{96,160},{128,64},{160,96},{192,0},{224,... | collective-permute-start | bytes 737288 | tf_op jit(solution)/shard_map/ppermute | solution.py:495
  115.3 2.1 %collective-permute-start.25 = (f32[2,13,16,128]{3,2,1,0:T(8,128)S(1)}, f32[2,13,16,128]{3,2,1,0:T(8,128)S(1)}, u32[]{:S(2)}, u32[]{:S(2)}) collective-permute-start(f32[2,13,16,128]{3,2,1,0:T(8,128)S(1)} %pad_maximum_fusion.5), channel_id=1, source_target_pairs={{0,64},{32,96},{64,0},{96,32},{128,192},{160,224},{192,128},{224,1... | collective-permute-start | bytes 638984 | tf_op jit(solution)/shard_map/ppermute | solution.py:495
  117.4 2.0 %collective-permute-start.23 = (f32[4,13,16,128]{3,2,1,0:T(8,128)S(1)}, f32[4,13,16,128]{3,2,1,0:T(8,128)S(1)}, u32[]{:S(2)}, u32[]{:S(2)}) collective-permute-start(f32[4,13,16,128]{3,2,1,0:T(8,128)S(1)} %pad_maximum_fusion.1), channel_id=1, source_target_pairs={{0,192},{32,224},{64,128},{96,160},{128,64},{160,96},{192,0},{224,... | collective-permute-start | bytes 1277960 | tf_op jit(solution)/shard_map/ppermute | solution.py:495
  120.3 4.9 %collective-permute-start.20 = (f32[4,15,16,128]{3,2,1,0:T(8,128)S(1)}, f32[4,15,16,128]{3,2,1,0:T(8,128)S(1)}, u32[]{:S(2)}, u32[]{:S(2)}) collective-permute-start(f32[4,15,16,128]{3,2,1,0:T(8,128)S(1)} %pad_maximum_fusion), channel_id=1, source_target_pairs={{0,64},{32,96},{64,0},{96,32},{128,192},{160,224},{192,128},{224,1... | collective-permute-start | bytes 1474568 | tf_op jit(solution)/shard_map/ppermute | solution.py:495
  126.4 2.2 %collective-permute-done.23.refs_7_ = f32[4,13,16,128]{3,2,1,0:T(8,128)S(1)} collective-permute-done((f32[4,13,16,128]{3,2,1,0:T(8,128)S(1)}, f32[4,13,16,128]{3,2,1,0:T(8,128)S(1)}, u32[]{:S(2)}, u32[]{:S(2)}) %collective-permute-start.23) | collective-permute-done | bytes 426016 | tf_op jit(solution)/shard_map/ppermute | solution.py:495
  128.6 4.8 %collective-permute-done.26.refs_11_ = f32[4,13,16,128]{3,2,1,0:T(8,128)S(1)} collective-permute-done((f32[4,13,16,128]{3,2,1,0:T(8,128)S(1)}, f32[4,13,16,128]{3,2,1,0:T(8,128)S(1)}, u32[]{:S(2)}, u32[]{:S(2)}) %collective-permute-start.26) | collective-permute-done | bytes 426016 | tf_op jit(solution)/shard_map/ppermute | solution.py:495
  133.4 2.7 %final.1 = (f32[4,8,128,128]{3,2,1,0:T(8,128)}, f32[8,128,128]{2,1,0:T(8,128)}) custom-call(s32[2]{0:T(128)S(1)} %copy-done.7, f32[8,5]{1,0:T(8,128)S(1)} %copy-done.2, s32[8,128,128]{2,1,0:T(8,128)S(1)} %copy-done, f32[1,15,16,128]{3,2,1,0:T(8,128)S(1)} %pad_maximum_fusion.6.refs_0_, f32[1,15,16,128]{3,2,1,0:T(8,128)S(1)} %collective-permute-done.18.refs_1_, ...), custom_call_target="tpu_custom_call" | custom-call | tf_op jit(solution)/shard_map/final/pallas_call | solution.py:624
  (75 shorter events, 19.1 us)
Async XLA Ops:
  3.2 35.4 %collective-permute-start = (f32[19,128,128]{2,1,0:T(8,128)S(1)}, f32[19,128,128]{2,1,0:T(8,128)S(1)}, u32[]{:S(2)}, u32[]{:S(2)}) collective-permute-start(f32[19,128,128]{2,1,0:T(8,128)S(1)} %get-tuple-element.38), channel_id=1, source_target_pairs={{0,1},{1,0},{2,3},{3,2},{4,5},{5,4},{6,7},{7,6},{8,9},{9,8},{10,11... | collective-permute-start | bytes 3735560 | tf_op jit(solution)/shard_map/ppermute | solution.py:529
  3.3 35.2 %collective-permute-start.1 = (f32[14,128,128]{2,1,0:T(8,128)S(1)}, f32[14,128,128]{2,1,0:T(8,128)S(1)}, u32[]{:S(2)}, u32[]{:S(2)}) collective-permute-start(f32[14,128,128]{2,1,0:T(8,128)S(1)} %get-tuple-element.39), channel_id=1, source_target_pairs={{0,31},{1,2},{2,1},{3,4},{4,3},{5,6},{6,5},{7,8},{8,7},{9,10},{10,... | collective-permute-start | bytes 2752520 | tf_op jit(solution)/shard_map/ppermute | solution.py:527
  11.9 15.2 %collective-permute-start.2 = (f32[5,128,128]{2,1,0:T(8,128)S(1)}, f32[5,128,128]{2,1,0:T(8,128)S(1)}, u32[]{:S(2)}, u32[]{:S(2)}) collective-permute-start(f32[5,128,128]{2,1,0:T(8,128)S(1)} %get-tuple-element.40), channel_id=1, source_target_pairs={{0,7},{1,2},{2,1},{3,4},{4,3},{5,6},{6,5},{7,0},{8,15},{9,10},{10,... | collective-permute-start | bytes 983048 | tf_op jit(solution)/shard_map/ppermute | solution.py:528
  27.1 11.5 %collective-permute-start.3 = (f32[5,128,128]{2,1,0:T(8,128)S(1)}, f32[5,128,128]{2,1,0:T(8,128)S(1)}, u32[]{:S(2)}, u32[]{:S(2)}) collective-permute-start(f32[5,128,128]{2,1,0:T(8,128)S(1)} %collective-permute-done.2.straight_b), channel_id=1, source_target_pairs={{0,8},{8,16},{16,24},{15,7},{23,15},{31,23},{32,40},{40,48},{48,56... | collective-permute-start | bytes 983048 | tf_op jit(solution)/shard_map/ppermute | solution.py:530
  57.5 8.2 %collective-permute-start.7 = (f32[4,13,16,128]{3,2,1,0:T(8,128)S(1)}, f32[4,13,16,128]{3,2,1,0:T(8,128)S(1)}, u32[]{:S(2)}, u32[]{:S(2)}) collective-permute-start(f32[4,13,16,128]{3,2,1,0:T(8,128)S(1)} %get-tuple-element.60), channel_id=1, source_target_pairs={{0,192},{32,224},{64,128},{96,160},{128,64},{160,96},{192,0},{224,... | collective-permute-start | bytes 1277960 | tf_op jit(solution)/shard_map/ppermute | solution.py:495
  59.2 10.2 %collective-permute-start.8 = (f32[4,13,16,128]{3,2,1,0:T(8,128)S(1)}, f32[4,13,16,128]{3,2,1,0:T(8,128)S(1)}, u32[]{:S(2)}, u32[]{:S(2)}) collective-permute-start(f32[4,13,16,128]{3,2,1,0:T(8,128)S(1)} %get-tuple-element.62), channel_id=1, source_target_pairs={{0,32},{32,0},{64,96},{96,64},{128,160},{160,128},{192,224},{224,1... | collective-permute-start | bytes 1277960 | tf_op jit(solution)/shard_map/ppermute | solution.py:495
  59.2 13.1 %collective-permute-start.4 = (f32[4,128,128]{2,1,0:T(8,128)S(1)}, f32[4,128,128]{2,1,0:T(8,128)S(1)}, u32[]{:S(2)}, u32[]{:S(2)}) collective-permute-start(f32[4,128,128]{2,1,0:T(8,128)S(1)} %get-tuple-element.55), channel_id=1, source_target_pairs={{0,1},{1,0},{2,3},{3,2},{4,5},{5,4},{6,7},{7,6},{8,9},{9,8},{10,11... | collective-permute-start | bytes 786440 | tf_op jit(solution)/shard_map/ppermute | solution.py:505
  59.2 16.4 %collective-permute-start.5 = (f32[4,128,128]{2,1,0:T(8,128)S(1)}, f32[4,128,128]{2,1,0:T(8,128)S(1)}, u32[]{:S(2)}, u32[]{:S(2)}) collective-permute-start(f32[4,128,128]{2,1,0:T(8,128)S(1)} %get-tuple-element.56), channel_id=1, source_target_pairs={{0,31},{1,2},{2,1},{3,4},{4,3},{5,6},{6,5},{7,8},{8,7},{9,10},{10,... | collective-permute-start | bytes 786440 | tf_op jit(solution)/shard_map/ppermute | solution.py:505
  60.8 11.5 %collective-permute-start.6 = (f32[4,14,16,128]{3,2,1,0:T(8,128)S(1)}, f32[4,14,16,128]{3,2,1,0:T(8,128)S(1)}, u32[]{:S(2)}, u32[]{:S(2)}) collective-permute-start(f32[4,14,16,128]{3,2,1,0:T(8,128)S(1)} %get-tuple-element.58), channel_id=1, source_target_pairs={{0,64},{32,96},{64,0},{96,32},{128,192},{160,224},{192,128},{224,1... | collective-permute-start | bytes 1376264 | tf_op jit(solution)/shard_map/ppermute | solution.py:495
  78.2 6.4 %collective-permute-start.13 = (f32[2,13,16,128]{3,2,1,0:T(8,128)S(1)}, f32[2,13,16,128]{3,2,1,0:T(8,128)S(1)}, u32[]{:S(2)}, u32[]{:S(2)}) collective-permute-start(f32[2,13,16,128]{3,2,1,0:T(8,128)S(1)} %get-tuple-element.90), channel_id=1, source_target_pairs={{0,32},{32,0},{64,96},{96,64},{128,160},{160,128},{192,224},{224,1... | collective-permute-start | bytes 638984 | tf_op jit(solution)/shard_map/ppermute | solution.py:495
  78.2 6.7 %collective-permute-start.14 = (f32[2,13,16,128]{3,2,1,0:T(8,128)S(1)}, f32[2,13,16,128]{3,2,1,0:T(8,128)S(1)}, u32[]{:S(2)}, u32[]{:S(2)}) collective-permute-start(f32[2,13,16,128]{3,2,1,0:T(8,128)S(1)} %get-tuple-element.88), channel_id=1, source_target_pairs={{0,64},{32,96},{64,0},{96,32},{128,192},{160,224},{192,128},{224,1... | collective-permute-start | bytes 638984 | tf_op jit(solution)/shard_map/ppermute | solution.py:495
  78.4 7.2 %collective-permute-start.12 = (f32[2,14,16,128]{3,2,1,0:T(8,128)S(1)}, f32[2,14,16,128]{3,2,1,0:T(8,128)S(1)}, u32[]{:S(2)}, u32[]{:S(2)}) collective-permute-start(f32[2,14,16,128]{3,2,1,0:T(8,128)S(1)} %get-tuple-element.86), channel_id=1, source_target_pairs={{0,192},{32,224},{64,128},{96,160},{128,64},{160,96},{192,0},{224,... | collective-permute-start | bytes 688136 | tf_op jit(solution)/shard_map/ppermute | solution.py:495
  81.0 6.6 %collective-permute-start.10 = (f32[2,2,16,128]{3,2,1,0:T(8,128)S(1)}, f32[2,2,16,128]{3,2,1,0:T(8,128)S(1)}, u32[]{:S(2)}, u32[]{:S(2)}) collective-permute-start(f32[2,2,16,128]{3,2,1,0:T(8,128)S(1)} %get-tuple-element.98), channel_id=1, source_target_pairs={{0,192},{32,224},{64,128},{96,160},{128,64},{160,96},{192,0},{224,... | collective-permute-start | bytes 98312 | tf_op jit(solution)/shard_map/ppermute | solution.py:495
  84.6 6.8 %collective-permute-start.16 = (f32[1,13,16,128]{3,2,1,0:T(8,128)S(1)}, f32[1,13,16,128]{3,2,1,0:T(8,128)S(1)}, u32[]{:S(2)}, u32[]{:S(2)}) collective-permute-start(f32[1,13,16,128]{3,2,1,0:T(8,128)S(1)} %get-tuple-element.95), channel_id=1, source_target_pairs={{0,64},{32,96},{64,0},{96,32},{128,192},{160,224},{192,128},{224,1... | collective-permute-start | bytes 319496 | tf_op jit(solution)/shard_map/ppermute | solution.py:495
  85.0 6.4 %collective-permute-start.17 = (f32[1,13,16,128]{3,2,1,0:T(8,128)S(1)}, f32[1,13,16,128]{3,2,1,0:T(8,128)S(1)}, u32[]{:S(2)}, u32[]{:S(2)}) collective-permute-start(f32[1,13,16,128]{3,2,1,0:T(8,128)S(1)} %get-tuple-element.93), channel_id=1, source_target_pairs={{0,192},{32,224},{64,128},{96,160},{128,64},{160,96},{192,0},{224,... | collective-permute-start | bytes 319496 | tf_op jit(solution)/shard_map/ppermute | solution.py:495
  92.7 14.4 %all-to-all-start = ((f32[32,1,128]{2,1,0:T(1,128)}), f32[32,1,128]{2,1,0:T(1,128)S(1)}, u32[]{:S(2)}, u32[]{:S(2)}) async-start(f32[32,1,128]{2,1,0:T(1,128)} %get-tuple-element.68), calls=%async_computation | async-start | bytes 32768 | tf_op jit(solution)/shard_map/all_to_all | solution.py:617
  97.3 12.8 %collective-permute-start.21 = (f32[1,13,16,128]{3,2,1,0:T(8,128)S(1)}, f32[1,13,16,128]{3,2,1,0:T(8,128)S(1)}, u32[]{:S(2)}, u32[]{:S(2)}) collective-permute-start(f32[1,13,16,128]{3,2,1,0:T(8,128)S(1)} %get-tuple-element.69.refs_4_), channel_id=1, source_target_pairs={{0,64},{32,96},{64,0},{96,32},{128,192},{160,224},{192,128},{224,1... | collective-permute-start | bytes 319496 | tf_op jit(solution)/shard_map/ppermute | solution.py:495
  108.3 7.1 %collective-permute-start.24 = (f32[1,13,16,128]{3,2,1,0:T(8,128)S(1)}, f32[1,13,16,128]{3,2,1,0:T(8,128)S(1)}, u32[]{:S(2)}, u32[]{:S(2)}) collective-permute-start(f32[1,13,16,128]{3,2,1,0:T(8,128)S(1)} %get-tuple-element.70.refs_8_), channel_id=1, source_target_pairs={{0,192},{32,224},{64,128},{96,160},{128,64},{160,96},{192,0},{224,... | collective-permute-start | bytes 319496 | tf_op jit(solution)/shard_map/ppermute | solution.py:495
  110.1 7.3 %collective-permute-start.22 = (f32[2,13,16,128]{3,2,1,0:T(8,128)S(1)}, f32[2,13,16,128]{3,2,1,0:T(8,128)S(1)}, u32[]{:S(2)}, u32[]{:S(2)}) collective-permute-start(f32[2,13,16,128]{3,2,1,0:T(8,128)S(1)} %pad_maximum_fusion.4), channel_id=1, source_target_pairs={{0,32},{32,0},{64,96},{96,64},{128,160},{160,128},{192,224},{224,1... | collective-permute-start | bytes 638984 | tf_op jit(solution)/shard_map/ppermute | solution.py:495
  112.5 7.8 %collective-permute-start.19 = (f32[2,15,16,128]{3,2,1,0:T(8,128)S(1)}, f32[2,15,16,128]{3,2,1,0:T(8,128)S(1)}, u32[]{:S(2)}, u32[]{:S(2)}) collective-permute-start(f32[2,15,16,128]{3,2,1,0:T(8,128)S(1)} %pad_maximum_fusion.3), channel_id=1, source_target_pairs={{0,192},{32,224},{64,128},{96,160},{128,64},{160,96},{192,0},{224,... | collective-permute-start | bytes 737288 | tf_op jit(solution)/shard_map/ppermute | solution.py:495
  115.3 9.8 %collective-permute-start.25 = (f32[2,13,16,128]{3,2,1,0:T(8,128)S(1)}, f32[2,13,16,128]{3,2,1,0:T(8,128)S(1)}, u32[]{:S(2)}, u32[]{:S(2)}) collective-permute-start(f32[2,13,16,128]{3,2,1,0:T(8,128)S(1)} %pad_maximum_fusion.5), channel_id=1, source_target_pairs={{0,64},{32,96},{64,0},{96,32},{128,192},{160,224},{192,128},{224,1... | collective-permute-start | bytes 638984 | tf_op jit(solution)/shard_map/ppermute | solution.py:495
  117.4 11.2 %collective-permute-start.23 = (f32[4,13,16,128]{3,2,1,0:T(8,128)S(1)}, f32[4,13,16,128]{3,2,1,0:T(8,128)S(1)}, u32[]{:S(2)}, u32[]{:S(2)}) collective-permute-start(f32[4,13,16,128]{3,2,1,0:T(8,128)S(1)} %pad_maximum_fusion.1), channel_id=1, source_target_pairs={{0,192},{32,224},{64,128},{96,160},{128,64},{160,96},{192,0},{224,... | collective-permute-start | bytes 1277960 | tf_op jit(solution)/shard_map/ppermute | solution.py:495
  120.3 13.1 %collective-permute-start.20 = (f32[4,15,16,128]{3,2,1,0:T(8,128)S(1)}, f32[4,15,16,128]{3,2,1,0:T(8,128)S(1)}, u32[]{:S(2)}, u32[]{:S(2)}) collective-permute-start(f32[4,15,16,128]{3,2,1,0:T(8,128)S(1)} %pad_maximum_fusion), channel_id=1, source_target_pairs={{0,64},{32,96},{64,0},{96,32},{128,192},{160,224},{192,128},{224,1... | collective-permute-start | bytes 1474568 | tf_op jit(solution)/shard_map/ppermute | solution.py:495
  125.2 8.2 %collective-permute-start.26 = (f32[4,13,16,128]{3,2,1,0:T(8,128)S(1)}, f32[4,13,16,128]{3,2,1,0:T(8,128)S(1)}, u32[]{:S(2)}, u32[]{:S(2)}) collective-permute-start(f32[4,13,16,128]{3,2,1,0:T(8,128)S(1)} %pad_maximum_fusion.2), channel_id=1, source_target_pairs={{0,32},{32,0},{64,96},{96,64},{128,160},{160,128},{192,224},{224,1... | collective-permute-start | bytes 1277960 | tf_op jit(solution)/shard_map/ppermute | solution.py:495
  (12 other events, 219.5 us)

commit v6 on v5

--- a/solution.py
+++ b/solution.py
@@ -445,6 +445,14 @@
         row = jnp.where(lane == field, whole, row)
     for target in range(32):
         sums[target] = row
+
+
+def share_kernel(own, sums, out):
+    out[0, 0 : PARTS[0][1]] = own[0]
+    slab = sums[0]
+    for source in range(1, 32):
+        slab = slab + sums[source]
+    out[0, PARTS[0][1]] = jnp.broadcast_to(slab, (ROWS, N))
 
 
 def final_kernel(where, table, labels, *refs):
@@ -614,8 +622,15 @@
             have = steps[q]
             mine = have[0] if len(have) == 1 else jnp.concatenate(have)
             have.append(swap(mine, GENS[ORDERS[q][phase]]))
-    slab = jnp.sum(lax.all_to_all(sums, "gz", 0, 0), axis=0)
-    steps[0] = [jnp.concatenate([owns[0], jnp.broadcast_to(slab[None, None], (1, 1, ROWS, N))], axis=1)]
+    shared = pl.pallas_call(
+        share_kernel,
+        out_shape=jax.ShapeDtypeStruct((1, sizes[0] + 1, ROWS, N), F32),
+        in_specs=[VMEM] * 2,
+        out_specs=VMEM,
+        compiler_params=small,
+        name="share",
+    )(owns[0], lax.all_to_all(sums, "gz", 0, 0))
+    steps[0] = [shared]
     for phase in (2, 1, 0):
         have = steps[0]
         mine = have[0] if len(have) == 1 else jnp.concatenate(have)

time: 137 us -> 136 us (level)
  starting transfers between devices: 45.9 us -> 28.6 us
  blocking collectives: 0 us -> 14.8 us
  waiting for transfers between devices: 52.4 us -> 54.5 us
    all_to_all x0 -> x1, blocking collectives: none -> 14.8 us  [shards(): lax.all_to_all(sums, 'gz', 0, 0)]
    ppermute x21, starting transfers between devices: 29.6 us -> 17 us  [swap(): return lax.ppermute(x, 'wl', [(i, i ^ code) for i in range(8)])]
    ppermute x21, waiting for transfers between devices: 27.7 us -> 36.3 us  [swap(): return lax.ppermute(x, 'wl', [(i, i ^ code) for i in range(8)])]
    all_to_all x1 -> x0, waiting for transfers between devices: 6.56 us -> none  [shards(): slab = jnp.sum(lax.all_to_all(sums, 'gz', 0, 0), axis=0)]
    all_to_all x1 -> x0, starting transfers between devices: 4.66 us -> none  [shards(): slab = jnp.sum(lax.all_to_all(sums, 'gz', 0, 0), axis=0)]
  transfers between devices with their start and end apart: 28 -> 27, of which waited for: 13 -> 14; matrix products, arithmetic and copies ran while one was open for 1% -> 1% of each run, Pallas kernels for 7% -> 7%
where the time goes in v6:
time: 136 us; the launch traced here: 135 us
  waiting for transfers between devices  54.5 us (40%)
  Pallas kernels  35.1 us (26%)
  starting transfers between devices  28.6 us (21%)
  blocking collectives  14.8 us (11%)
    ppermute x21, waiting for transfers between devices, swap(): return lax.ppermute(x, 'wl', [(i, i ^ code) for i in range(8)])  36.3 us
    pallas_call x1, Pallas kernels, shards(): pl.pallas_call(solve_kernel, out_shape=[jax.ShapeDtypeStruct((4, NP, N, N...  18.9 us
    ppermute x21, starting transfers between devices, swap(): return lax.ppermute(x, 'wl', [(i, i ^ code) for i in range(8)])  17 us
    ppermute x1, waiting for transfers between devices, shards(): straight_b = lax.ppermute(extra_b, 'gz', AROUND)  14.9 us
    all_to_all x1, blocking collectives, shards(): lax.all_to_all(sums, 'gz', 0, 0)  14.8 us
    pallas_call x1, Pallas kernels, shards(): pl.pallas_call(inner_kernel, out_shape=held, in_specs=[SMEM] * 4 + [ANY]...  9.75 us
    ppermute x1, starting transfers between devices, shards(): bulk_b = lax.ppermute(bulk_b, 'gz', OFF_CHIP)  8.6 us
    ppermute x2, waiting for transfers between devices, beside(): return (lax.ppermute(a, 'gz', ON_CHIP), lax.ppermute(b, 'gz', OFF_CHIP))  3.27 us
  transfers between devices with their start and end apart: 27, of which 14 were waited for; matrix products, arithmetic and copies ran while one was open for 1% of the time, Pallas kernels for 7%

profile of v6, /device:TPU:8, one launch (start us, length us, event | category | flops | bytes accessed | tf_op | source)
XLA Modules:
  0.0 135.2 jit_solution(12830791690236719000)
XLA Ops:
  0.7 2.5 %pack.1 = (f32[14,128,128]{2,1,0:T(8,128)S(1)}, f32[5,128,128]{2,1,0:T(8,128)S(1)}, f32[19,128,128]{2,1,0:T(8,128)S(1)}) custom-call(s32[2]{0:T(128)S(1)} %pad_add_fusion.where, s32[8,128,128]{2,1,0:T(8,128)} %labels.5, f32[4,8,128,128]{3,2,1,0:T(8,128)} %start.3, f32[4,8,128,128]{3,2,1,0:T(8,128)} %meas.3), custom_call_target="tpu_custom_call" | custom-call | tf_op jit(solution)/shard_map/pack/pallas_call | solution.py:526
  3.3 8.6 %collective-permute-start.1 = (f32[14,128,128]{2,1,0:T(8,128)S(1)}, f32[14,128,128]{2,1,0:T(8,128)S(1)}, u32[]{:S(2)}, u32[]{:S(2)}) collective-permute-start(f32[14,128,128]{2,1,0:T(8,128)S(1)} %get-tuple-element.39), channel_id=1, source_target_pairs={{0,31},{1,2},{2,1},{3,4},{4,3},{5,6},{6,5},{7,8},{8,7},{9,10},{10,... | collective-permute-start | bytes 2752520 | tf_op jit(solution)/shard_map/ppermute | solution.py:535
  12.2 14.9 %collective-permute-done.2.straight_b = f32[5,128,128]{2,1,0:T(8,128)S(1)} collective-permute-done((f32[5,128,128]{2,1,0:T(8,128)S(1)}, f32[5,128,128]{2,1,0:T(8,128)S(1)}, u32[]{:S(2)}, u32[]{:S(2)}) %collective-permute-start.2) | collective-permute-done | bytes 327712 | tf_op jit(solution)/shard_map/ppermute | solution.py:536
  28.8 9.7 %inner.1 = (f32[4,14,144,128]{3,2,1,0:T(8,128)S(1)}, f32[4,14,144,128]{3,2,1,0:T(8,128)S(1)}, f32[4,14,144,128]{3,2,1,0:T(8,128)S(1)}, f32[4,14,144,128]{3,2,1,0...) custom-call(s32[2]{0:T(128)S(1)} %pad_add_fusion.where, ...), custom_call_target="tpu_custom_call" | custom-call | tf_op jit(solution)/shard_map/inner/pallas_call | solution.py:558
  38.6 18.9 %solve.1 = (f32[4,8,128,128]{3,2,1,0:T(8,128)}, f32[4,128,128]{2,1,0:T(8,128)S(1)}, f32[4,128,128]{2,1,0:T(8,128)S(1)}, f32[4,128,128]{2,1,0:T(8,128)S(1)}, f32[...) custom-call(s32[2]{0:T(128)} %copy-done.6, ...), custom_call_target="tpu_custom_call", output_to_operand_aliasing={{11}: (9, {}), {12}: (10, {}), {13}: (11, {}), {14}: (12, {... | custom-call | tf_op jit(solution)/shard_map/solve/pallas_call | solution.py:567
  57.5 1.7 %collective-permute-start.7 = (f32[4,13,16,128]{3,2,1,0:T(8,128)S(1)}, f32[4,13,16,128]{3,2,1,0:T(8,128)S(1)}, u32[]{:S(2)}, u32[]{:S(2)}) collective-permute-start(f32[4,13,16,128]{3,2,1,0:T(8,128)S(1)} %get-tuple-element.60), channel_id=1, source_target_pairs={{0,192},{32,224},{64,128},{96,160},{128,64},{160,96},{192,0},{224,... | collective-permute-start | bytes 1277960 | tf_op jit(solution)/shard_map/ppermute | solution.py:503
  59.2 1.6 %collective-permute-start.5 = (f32[4,128,128]{2,1,0:T(8,128)S(1)}, f32[4,128,128]{2,1,0:T(8,128)S(1)}, u32[]{:S(2)}, u32[]{:S(2)}) collective-permute-start(f32[4,128,128]{2,1,0:T(8,128)S(1)} %get-tuple-element.56), channel_id=1, source_target_pairs={{0,31},{1,2},{2,1},{3,4},{4,3},{5,6},{6,5},{7,8},{8,7},{9,10},{10,... | collective-permute-start | bytes 786440 | tf_op jit(solution)/shard_map/ppermute | solution.py:513
  60.8 1.9 %collective-permute-start.6 = (f32[4,14,16,128]{3,2,1,0:T(8,128)S(1)}, f32[4,14,16,128]{3,2,1,0:T(8,128)S(1)}, u32[]{:S(2)}, u32[]{:S(2)}) collective-permute-start(f32[4,14,16,128]{3,2,1,0:T(8,128)S(1)} %get-tuple-element.58), channel_id=1, source_target_pairs={{0,64},{32,96},{64,0},{96,32},{128,192},{160,224},{192,128},{224,1... | collective-permute-start | bytes 1376264 | tf_op jit(solution)/shard_map/ppermute | solution.py:503
  62.7 3.1 %collective-permute-done.7 = f32[4,13,16,128]{3,2,1,0:T(8,128)S(1)} collective-permute-done((f32[4,13,16,128]{3,2,1,0:T(8,128)S(1)}, f32[4,13,16,128]{3,2,1,0:T(8,128)S(1)}, u32[]{:S(2)}, u32[]{:S(2)}) %collective-permute-start.7) | collective-permute-done | bytes 426016 | tf_op jit(solution)/shard_map/ppermute | solution.py:503
  65.8 3.6 %collective-permute-done.8 = f32[4,13,16,128]{3,2,1,0:T(8,128)S(1)} collective-permute-done((f32[4,13,16,128]{3,2,1,0:T(8,128)S(1)}, f32[4,13,16,128]{3,2,1,0:T(8,128)S(1)}, u32[]{:S(2)}, u32[]{:S(2)}) %collective-permute-start.8) | collective-permute-done | bytes 426016 | tf_op jit(solution)/shard_map/ppermute | solution.py:503
  69.5 2.8 %collective-permute-done.6 = f32[4,14,16,128]{3,2,1,0:T(8,128)S(1)} collective-permute-done((f32[4,14,16,128]{3,2,1,0:T(8,128)S(1)}, f32[4,14,16,128]{3,2,1,0:T(8,128)S(1)}, u32[]{:S(2)}, u32[]{:S(2)}) %collective-permute-start.6) | collective-permute-done | bytes 458784 | tf_op jit(solution)/shard_map/ppermute | solution.py:503
  72.4 3.3 %collective-permute-done.5.edge_b = f32[4,128,128]{2,1,0:T(8,128)S(1)} collective-permute-done((f32[4,128,128]{2,1,0:T(8,128)S(1)}, f32[4,128,128]{2,1,0:T(8,128)S(1)}, u32[]{:S(2)}, u32[]{:S(2)}) %collective-permute-start.5) | collective-permute-done | bytes 262176 | tf_op jit(solution)/shard_map/ppermute | solution.py:513
  76.3 2.0 %collective-permute-start.9 = (f32[4,2,16,128]{3,2,1,0:T(8,128)S(1)}, f32[4,2,16,128]{3,2,1,0:T(8,128)S(1)}, u32[]{:S(2)}, u32[]{:S(2)}) collective-permute-start(f32[4,2,16,128]{3,2,1,0:T(8,128)S(1)} %get-tuple-element.66), channel_id=1, source_target_pairs={{0,64},{32,96},{64,0},{96,32},{128,192},{160,224},{192,128},{224,1... | collective-permute-start | bytes 196616 | tf_op jit(solution)/shard_map/ppermute | solution.py:503
  78.8 2.1 %collective-permute-done.9 = f32[4,2,16,128]{3,2,1,0:T(8,128)S(1)} collective-permute-done((f32[4,2,16,128]{3,2,1,0:T(8,128)S(1)}, f32[4,2,16,128]{3,2,1,0:T(8,128)S(1)}, u32[]{:S(2)}, u32[]{:S(2)}) %collective-permute-start.9) | collective-permute-done | bytes 65568 | tf_op jit(solution)/shard_map/ppermute | solution.py:503
  81.2 3.4 %collective-permute-done.13 = f32[2,13,16,128]{3,2,1,0:T(8,128)S(1)} collective-permute-done((f32[2,13,16,128]{3,2,1,0:T(8,128)S(1)}, f32[2,13,16,128]{3,2,1,0:T(8,128)S(1)}, u32[]{:S(2)}, u32[]{:S(2)}) %collective-permute-start.13) | collective-permute-done | bytes 213024 | tf_op jit(solution)/shard_map/ppermute | solution.py:503
  85.7 1.8 %collective-permute-start.15 = (f32[1,14,16,128]{3,2,1,0:T(8,128)S(1)}, f32[1,14,16,128]{3,2,1,0:T(8,128)S(1)}, u32[]{:S(2)}, u32[]{:S(2)}) collective-permute-start(f32[1,14,16,128]{3,2,1,0:T(8,128)S(1)} %get-tuple-element.91), channel_id=1, source_target_pairs={{0,32},{32,0},{64,96},{96,64},{128,160},{160,128},{192,224},{224,1... | collective-permute-start | bytes 344072 | tf_op jit(solution)/shard_map/ppermute | solution.py:503
  87.9 3.5 %collective-permute-done.11.late_recv = f32[1,2,16,128]{3,2,1,0:T(8,128)S(1)} collective-permute-done((f32[1,2,16,128]{3,2,1,0:T(8,128)S(1)}, f32[1,2,16,128]{3,2,1,0:T(8,128)S(1)}, u32[]{:S(2)}, u32[]{:S(2)}) %collective-permute-start.11) | collective-permute-done | bytes 16416 | tf_op jit(solution)/shard_map/ppermute | solution.py:503
  92.1 2.6 %collective-permute-start.21 = (f32[1,13,16,128]{3,2,1,0:T(8,128)S(1)}, f32[1,13,16,128]{3,2,1,0:T(8,128)S(1)}, u32[]{:S(2)}, u32[]{:S(2)}) collective-permute-start(f32[1,13,16,128]{3,2,1,0:T(8,128)S(1)} %get-tuple-element.69.refs_4_), channel_id=1, source_target_pairs={{0,64},{32,96},{64,0},{96,32},{128,192},{160,224},{192,128},{224,1... | collective-permute-start | bytes 319496 | tf_op jit(solution)/shard_map/ppermute | solution.py:503
  94.7 14.8 %all_to_all.5.sums = f32[32,1,128]{2,1,0:T(1,128)S(1)} all-to-all(f32[32,1,128]{2,1,0:T(1,128)S(1)} %get-tuple-element.68), channel_id=1, replica_groups=mesh['wl'=8,'gz'=32] {'gz'}, dimensions={0} | all-to-all | bytes 32768 | tf_op jit(solution)/shard_map/all_to_all | solution.py:632
  111.7 4.1 %collective-permute-done.18.refs_1_ = f32[1,15,16,128]{3,2,1,0:T(8,128)S(1)} collective-permute-done((f32[1,15,16,128]{3,2,1,0:T(8,128)S(1)}, f32[1,15,16,128]{3,2,1,0:T(8,128)S(1)}, u32[]{:S(2)}, u32[]{:S(2)}) %collective-permute-start.18) | collective-permute-done | bytes 122912 | tf_op jit(solution)/shard_map/ppermute | solution.py:503
  116.7 2.5 %collective-permute-done.22.refs_6_ = f32[2,13,16,128]{3,2,1,0:T(8,128)S(1)} collective-permute-done((f32[2,13,16,128]{3,2,1,0:T(8,128)S(1)}, f32[2,13,16,128]{3,2,1,0:T(8,128)S(1)}, u32[]{:S(2)}, u32[]{:S(2)}) %collective-permute-start.22) | collective-permute-done | bytes 213024 | tf_op jit(solution)/shard_map/ppermute | solution.py:503
  119.4 3.7 %collective-permute-done.19.refs_2_ = f32[2,15,16,128]{3,2,1,0:T(8,128)S(1)} collective-permute-done((f32[2,15,16,128]{3,2,1,0:T(8,128)S(1)}, f32[2,15,16,128]{3,2,1,0:T(8,128)S(1)}, u32[]{:S(2)}, u32[]{:S(2)}) %collective-permute-start.19) | collective-permute-done | bytes 245792 | tf_op jit(solution)/shard_map/ppermute | solution.py:503
  125.0 6.2 %collective-permute-done.23.refs_7_ = f32[4,13,16,128]{3,2,1,0:T(8,128)S(1)} collective-permute-done((f32[4,13,16,128]{3,2,1,0:T(8,128)S(1)}, f32[4,13,16,128]{3,2,1,0:T(8,128)S(1)}, u32[]{:S(2)}, u32[]{:S(2)}) %collective-permute-start.23) | collective-permute-done | bytes 426016 | tf_op jit(solution)/shard_map/ppermute | solution.py:503
  132.4 2.7 %final.1 = (f32[4,8,128,128]{3,2,1,0:T(8,128)}, f32[8,128,128]{2,1,0:T(8,128)}) custom-call(s32[2]{0:T(128)S(1)} %copy-done.7, f32[8,5]{1,0:T(8,128)S(1)} %copy-done.2, s32[8,128,128]{2,1,0:T(8,128)S(1)} %copy-done, f32[1,15,16,128]{3,2,1,0:T(8,128)S(1)} %share.1.refs_0_, f32[1,15,16,128]{3,2,1,0:T(8,128)S(1)} %collective-permute-done.18.refs_1_, ...), custom_call_target="tpu_custom_call" | custom-call | tf_op jit(solution)/shard_map/final/pallas_call | solution.py:639
  (72 shorter events, 12.2 us)
Async XLA Ops:
  3.2 35.4 %collective-permute-start = (f32[19,128,128]{2,1,0:T(8,128)S(1)}, f32[19,128,128]{2,1,0:T(8,128)S(1)}, u32[]{:S(2)}, u32[]{:S(2)}) collective-permute-start(f32[19,128,128]{2,1,0:T(8,128)S(1)} %get-tuple-element.38), channel_id=1, source_target_pairs={{0,1},{1,0},{2,3},{3,2},{4,5},{5,4},{6,7},{7,6},{8,9},{9,8},{10,11... | collective-permute-start | bytes 3735560 | tf_op jit(solution)/shard_map/ppermute | solution.py:537
  3.3 35.2 %collective-permute-start.1 = (f32[14,128,128]{2,1,0:T(8,128)S(1)}, f32[14,128,128]{2,1,0:T(8,128)S(1)}, u32[]{:S(2)}, u32[]{:S(2)}) collective-permute-start(f32[14,128,128]{2,1,0:T(8,128)S(1)} %get-tuple-element.39), channel_id=1, source_target_pairs={{0,31},{1,2},{2,1},{3,4},{4,3},{5,6},{6,5},{7,8},{8,7},{9,10},{10,... | collective-permute-start | bytes 2752520 | tf_op jit(solution)/shard_map/ppermute | solution.py:535
  11.9 15.2 %collective-permute-start.2 = (f32[5,128,128]{2,1,0:T(8,128)S(1)}, f32[5,128,128]{2,1,0:T(8,128)S(1)}, u32[]{:S(2)}, u32[]{:S(2)}) collective-permute-start(f32[5,128,128]{2,1,0:T(8,128)S(1)} %get-tuple-element.40), channel_id=1, source_target_pairs={{0,7},{1,2},{2,1},{3,4},{4,3},{5,6},{6,5},{7,0},{8,15},{9,10},{10,... | collective-permute-start | bytes 983048 | tf_op jit(solution)/shard_map/ppermute | solution.py:536
  27.1 11.5 %collective-permute-start.3 = (f32[5,128,128]{2,1,0:T(8,128)S(1)}, f32[5,128,128]{2,1,0:T(8,128)S(1)}, u32[]{:S(2)}, u32[]{:S(2)}) collective-permute-start(f32[5,128,128]{2,1,0:T(8,128)S(1)} %collective-permute-done.2.straight_b), channel_id=1, source_target_pairs={{0,8},{8,16},{16,24},{15,7},{23,15},{31,23},{32,40},{40,48},{48,56... | collective-permute-start | bytes 983048 | tf_op jit(solution)/shard_map/ppermute | solution.py:538
  57.5 8.2 %collective-permute-start.7 = (f32[4,13,16,128]{3,2,1,0:T(8,128)S(1)}, f32[4,13,16,128]{3,2,1,0:T(8,128)S(1)}, u32[]{:S(2)}, u32[]{:S(2)}) collective-permute-start(f32[4,13,16,128]{3,2,1,0:T(8,128)S(1)} %get-tuple-element.60), channel_id=1, source_target_pairs={{0,192},{32,224},{64,128},{96,160},{128,64},{160,96},{192,0},{224,... | collective-permute-start | bytes 1277960 | tf_op jit(solution)/shard_map/ppermute | solution.py:503
  59.2 10.2 %collective-permute-start.8 = (f32[4,13,16,128]{3,2,1,0:T(8,128)S(1)}, f32[4,13,16,128]{3,2,1,0:T(8,128)S(1)}, u32[]{:S(2)}, u32[]{:S(2)}) collective-permute-start(f32[4,13,16,128]{3,2,1,0:T(8,128)S(1)} %get-tuple-element.62), channel_id=1, source_target_pairs={{0,32},{32,0},{64,96},{96,64},{128,160},{160,128},{192,224},{224,1... | collective-permute-start | bytes 1277960 | tf_op jit(solution)/shard_map/ppermute | solution.py:503
  59.2 13.1 %collective-permute-start.4 = (f32[4,128,128]{2,1,0:T(8,128)S(1)}, f32[4,128,128]{2,1,0:T(8,128)S(1)}, u32[]{:S(2)}, u32[]{:S(2)}) collective-permute-start(f32[4,128,128]{2,1,0:T(8,128)S(1)} %get-tuple-element.55), channel_id=1, source_target_pairs={{0,1},{1,0},{2,3},{3,2},{4,5},{5,4},{6,7},{7,6},{8,9},{9,8},{10,11... | collective-permute-start | bytes 786440 | tf_op jit(solution)/shard_map/ppermute | solution.py:513
  59.2 16.4 %collective-permute-start.5 = (f32[4,128,128]{2,1,0:T(8,128)S(1)}, f32[4,128,128]{2,1,0:T(8,128)S(1)}, u32[]{:S(2)}, u32[]{:S(2)}) collective-permute-start(f32[4,128,128]{2,1,0:T(8,128)S(1)} %get-tuple-element.56), channel_id=1, source_target_pairs={{0,31},{1,2},{2,1},{3,4},{4,3},{5,6},{6,5},{7,8},{8,7},{9,10},{10,... | collective-permute-start | bytes 786440 | tf_op jit(solution)/shard_map/ppermute | solution.py:513
  60.8 11.5 %collective-permute-start.6 = (f32[4,14,16,128]{3,2,1,0:T(8,128)S(1)}, f32[4,14,16,128]{3,2,1,0:T(8,128)S(1)}, u32[]{:S(2)}, u32[]{:S(2)}) collective-permute-start(f32[4,14,16,128]{3,2,1,0:T(8,128)S(1)} %get-tuple-element.58), channel_id=1, source_target_pairs={{0,64},{32,96},{64,0},{96,32},{128,192},{160,224},{192,128},{224,1... | collective-permute-start | bytes 1376264 | tf_op jit(solution)/shard_map/ppermute | solution.py:503
  78.2 6.4 %collective-permute-start.13 = (f32[2,13,16,128]{3,2,1,0:T(8,128)S(1)}, f32[2,13,16,128]{3,2,1,0:T(8,128)S(1)}, u32[]{:S(2)}, u32[]{:S(2)}) collective-permute-start(f32[2,13,16,128]{3,2,1,0:T(8,128)S(1)} %get-tuple-element.90), channel_id=1, source_target_pairs={{0,32},{32,0},{64,96},{96,64},{128,160},{160,128},{192,224},{224,1... | collective-permute-start | bytes 638984 | tf_op jit(solution)/shard_map/ppermute | solution.py:503
  78.2 6.7 %collective-permute-start.14 = (f32[2,13,16,128]{3,2,1,0:T(8,128)S(1)}, f32[2,13,16,128]{3,2,1,0:T(8,128)S(1)}, u32[]{:S(2)}, u32[]{:S(2)}) collective-permute-start(f32[2,13,16,128]{3,2,1,0:T(8,128)S(1)} %get-tuple-element.88), channel_id=1, source_target_pairs={{0,64},{32,96},{64,0},{96,32},{128,192},{160,224},{192,128},{224,1... | collective-permute-start | bytes 638984 | tf_op jit(solution)/shard_map/ppermute | solution.py:503
  78.4 7.2 %collective-permute-start.12 = (f32[2,14,16,128]{3,2,1,0:T(8,128)S(1)}, f32[2,14,16,128]{3,2,1,0:T(8,128)S(1)}, u32[]{:S(2)}, u32[]{:S(2)}) collective-permute-start(f32[2,14,16,128]{3,2,1,0:T(8,128)S(1)} %get-tuple-element.86), channel_id=1, source_target_pairs={{0,192},{32,224},{64,128},{96,160},{128,64},{160,96},{192,0},{224,... | collective-permute-start | bytes 688136 | tf_op jit(solution)/shard_map/ppermute | solution.py:503
  81.0 6.6 %collective-permute-start.10 = (f32[2,2,16,128]{3,2,1,0:T(8,128)S(1)}, f32[2,2,16,128]{3,2,1,0:T(8,128)S(1)}, u32[]{:S(2)}, u32[]{:S(2)}) collective-permute-start(f32[2,2,16,128]{3,2,1,0:T(8,128)S(1)} %get-tuple-element.98), channel_id=1, source_target_pairs={{0,192},{32,224},{64,128},{96,160},{128,64},{160,96},{192,0},{224,... | collective-permute-start | bytes 98312 | tf_op jit(solution)/shard_map/ppermute | solution.py:503
  84.6 6.8 %collective-permute-start.16 = (f32[1,13,16,128]{3,2,1,0:T(8,128)S(1)}, f32[1,13,16,128]{3,2,1,0:T(8,128)S(1)}, u32[]{:S(2)}, u32[]{:S(2)}) collective-permute-start(f32[1,13,16,128]{3,2,1,0:T(8,128)S(1)} %get-tuple-element.95), channel_id=1, source_target_pairs={{0,64},{32,96},{64,0},{96,32},{128,192},{160,224},{192,128},{224,1... | collective-permute-start | bytes 319496 | tf_op jit(solution)/shard_map/ppermute | solution.py:503
  84.9 6.4 %collective-permute-start.17 = (f32[1,13,16,128]{3,2,1,0:T(8,128)S(1)}, f32[1,13,16,128]{3,2,1,0:T(8,128)S(1)}, u32[]{:S(2)}, u32[]{:S(2)}) collective-permute-start(f32[1,13,16,128]{3,2,1,0:T(8,128)S(1)} %get-tuple-element.93), channel_id=1, source_target_pairs={{0,192},{32,224},{64,128},{96,160},{128,64},{160,96},{192,0},{224,... | collective-permute-start | bytes 319496 | tf_op jit(solution)/shard_map/ppermute | solution.py:503
  85.7 5.7 %collective-permute-start.15 = (f32[1,14,16,128]{3,2,1,0:T(8,128)S(1)}, f32[1,14,16,128]{3,2,1,0:T(8,128)S(1)}, u32[]{:S(2)}, u32[]{:S(2)}) collective-permute-start(f32[1,14,16,128]{3,2,1,0:T(8,128)S(1)} %get-tuple-element.91), channel_id=1, source_target_pairs={{0,32},{32,0},{64,96},{96,64},{128,160},{160,128},{192,224},{224,1... | collective-permute-start | bytes 344072 | tf_op jit(solution)/shard_map/ppermute | solution.py:503
  92.1 18.6 %collective-permute-start.21 = (f32[1,13,16,128]{3,2,1,0:T(8,128)S(1)}, f32[1,13,16,128]{3,2,1,0:T(8,128)S(1)}, u32[]{:S(2)}, u32[]{:S(2)}) collective-permute-start(f32[1,13,16,128]{3,2,1,0:T(8,128)S(1)} %get-tuple-element.69.refs_4_), channel_id=1, source_target_pairs={{0,64},{32,96},{64,0},{96,32},{128,192},{160,224},{192,128},{224,1... | collective-permute-start | bytes 319496 | tf_op jit(solution)/shard_map/ppermute | solution.py:503
  109.5 6.3 %collective-permute-start.18 = (f32[1,15,16,128]{3,2,1,0:T(8,128)S(1)}, f32[1,15,16,128]{3,2,1,0:T(8,128)S(1)}, u32[]{:S(2)}, u32[]{:S(2)}) collective-permute-start(f32[1,15,16,128]{3,2,1,0:T(8,128)S(1)} %share.1.refs_0_), channel_id=1, source_target_pairs={{0,32},{32,0},{64,96},{96,64},{128,160},{160,128},{192,224},{224,1... | collective-permute-start | bytes 368648 | tf_op jit(solution)/shard_map/ppermute | solution.py:503
  110.7 8.5 %collective-permute-start.22 = (f32[2,13,16,128]{3,2,1,0:T(8,128)S(1)}, f32[2,13,16,128]{3,2,1,0:T(8,128)S(1)}, u32[]{:S(2)}, u32[]{:S(2)}) collective-permute-start(f32[2,13,16,128]{3,2,1,0:T(8,128)S(1)} %pad_maximum_fusion.4), channel_id=1, source_target_pairs={{0,32},{32,0},{64,96},{96,64},{128,160},{160,128},{192,224},{224,1... | collective-permute-start | bytes 638984 | tf_op jit(solution)/shard_map/ppermute | solution.py:503
  115.8 7.3 %collective-permute-start.19 = (f32[2,15,16,128]{3,2,1,0:T(8,128)S(1)}, f32[2,15,16,128]{3,2,1,0:T(8,128)S(1)}, u32[]{:S(2)}, u32[]{:S(2)}) collective-permute-start(f32[2,15,16,128]{3,2,1,0:T(8,128)S(1)} %pad_maximum_fusion.3), channel_id=1, source_target_pairs={{0,192},{32,224},{64,128},{96,160},{128,64},{160,96},{192,0},{224,... | collective-permute-start | bytes 737288 | tf_op jit(solution)/shard_map/ppermute | solution.py:503
  115.9 7.7 %collective-permute-start.25 = (f32[2,13,16,128]{3,2,1,0:T(8,128)S(1)}, f32[2,13,16,128]{3,2,1,0:T(8,128)S(1)}, u32[]{:S(2)}, u32[]{:S(2)}) collective-permute-start(f32[2,13,16,128]{3,2,1,0:T(8,128)S(1)} %pad_maximum_fusion.5), channel_id=1, source_target_pairs={{0,64},{32,96},{64,0},{96,32},{128,192},{160,224},{192,128},{224,1... | collective-permute-start | bytes 638984 | tf_op jit(solution)/shard_map/ppermute | solution.py:503
  119.3 11.9 %collective-permute-start.23 = (f32[4,13,16,128]{3,2,1,0:T(8,128)S(1)}, f32[4,13,16,128]{3,2,1,0:T(8,128)S(1)}, u32[]{:S(2)}, u32[]{:S(2)}) collective-permute-start(f32[4,13,16,128]{3,2,1,0:T(8,128)S(1)} %pad_maximum_fusion.1), channel_id=1, source_target_pairs={{0,192},{32,224},{64,128},{96,160},{128,64},{160,96},{192,0},{224,... | collective-permute-start | bytes 1277960 | tf_op jit(solution)/shard_map/ppermute | solution.py:503
  123.2 9.2 %collective-permute-start.20 = (f32[4,15,16,128]{3,2,1,0:T(8,128)S(1)}, f32[4,15,16,128]{3,2,1,0:T(8,128)S(1)}, u32[]{:S(2)}, u32[]{:S(2)}) collective-permute-start(f32[4,15,16,128]{3,2,1,0:T(8,128)S(1)} %pad_maximum_fusion), channel_id=1, source_target_pairs={{0,64},{32,96},{64,0},{96,32},{128,192},{160,224},{192,128},{224,1... | collective-permute-start | bytes 1474568 | tf_op jit(solution)/shard_map/ppermute | solution.py:503
  123.7 8.2 %collective-permute-start.26 = (f32[4,13,16,128]{3,2,1,0:T(8,128)S(1)}, f32[4,13,16,128]{3,2,1,0:T(8,128)S(1)}, u32[]{:S(2)}, u32[]{:S(2)}) collective-permute-start(f32[4,13,16,128]{3,2,1,0:T(8,128)S(1)} %pad_maximum_fusion.2), channel_id=1, source_target_pairs={{0,32},{32,0},{64,96},{96,64},{128,160},{160,128},{192,224},{224,1... | collective-permute-start | bytes 1277960 | tf_op jit(solution)/shard_map/ppermute | solution.py:503
  (11 other events, 212.6 us)

commit v7 on v5

--- a/solution.py
+++ b/solution.py
@@ -16,7 +16,7 @@
 BULK = 4 * HF + 2 * HM
 N = 128
 PAD = 8
-CHUNK = 32
+CHUNK = 64
 F32 = jnp.float32
 
 GENS = (2, 6, 1)

time: 137 us -> 137 us (level)
  no operation moved by 1% of the time
where the time goes in v7:
time: 137 us
  waiting for transfers between devices  52.4 us (38%)
  starting transfers between devices  46 us (34%)
  Pallas kernels  36.1 us (26%)
    ppermute x21, starting transfers between devices, swap(): return lax.ppermute(x, 'wl', [(i, i ^ code) for i in range(8)])  29.7 us
    ppermute x21, waiting for transfers between devices, swap(): return lax.ppermute(x, 'wl', [(i, i ^ code) for i in range(8)])  27.6 us
    pallas_call x1, Pallas kernels, shards(): pl.pallas_call(solve_kernel, out_shape=[jax.ShapeDtypeStruct((4, NP, N, N...  19 us
    ppermute x1, waiting for transfers between devices, shards(): straight_b = lax.ppermute(extra_b, 'gz', AROUND)  14.9 us
    pallas_call x1, Pallas kernels, shards(): pl.pallas_call(inner_kernel, out_shape=held, in_specs=[SMEM] * 4 + [ANY]...  9.98 us
    ppermute x1, starting transfers between devices, shards(): bulk_b = lax.ppermute(bulk_b, 'gz', OFF_CHIP)  8.6 us
    all_to_all x1, waiting for transfers between devices, shards(): slab = jnp.sum(lax.all_to_all(sums, 'gz', 0, 0), axis=0)  6.55 us
    all_to_all x1, starting transfers between devices, shards(): slab = jnp.sum(lax.all_to_all(sums, 'gz', 0, 0), axis=0)  4.72 us
  transfers between devices with their start and end apart: 28, of which 13 were waited for; matrix products, arithmetic and copies ran while one was open for 1% of the time, Pallas kernels for 7%

profile of v7, /device:TPU:8, one launch (start us, length us, event | category | flops | bytes accessed | tf_op | source)
XLA Modules:
  0.0 136.7 jit_solution(18421765512871350288)
XLA Ops:
  0.7 2.5 %pack.1 = (f32[14,128,128]{2,1,0:T(8,128)S(1)}, f32[5,128,128]{2,1,0:T(8,128)S(1)}, f32[19,128,128]{2,1,0:T(8,128)S(1)}) custom-call(s32[2]{0:T(128)S(1)} %pad_add_fusion.where, s32[8,128,128]{2,1,0:T(8,128)} %labels.5, f32[4,8,128,128]{3,2,1,0:T(8,128)} %start.3, f32[4,8,128,128]{3,2,1,0:T(8,128)} %meas.3), custom_call_target="tpu_custom_call" | custom-call | tf_op jit(solution)/shard_map/pack/pallas_call | solution.py:518
  3.3 8.6 %collective-permute-start.1 = (f32[14,128,128]{2,1,0:T(8,128)S(1)}, f32[14,128,128]{2,1,0:T(8,128)S(1)}, u32[]{:S(2)}, u32[]{:S(2)}) collective-permute-start(f32[14,128,128]{2,1,0:T(8,128)S(1)} %get-tuple-element.39), channel_id=1, source_target_pairs={{0,31},{1,2},{2,1},{3,4},{4,3},{5,6},{6,5},{7,8},{8,7},{9,10},{10,... | collective-permute-start | bytes 2752520 | tf_op jit(solution)/shard_map/ppermute | solution.py:527
  12.2 14.9 %collective-permute-done.2.straight_b = f32[5,128,128]{2,1,0:T(8,128)S(1)} collective-permute-done((f32[5,128,128]{2,1,0:T(8,128)S(1)}, f32[5,128,128]{2,1,0:T(8,128)S(1)}, u32[]{:S(2)}, u32[]{:S(2)}) %collective-permute-start.2) | collective-permute-done | bytes 327712 | tf_op jit(solution)/shard_map/ppermute | solution.py:528
  28.8 10.0 %inner.1 = (f32[4,14,144,128]{3,2,1,0:T(8,128)S(1)}, f32[4,14,144,128]{3,2,1,0:T(8,128)S(1)}, f32[4,14,144,128]{3,2,1,0:T(8,128)S(1)}, f32[4,14,144,128]{3,2,1,0...) custom-call(s32[2]{0:T(128)S(1)} %pad_add_fusion.where, ...), custom_call_target="tpu_custom_call" | custom-call | tf_op jit(solution)/shard_map/inner/pallas_call | solution.py:550
  38.8 19.0 %solve.1 = (f32[4,8,128,128]{3,2,1,0:T(8,128)}, f32[4,128,128]{2,1,0:T(8,128)S(1)}, f32[4,128,128]{2,1,0:T(8,128)S(1)}, f32[4,128,128]{2,1,0:T(8,128)S(1)}, f32[...) custom-call(s32[2]{0:T(128)} %copy-done.6, ...), custom_call_target="tpu_custom_call", output_to_operand_aliasing={{11}: (9, {}), {12}: (10, {}), {13}: (11, {}), {14}: (12, {... | custom-call | tf_op jit(solution)/shard_map/solve/pallas_call | solution.py:559
  61.2 1.9 %collective-permute-start.6 = (f32[4,14,16,128]{3,2,1,0:T(8,128)S(1)}, f32[4,14,16,128]{3,2,1,0:T(8,128)S(1)}, u32[]{:S(2)}, u32[]{:S(2)}) collective-permute-start(f32[4,14,16,128]{3,2,1,0:T(8,128)S(1)} %get-tuple-element.58), channel_id=1, source_target_pairs={{0,64},{32,96},{64,0},{96,32},{128,192},{160,224},{192,128},{224,1... | collective-permute-start | bytes 1376264 | tf_op jit(solution)/shard_map/ppermute | solution.py:495
  63.1 3.0 %collective-permute-done.7 = f32[4,13,16,128]{3,2,1,0:T(8,128)S(1)} collective-permute-done((f32[4,13,16,128]{3,2,1,0:T(8,128)S(1)}, f32[4,13,16,128]{3,2,1,0:T(8,128)S(1)}, u32[]{:S(2)}, u32[]{:S(2)}) %collective-permute-start.7) | collective-permute-done | bytes 426016 | tf_op jit(solution)/shard_map/ppermute | solution.py:495
  66.2 3.6 %collective-permute-done.8 = f32[4,13,16,128]{3,2,1,0:T(8,128)S(1)} collective-permute-done((f32[4,13,16,128]{3,2,1,0:T(8,128)S(1)}, f32[4,13,16,128]{3,2,1,0:T(8,128)S(1)}, u32[]{:S(2)}, u32[]{:S(2)}) %collective-permute-start.8) | collective-permute-done | bytes 426016 | tf_op jit(solution)/shard_map/ppermute | solution.py:495
  69.9 2.8 %collective-permute-done.6 = f32[4,14,16,128]{3,2,1,0:T(8,128)S(1)} collective-permute-done((f32[4,14,16,128]{3,2,1,0:T(8,128)S(1)}, f32[4,14,16,128]{3,2,1,0:T(8,128)S(1)}, u32[]{:S(2)}, u32[]{:S(2)}) %collective-permute-start.6) | collective-permute-done | bytes 458784 | tf_op jit(solution)/shard_map/ppermute | solution.py:495
  72.7 3.3 %collective-permute-done.5.edge_b = f32[4,128,128]{2,1,0:T(8,128)S(1)} collective-permute-done((f32[4,128,128]{2,1,0:T(8,128)S(1)}, f32[4,128,128]{2,1,0:T(8,128)S(1)}, u32[]{:S(2)}, u32[]{:S(2)}) %collective-permute-start.5) | collective-permute-done | bytes 262176 | tf_op jit(solution)/shard_map/ppermute | solution.py:505
  76.6 2.0 %collective-permute-start.9 = (f32[4,2,16,128]{3,2,1,0:T(8,128)S(1)}, f32[4,2,16,128]{3,2,1,0:T(8,128)S(1)}, u32[]{:S(2)}, u32[]{:S(2)}) collective-permute-start(f32[4,2,16,128]{3,2,1,0:T(8,128)S(1)} %get-tuple-element.66), channel_id=1, source_target_pairs={{0,64},{32,96},{64,0},{96,32},{128,192},{160,224},{192,128},{224,1... | collective-permute-start | bytes 196616 | tf_op jit(solution)/shard_map/ppermute | solution.py:495
  79.2 2.1 %collective-permute-done.9 = f32[4,2,16,128]{3,2,1,0:T(8,128)S(1)} collective-permute-done((f32[4,2,16,128]{3,2,1,0:T(8,128)S(1)}, f32[4,2,16,128]{3,2,1,0:T(8,128)S(1)}, u32[]{:S(2)}, u32[]{:S(2)}) %collective-permute-start.9) | collective-permute-done | bytes 65568 | tf_op jit(solution)/shard_map/ppermute | solution.py:495
  81.5 3.5 %collective-permute-done.13 = f32[2,13,16,128]{3,2,1,0:T(8,128)S(1)} collective-permute-done((f32[2,13,16,128]{3,2,1,0:T(8,128)S(1)}, f32[2,13,16,128]{3,2,1,0:T(8,128)S(1)}, u32[]{:S(2)}, u32[]{:S(2)}) %collective-permute-start.13) | collective-permute-done | bytes 213024 | tf_op jit(solution)/shard_map/ppermute | solution.py:495
  88.3 3.5 %collective-permute-done.11.late_recv = f32[1,2,16,128]{3,2,1,0:T(8,128)S(1)} collective-permute-done((f32[1,2,16,128]{3,2,1,0:T(8,128)S(1)}, f32[1,2,16,128]{3,2,1,0:T(8,128)S(1)}, u32[]{:S(2)}, u32[]{:S(2)}) %collective-permute-start.11) | collective-permute-done | bytes 16416 | tf_op jit(solution)/shard_map/ppermute | solution.py:495
  93.0 4.7 %all-to-all-start = ((f32[32,1,128]{2,1,0:T(1,128)}), f32[32,1,128]{2,1,0:T(1,128)S(1)}, u32[]{:S(2)}, u32[]{:S(2)}) async-start(f32[32,1,128]{2,1,0:T(1,128)} %get-tuple-element.68), calls=%async_computation | async-start | bytes 32768 | tf_op jit(solution)/shard_map/all_to_all | solution.py:617
  97.8 3.2 %collective-permute-start.21 = (f32[1,13,16,128]{3,2,1,0:T(8,128)S(1)}, f32[1,13,16,128]{3,2,1,0:T(8,128)S(1)}, u32[]{:S(2)}, u32[]{:S(2)}) collective-permute-start(f32[1,13,16,128]{3,2,1,0:T(8,128)S(1)} %get-tuple-element.69.refs_4_), channel_id=1, source_target_pairs={{0,64},{32,96},{64,0},{96,32},{128,192},{160,224},{192,128},{224,1... | collective-permute-start | bytes 319496 | tf_op jit(solution)/shard_map/ppermute | solution.py:495
  100.9 6.6 %all-to-all-done = f32[32,1,128]{2,1,0:T(1,128)S(1)} async-done(((f32[32,1,128]{2,1,0:T(1,128)}), f32[32,1,128]{2,1,0:T(1,128)S(1)}, u32[]{:S(2)}, u32[]{:S(2)}) %all-to-all-start) | async-done | bytes 16416 | tf_op jit(solution)/shard_map/all_to_all | solution.py:617
  112.9 2.9 %collective-permute-start.19 = (f32[2,15,16,128]{3,2,1,0:T(8,128)S(1)}, f32[2,15,16,128]{3,2,1,0:T(8,128)S(1)}, u32[]{:S(2)}, u32[]{:S(2)}) collective-permute-start(f32[2,15,16,128]{3,2,1,0:T(8,128)S(1)} %pad_maximum_fusion.3), channel_id=1, source_target_pairs={{0,192},{32,224},{64,128},{96,160},{128,64},{160,96},{192,0},{224,... | collective-permute-start | bytes 737288 | tf_op jit(solution)/shard_map/ppermute | solution.py:495
  115.8 2.1 %collective-permute-start.25 = (f32[2,13,16,128]{3,2,1,0:T(8,128)S(1)}, f32[2,13,16,128]{3,2,1,0:T(8,128)S(1)}, u32[]{:S(2)}, u32[]{:S(2)}) collective-permute-start(f32[2,13,16,128]{3,2,1,0:T(8,128)S(1)} %pad_maximum_fusion.5), channel_id=1, source_target_pairs={{0,64},{32,96},{64,0},{96,32},{128,192},{160,224},{192,128},{224,1... | collective-permute-start | bytes 638984 | tf_op jit(solution)/shard_map/ppermute | solution.py:495
  117.9 2.0 %collective-permute-start.23 = (f32[4,13,16,128]{3,2,1,0:T(8,128)S(1)}, f32[4,13,16,128]{3,2,1,0:T(8,128)S(1)}, u32[]{:S(2)}, u32[]{:S(2)}) collective-permute-start(f32[4,13,16,128]{3,2,1,0:T(8,128)S(1)} %pad_maximum_fusion.1), channel_id=1, source_target_pairs={{0,192},{32,224},{64,128},{96,160},{128,64},{160,96},{192,0},{224,... | collective-permute-start | bytes 1277960 | tf_op jit(solution)/shard_map/ppermute | solution.py:495
  120.7 4.9 %collective-permute-start.20 = (f32[4,15,16,128]{3,2,1,0:T(8,128)S(1)}, f32[4,15,16,128]{3,2,1,0:T(8,128)S(1)}, u32[]{:S(2)}, u32[]{:S(2)}) collective-permute-start(f32[4,15,16,128]{3,2,1,0:T(8,128)S(1)} %pad_maximum_fusion), channel_id=1, source_target_pairs={{0,64},{32,96},{64,0},{96,32},{128,192},{160,224},{192,128},{224,1... | collective-permute-start | bytes 1474568 | tf_op jit(solution)/shard_map/ppermute | solution.py:495
  126.8 2.2 %collective-permute-done.23.refs_7_ = f32[4,13,16,128]{3,2,1,0:T(8,128)S(1)} collective-permute-done((f32[4,13,16,128]{3,2,1,0:T(8,128)S(1)}, f32[4,13,16,128]{3,2,1,0:T(8,128)S(1)}, u32[]{:S(2)}, u32[]{:S(2)}) %collective-permute-start.23) | collective-permute-done | bytes 426016 | tf_op jit(solution)/shard_map/ppermute | solution.py:495
  129.0 4.8 %collective-permute-done.26.refs_11_ = f32[4,13,16,128]{3,2,1,0:T(8,128)S(1)} collective-permute-done((f32[4,13,16,128]{3,2,1,0:T(8,128)S(1)}, f32[4,13,16,128]{3,2,1,0:T(8,128)S(1)}, u32[]{:S(2)}, u32[]{:S(2)}) %collective-permute-start.26) | collective-permute-done | bytes 426016 | tf_op jit(solution)/shard_map/ppermute | solution.py:495
  133.8 2.7 %final.1 = (f32[4,8,128,128]{3,2,1,0:T(8,128)}, f32[8,128,128]{2,1,0:T(8,128)}) custom-call(s32[2]{0:T(128)S(1)} %copy-done.7, f32[8,5]{1,0:T(8,128)S(1)} %copy-done.2, s32[8,128,128]{2,1,0:T(8,128)S(1)} %copy-done, f32[1,15,16,128]{3,2,1,0:T(8,128)S(1)} %pad_maximum_fusion.6.refs_0_, f32[1,15,16,128]{3,2,1,0:T(8,128)S(1)} %collective-permute-done.18.refs_1_, ...), custom_call_target="tpu_custom_call" | custom-call | tf_op jit(solution)/shard_map/final/pallas_call | solution.py:624
  (75 shorter events, 19.1 us)
Async XLA Ops:
  3.2 35.6 %collective-permute-start = (f32[19,128,128]{2,1,0:T(8,128)S(1)}, f32[19,128,128]{2,1,0:T(8,128)S(1)}, u32[]{:S(2)}, u32[]{:S(2)}) collective-permute-start(f32[19,128,128]{2,1,0:T(8,128)S(1)} %get-tuple-element.38), channel_id=1, source_target_pairs={{0,1},{1,0},{2,3},{3,2},{4,5},{5,4},{6,7},{7,6},{8,9},{9,8},{10,11... | collective-permute-start | bytes 3735560 | tf_op jit(solution)/shard_map/ppermute | solution.py:529
  3.3 35.5 %collective-permute-start.1 = (f32[14,128,128]{2,1,0:T(8,128)S(1)}, f32[14,128,128]{2,1,0:T(8,128)S(1)}, u32[]{:S(2)}, u32[]{:S(2)}) collective-permute-start(f32[14,128,128]{2,1,0:T(8,128)S(1)} %get-tuple-element.39), channel_id=1, source_target_pairs={{0,31},{1,2},{2,1},{3,4},{4,3},{5,6},{6,5},{7,8},{8,7},{9,10},{10,... | collective-permute-start | bytes 2752520 | tf_op jit(solution)/shard_map/ppermute | solution.py:527
  11.9 15.2 %collective-permute-start.2 = (f32[5,128,128]{2,1,0:T(8,128)S(1)}, f32[5,128,128]{2,1,0:T(8,128)S(1)}, u32[]{:S(2)}, u32[]{:S(2)}) collective-permute-start(f32[5,128,128]{2,1,0:T(8,128)S(1)} %get-tuple-element.40), channel_id=1, source_target_pairs={{0,7},{1,2},{2,1},{3,4},{4,3},{5,6},{6,5},{7,0},{8,15},{9,10},{10,... | collective-permute-start | bytes 983048 | tf_op jit(solution)/shard_map/ppermute | solution.py:528
  27.1 11.7 %collective-permute-start.3 = (f32[5,128,128]{2,1,0:T(8,128)S(1)}, f32[5,128,128]{2,1,0:T(8,128)S(1)}, u32[]{:S(2)}, u32[]{:S(2)}) collective-permute-start(f32[5,128,128]{2,1,0:T(8,128)S(1)} %collective-permute-done.2.straight_b), channel_id=1, source_target_pairs={{0,8},{8,16},{16,24},{15,7},{23,15},{31,23},{32,40},{40,48},{48,56... | collective-permute-start | bytes 983048 | tf_op jit(solution)/shard_map/ppermute | solution.py:530
  57.9 8.2 %collective-permute-start.7 = (f32[4,13,16,128]{3,2,1,0:T(8,128)S(1)}, f32[4,13,16,128]{3,2,1,0:T(8,128)S(1)}, u32[]{:S(2)}, u32[]{:S(2)}) collective-permute-start(f32[4,13,16,128]{3,2,1,0:T(8,128)S(1)} %get-tuple-element.60), channel_id=1, source_target_pairs={{0,192},{32,224},{64,128},{96,160},{128,64},{160,96},{192,0},{224,... | collective-permute-start | bytes 1277960 | tf_op jit(solution)/shard_map/ppermute | solution.py:495
  59.6 10.2 %collective-permute-start.8 = (f32[4,13,16,128]{3,2,1,0:T(8,128)S(1)}, f32[4,13,16,128]{3,2,1,0:T(8,128)S(1)}, u32[]{:S(2)}, u32[]{:S(2)}) collective-permute-start(f32[4,13,16,128]{3,2,1,0:T(8,128)S(1)} %get-tuple-element.62), channel_id=1, source_target_pairs={{0,32},{32,0},{64,96},{96,64},{128,160},{160,128},{192,224},{224,1... | collective-permute-start | bytes 1277960 | tf_op jit(solution)/shard_map/ppermute | solution.py:495
  59.6 13.1 %collective-permute-start.4 = (f32[4,128,128]{2,1,0:T(8,128)S(1)}, f32[4,128,128]{2,1,0:T(8,128)S(1)}, u32[]{:S(2)}, u32[]{:S(2)}) collective-permute-start(f32[4,128,128]{2,1,0:T(8,128)S(1)} %get-tuple-element.55), channel_id=1, source_target_pairs={{0,1},{1,0},{2,3},{3,2},{4,5},{5,4},{6,7},{7,6},{8,9},{9,8},{10,11... | collective-permute-start | bytes 786440 | tf_op jit(solution)/shard_map/ppermute | solution.py:505
  59.6 16.4 %collective-permute-start.5 = (f32[4,128,128]{2,1,0:T(8,128)S(1)}, f32[4,128,128]{2,1,0:T(8,128)S(1)}, u32[]{:S(2)}, u32[]{:S(2)}) collective-permute-start(f32[4,128,128]{2,1,0:T(8,128)S(1)} %get-tuple-element.56), channel_id=1, source_target_pairs={{0,31},{1,2},{2,1},{3,4},{4,3},{5,6},{6,5},{7,8},{8,7},{9,10},{10,... | collective-permute-start | bytes 786440 | tf_op jit(solution)/shard_map/ppermute | solution.py:505
  61.2 11.5 %collective-permute-start.6 = (f32[4,14,16,128]{3,2,1,0:T(8,128)S(1)}, f32[4,14,16,128]{3,2,1,0:T(8,128)S(1)}, u32[]{:S(2)}, u32[]{:S(2)}) collective-permute-start(f32[4,14,16,128]{3,2,1,0:T(8,128)S(1)} %get-tuple-element.58), channel_id=1, source_target_pairs={{0,64},{32,96},{64,0},{96,32},{128,192},{160,224},{192,128},{224,1... | collective-permute-start | bytes 1376264 | tf_op jit(solution)/shard_map/ppermute | solution.py:495
  78.6 6.4 %collective-permute-start.13 = (f32[2,13,16,128]{3,2,1,0:T(8,128)S(1)}, f32[2,13,16,128]{3,2,1,0:T(8,128)S(1)}, u32[]{:S(2)}, u32[]{:S(2)}) collective-permute-start(f32[2,13,16,128]{3,2,1,0:T(8,128)S(1)} %get-tuple-element.90), channel_id=1, source_target_pairs={{0,32},{32,0},{64,96},{96,64},{128,160},{160,128},{192,224},{224,1... | collective-permute-start | bytes 638984 | tf_op jit(solution)/shard_map/ppermute | solution.py:495
  78.6 6.7 %collective-permute-start.14 = (f32[2,13,16,128]{3,2,1,0:T(8,128)S(1)}, f32[2,13,16,128]{3,2,1,0:T(8,128)S(1)}, u32[]{:S(2)}, u32[]{:S(2)}) collective-permute-start(f32[2,13,16,128]{3,2,1,0:T(8,128)S(1)} %get-tuple-element.88), channel_id=1, source_target_pairs={{0,64},{32,96},{64,0},{96,32},{128,192},{160,224},{192,128},{224,1... | collective-permute-start | bytes 638984 | tf_op jit(solution)/shard_map/ppermute | solution.py:495
  78.8 7.2 %collective-permute-start.12 = (f32[2,14,16,128]{3,2,1,0:T(8,128)S(1)}, f32[2,14,16,128]{3,2,1,0:T(8,128)S(1)}, u32[]{:S(2)}, u32[]{:S(2)}) collective-permute-start(f32[2,14,16,128]{3,2,1,0:T(8,128)S(1)} %get-tuple-element.86), channel_id=1, source_target_pairs={{0,192},{32,224},{64,128},{96,160},{128,64},{160,96},{192,0},{224,... | collective-permute-start | bytes 688136 | tf_op jit(solution)/shard_map/ppermute | solution.py:495
  81.3 6.6 %collective-permute-start.10 = (f32[2,2,16,128]{3,2,1,0:T(8,128)S(1)}, f32[2,2,16,128]{3,2,1,0:T(8,128)S(1)}, u32[]{:S(2)}, u32[]{:S(2)}) collective-permute-start(f32[2,2,16,128]{3,2,1,0:T(8,128)S(1)} %get-tuple-element.98), channel_id=1, source_target_pairs={{0,192},{32,224},{64,128},{96,160},{128,64},{160,96},{192,0},{224,... | collective-permute-start | bytes 98312 | tf_op jit(solution)/shard_map/ppermute | solution.py:495
  85.0 6.7 %collective-permute-start.16 = (f32[1,13,16,128]{3,2,1,0:T(8,128)S(1)}, f32[1,13,16,128]{3,2,1,0:T(8,128)S(1)}, u32[]{:S(2)}, u32[]{:S(2)}) collective-permute-start(f32[1,13,16,128]{3,2,1,0:T(8,128)S(1)} %get-tuple-element.95), channel_id=1, source_target_pairs={{0,64},{32,96},{64,0},{96,32},{128,192},{160,224},{192,128},{224,1... | collective-permute-start | bytes 319496 | tf_op jit(solution)/shard_map/ppermute | solution.py:495
  85.3 6.4 %collective-permute-start.17 = (f32[1,13,16,128]{3,2,1,0:T(8,128)S(1)}, f32[1,13,16,128]{3,2,1,0:T(8,128)S(1)}, u32[]{:S(2)}, u32[]{:S(2)}) collective-permute-start(f32[1,13,16,128]{3,2,1,0:T(8,128)S(1)} %get-tuple-element.93), channel_id=1, source_target_pairs={{0,192},{32,224},{64,128},{96,160},{128,64},{160,96},{192,0},{224,... | collective-permute-start | bytes 319496 | tf_op jit(solution)/shard_map/ppermute | solution.py:495
  93.0 14.4 %all-to-all-start = ((f32[32,1,128]{2,1,0:T(1,128)}), f32[32,1,128]{2,1,0:T(1,128)S(1)}, u32[]{:S(2)}, u32[]{:S(2)}) async-start(f32[32,1,128]{2,1,0:T(1,128)} %get-tuple-element.68), calls=%async_computation | async-start | bytes 32768 | tf_op jit(solution)/shard_map/all_to_all | solution.py:617
  97.8 12.8 %collective-permute-start.21 = (f32[1,13,16,128]{3,2,1,0:T(8,128)S(1)}, f32[1,13,16,128]{3,2,1,0:T(8,128)S(1)}, u32[]{:S(2)}, u32[]{:S(2)}) collective-permute-start(f32[1,13,16,128]{3,2,1,0:T(8,128)S(1)} %get-tuple-element.69.refs_4_), channel_id=1, source_target_pairs={{0,64},{32,96},{64,0},{96,32},{128,192},{160,224},{192,128},{224,1... | collective-permute-start | bytes 319496 | tf_op jit(solution)/shard_map/ppermute | solution.py:495
  108.7 7.1 %collective-permute-start.24 = (f32[1,13,16,128]{3,2,1,0:T(8,128)S(1)}, f32[1,13,16,128]{3,2,1,0:T(8,128)S(1)}, u32[]{:S(2)}, u32[]{:S(2)}) collective-permute-start(f32[1,13,16,128]{3,2,1,0:T(8,128)S(1)} %get-tuple-element.70.refs_8_), channel_id=1, source_target_pairs={{0,192},{32,224},{64,128},{96,160},{128,64},{160,96},{192,0},{224,... | collective-permute-start | bytes 319496 | tf_op jit(solution)/shard_map/ppermute | solution.py:495
  110.5 7.3 %collective-permute-start.22 = (f32[2,13,16,128]{3,2,1,0:T(8,128)S(1)}, f32[2,13,16,128]{3,2,1,0:T(8,128)S(1)}, u32[]{:S(2)}, u32[]{:S(2)}) collective-permute-start(f32[2,13,16,128]{3,2,1,0:T(8,128)S(1)} %pad_maximum_fusion.4), channel_id=1, source_target_pairs={{0,32},{32,0},{64,96},{96,64},{128,160},{160,128},{192,224},{224,1... | collective-permute-start | bytes 638984 | tf_op jit(solution)/shard_map/ppermute | solution.py:495
  112.9 7.8 %collective-permute-start.19 = (f32[2,15,16,128]{3,2,1,0:T(8,128)S(1)}, f32[2,15,16,128]{3,2,1,0:T(8,128)S(1)}, u32[]{:S(2)}, u32[]{:S(2)}) collective-permute-start(f32[2,15,16,128]{3,2,1,0:T(8,128)S(1)} %pad_maximum_fusion.3), channel_id=1, source_target_pairs={{0,192},{32,224},{64,128},{96,160},{128,64},{160,96},{192,0},{224,... | collective-permute-start | bytes 737288 | tf_op jit(solution)/shard_map/ppermute | solution.py:495
  115.8 9.8 %collective-permute-start.25 = (f32[2,13,16,128]{3,2,1,0:T(8,128)S(1)}, f32[2,13,16,128]{3,2,1,0:T(8,128)S(1)}, u32[]{:S(2)}, u32[]{:S(2)}) collective-permute-start(f32[2,13,16,128]{3,2,1,0:T(8,128)S(1)} %pad_maximum_fusion.5), channel_id=1, source_target_pairs={{0,64},{32,96},{64,0},{96,32},{128,192},{160,224},{192,128},{224,1... | collective-permute-start | bytes 638984 | tf_op jit(solution)/shard_map/ppermute | solution.py:495
  117.9 11.2 %collective-permute-start.23 = (f32[4,13,16,128]{3,2,1,0:T(8,128)S(1)}, f32[4,13,16,128]{3,2,1,0:T(8,128)S(1)}, u32[]{:S(2)}, u32[]{:S(2)}) collective-permute-start(f32[4,13,16,128]{3,2,1,0:T(8,128)S(1)} %pad_maximum_fusion.1), channel_id=1, source_target_pairs={{0,192},{32,224},{64,128},{96,160},{128,64},{160,96},{192,0},{224,... | collective-permute-start | bytes 1277960 | tf_op jit(solution)/shard_map/ppermute | solution.py:495
  120.7 13.1 %collective-permute-start.20 = (f32[4,15,16,128]{3,2,1,0:T(8,128)S(1)}, f32[4,15,16,128]{3,2,1,0:T(8,128)S(1)}, u32[]{:S(2)}, u32[]{:S(2)}) collective-permute-start(f32[4,15,16,128]{3,2,1,0:T(8,128)S(1)} %pad_maximum_fusion), channel_id=1, source_target_pairs={{0,64},{32,96},{64,0},{96,32},{128,192},{160,224},{192,128},{224,1... | collective-permute-start | bytes 1474568 | tf_op jit(solution)/shard_map/ppermute | solution.py:495
  125.6 8.2 %collective-permute-start.26 = (f32[4,13,16,128]{3,2,1,0:T(8,128)S(1)}, f32[4,13,16,128]{3,2,1,0:T(8,128)S(1)}, u32[]{:S(2)}, u32[]{:S(2)}) collective-permute-start(f32[4,13,16,128]{3,2,1,0:T(8,128)S(1)} %pad_maximum_fusion.2), channel_id=1, source_target_pairs={{0,32},{32,0},{64,96},{96,64},{128,160},{160,128},{192,224},{224,1... | collective-permute-start | bytes 1277960 | tf_op jit(solution)/shard_map/ppermute | solution.py:495
  (12 other events, 220.2 us)
